TPU v7x, 128 devices: a whole 4x4x4 slice. The times are simulated.
128 devices in a mesh: grp: 4 (over z_hi, core), blk: 32 (over z_lo, y, x).
Axes of the slice: x: 4, y: 4, z: 4 (z_hi: 2, z_lo: 2; z = z_hi * 2 + z_lo), core: 2. Of those that a mesh axis runs over, the one named last changes fastest.
Arguments:
- raw: bfloat16 [4, 4, 4096, 256], P('grp', None, 'blk'), may hold values from -6 to 6
- raw_kin: bfloat16 [4, 4, 4, 4096], P('grp', None, None, 'blk'), may hold values from -3.2 to 20, as said below
- reader: int32 [4, 4096], P('grp', 'blk'), may hold values from 0 to 3
- event_id: int32 [4, 4096], P('grp', 'blk'), may hold values from 0 to 7, never falling along the last dimension, each value on 1 to 2048 neighbouring positions
- pre_gain: float32 [256], replicated, may hold values from 0.25 to 1.75
- w_query: bfloat16 [256, 256], replicated, may hold values from -2 to 2
- w_key: bfloat16 [256, 256], replicated, may hold values from -2 to 2
- w_value: bfloat16 [256, 256], replicated, may hold values from -0.375 to 0.375
- w_out: bfloat16 [256, 256], replicated, may hold values from -0.375 to 0.375
- post_gain: float32 [256], replicated, may hold values from 0.25 to 1.75
- pair_w1: float32 [4, 32], replicated, may hold values from -3 to 3
- pair_b1: float32 [32], replicated, may hold values from -4 to 4
- pair_w2: float32 [32, 8], replicated, may hold values from -1 to 1
Outputs:
- encoded: bfloat16 [4, 4096, 256], P('grp', 'blk')
Inputs may be any that keep to these rules, and one draw needn't show every extreme that they name: `raw_kin`: rows are transverse momentum (positive), rapidity, azimuth and mass (positive). `event_id`: event numbers never fall along a group's slots; every event holds 1 to 2048 slots and some event exactly 2048.
All inputs are finite; a program needn't handle non-finite values.
Results may differ from a plain program's by a relative error of at most 0.0091.
Values may be sent and summed in bfloat16 or wider, within the bound.
A program may use at most 64 MiB of HBM per device.

v0:
```python
import jax
import jax.numpy as jnp
from jax import lax
from jax.sharding import PartitionSpec as P

exact_mode = lax.Precision.HIGHEST


def layer_norm(rows, gain):
    center = rows - jnp.mean(rows, axis=-1, keepdims=True)
    spread = jnp.mean(center * center, axis=-1, keepdims=True)
    return center * lax.rsqrt(spread + 1e-05) * gain


def particle_terms(kinematics):
    trans_mom = kinematics[0]
    rapidity = kinematics[1]
    azimuth = kinematics[2]
    mass_val = kinematics[3]
    trans_mass = jnp.sqrt(trans_mom * trans_mom + mass_val * mass_val)
    return (
        trans_mom,
        rapidity,
        jnp.cos(azimuth),
        jnp.sin(azimuth),
        trans_mass,
        mass_val * mass_val,
    )


def pair_bias(query_terms, key_terms, pair_params):
    pair_w1, pair_b1, pair_w2 = pair_params
    q_mom, q_rap, q_cos, q_sin, q_trans, q_mass = [term[:, None] for term in query_terms]
    k_mom, k_rap, k_cos, k_sin, k_trans, k_mass = [term[None, :] for term in key_terms]
    rap_gap = q_rap - k_rap
    cos_gap = q_cos * k_cos + q_sin * k_sin
    dist_sq = rap_gap * rap_gap + 2.0 * (1.0 - cos_gap)
    low_mom = jnp.minimum(q_mom, k_mom)
    mass_sq = (
        q_mass + k_mass + 2.0 * (q_trans * k_trans * jnp.cosh(rap_gap) - q_mom * k_mom * cos_gap)
    )
    features = jnp.stack(
        [
            jnp.log1p(dist_sq),
            jnp.log1p(low_mom * low_mom * dist_sq),
            low_mom / (q_mom + k_mom),
            jnp.log1p(mass_sq),
        ]
    )
    hidden = jax.nn.gelu(
        jnp.einsum("cqk,ch->hqk", features, pair_w1, precision=exact_mode) + pair_b1[:, None, None],
        approximate=True,
    )
    return jnp.einsum("hqk,hn->nqk", hidden, pair_w2, precision=exact_mode)


def project_cols(weight, rows_cols):
    product = lax.dot_general(
        weight, rows_cols, (((0,), (0,)), ((), ())), preferred_element_type=jnp.float32
    )
    return product.astype(jnp.bfloat16)


def attend_block(state, query_side, key_cols, value_cols, key_terms, key_ids, pair_params):
    run_max, run_sum, accum = state
    queries, query_terms, query_ids = query_side
    heads = run_max.shape[0]
    width = key_cols.shape[0]
    head_size = width // heads
    columns = key_cols.shape[1]
    key_heads = key_cols.reshape(heads, head_size, columns)
    value_heads = value_cols.reshape(heads, head_size, columns)
    scores = jnp.einsum(
        "qhd,hdk->hqk", queries, key_heads, preferred_element_type=jnp.float32
    ) * head_size ** (-0.5)
    scores = scores + pair_bias(query_terms, key_terms, pair_params)
    live = (query_ids[:, None] == key_ids[None, :])[None]
    block_max = jnp.max(jnp.where(live, scores, jnp.float32(-1e30)), axis=2)
    new_max = jnp.maximum(run_max, block_max)
    weights = jnp.where(live, jnp.exp(scores - new_max[:, :, None]), 0.0)
    decay = jnp.exp(run_max - new_max)
    new_sum = run_sum * decay + jnp.sum(weights, axis=2)
    update = jnp.einsum(
        "hqk,hdk->qhd",
        weights.astype(jnp.bfloat16),
        value_heads,
        preferred_element_type=jnp.float32,
    )
    new_accum = accum * decay.T[:, :, None] + update
    return (new_max, new_sum, new_accum)


def shards(
    raw,
    raw_kin,
    reader,
    event_id,
    pre_gain,
    w_query,
    w_key,
    w_value,
    w_out,
    post_gain,
    pair_w1,
    pair_b1,
    pair_w2,
):
    arrived, arrived_kin = (
        lax.all_to_all(raw, "grp", split_axis=1, concat_axis=0, tiled=True),
        lax.all_to_all(raw_kin, "grp", split_axis=1, concat_axis=0, tiled=True),
    )
    groups = arrived.shape[0]
    own_rows = arrived.shape[2]
    width = arrived.shape[3]
    heads = pair_w2.shape[1]
    head_size = width // heads
    picked = reader[0][None, :] == jnp.arange(groups, dtype=jnp.int32)[:, None]
    tokens = jnp.sum(
        jnp.where(picked[:, :, None], arrived[:, 0], jnp.zeros((), jnp.bfloat16)),
        axis=0,
        dtype=jnp.float32,
    )
    kin_rows = jnp.sum(
        jnp.where(picked[:, None, :], arrived_kin[:, 0], jnp.zeros((), jnp.bfloat16)),
        axis=0,
        dtype=jnp.float32,
    ).astype(jnp.bfloat16)
    normed = layer_norm(tokens, pre_gain).astype(jnp.bfloat16)
    normed_cols = normed.T
    queries = jnp.dot(normed, w_query, preferred_element_type=jnp.float32).astype(jnp.bfloat16)
    queries = queries.reshape(own_rows, heads, head_size)
    query_ids = event_id[0]
    query_side = (queries, particle_terms(kin_rows.astype(jnp.float32)), query_ids)
    pair_params = (pair_w1, pair_b1, pair_w2)
    initial = (
        jnp.full((heads, own_rows), -1e30, jnp.float32),
        jnp.zeros((heads, own_rows), jnp.float32),
        jnp.zeros((own_rows, heads, head_size), jnp.float32),
    )
    key_cols = project_cols(w_key, normed_cols)
    value_cols = project_cols(w_value, normed_cols)
    consume_key_cols = lax.all_gather(key_cols, "blk", axis=1, tiled=True)
    consume_value_cols = lax.all_gather(value_cols, "blk", axis=1, tiled=True)
    kin_piece = lax.all_gather(kin_rows, "blk", axis=1, tiled=True)
    id_piece = lax.all_gather(event_id, "blk", axis=1, tiled=True)
    columns = consume_key_cols.shape[1]
    span = 512

    def one_block(index, carried):
        start = index * span
        block_keys = lax.dynamic_slice_in_dim(consume_key_cols, start, span, 1)
        block_values = lax.dynamic_slice_in_dim(consume_value_cols, start, span, 1)
        block_kin = lax.dynamic_slice_in_dim(kin_piece, start, span, 1)
        block_ids = lax.dynamic_slice_in_dim(id_piece, start, span, 1)[0]
        return attend_block(
            carried,
            query_side,
            block_keys,
            block_values,
            particle_terms(block_kin.astype(jnp.float32)),
            block_ids,
            pair_params,
        )

    final = lax.fori_loop(0, columns // span, one_block, initial)
    run_max, run_sum, accum = final
    attended = (accum / run_sum.T[:, :, None]).reshape(own_rows, width).astype(jnp.bfloat16)
    mixed_out = jnp.dot(attended, w_out, preferred_element_type=jnp.float32)
    encoded = layer_norm(mixed_out, post_gain).astype(jnp.bfloat16)
    return encoded[None]


def solution(mesh):
    in_specs = (
        P("grp", None, "blk", None),
        P("grp", None, None, "blk"),
        P("grp", "blk"),
        P("grp", "blk"),
        P(),
        P(),
        P(),
        P(),
        P(),
        P(),
        P(),
        P(),
        P(),
    )
    out_specs = P("grp", "blk", None)
    return jax.shard_map(shards, mesh=mesh, in_specs=in_specs, out_specs=out_specs, check_vma=False)
```

profile of v0, /device:TPU:8, one launch (start us, length us, event | category | flops | bytes accessed | tf_op | source)
XLA Modules:
  0.0 511.6 jit_solution(5281460452214196107)
XLA Ops:
  6.5 5.3 %all-to-all-start = ((bf16[1,4,128,256]{3,2,0,1:T(8,128)(2,1)}), bf16[1,4,128,256]{3,2,0,1:T(8,128)(2,1)S(1)}, u32[]{:S(2)}, u32[]{:S(2)}) async-start(bf16[1,4,128,256]{3,2,0,1:T(8,128)(2,1)} %bitcast.120), calls=%async_computation | async-start | bytes 524288 | tf_op jit(solution)/shard_map/all_to_all | solution.py:109
  12.5 6.9 %all-to-all-done = bf16[1,4,128,256]{3,2,0,1:T(8,128)(2,1)S(1)} async-done(((bf16[1,4,128,256]{3,2,0,1:T(8,128)(2,1)}), bf16[1,4,128,256]{3,2,0,1:T(8,128)(2,1)S(1)}, u32[]{:S(2)}, u32[]{:S(2)}) %all-to-all-start) | async-done | bytes 262176 | tf_op jit(solution)/shard_map/all_to_all | solution.py:109
  20.6 1.7 fusion.44
  22.4 1.7 fusion.45
  24.1 3.3 all-to-all-start.1
  27.4 72.7 %all_gather.12 = s32[1,4096]{1,0:T(1,128)S(1)} all-gather(s32[1,128]{1,0:T(1,128)} %param.18), channel_id=1, replica_groups=mesh['grp'=4,'blk'=32] {'blk'}, dimensions={1}, use_global_device_ids=true | all-gather | bytes 16896 | tf_op jit(solution)/shard_map/all_gather | solution.py:145
  100.1 75.3 %all_gather.14 = bf16[4,4096]{1,0:T(4,128)(2,1)S(1)} all-gather(bf16[4,128]{1,0:T(4,128)(2,1)S(1)} %fusion.47), channel_id=1, replica_groups=mesh['grp'=4,'blk'=32] {'blk'}, dimensions={1}, use_global_device_ids=true | all-gather | bytes 33792 | tf_op jit(solution)/shard_map/all_gather | solution.py:144
  176.8 147.6 %all-gather.5.cloned.1.call-done = bf16[256,4096]{0,1:T(8,128)(2,1)} async-done(((bf16[256,128]{0,1:T(8,128)(2,1)}), bf16[256,4096]{0,1:T(8,128)(2,1)}) %all-gather.5.cloned.1.call-update) | async-done | bytes 2097168 | tf_op jit(solution)/shard_map/all_gather | solution.py:143
  324.3 179.1 %while.18 = (s32[]{:T(128)}, f32[8,128]{1,0:T(8,128)S(1)}, f32[8,128]{1,0:T(8,128)S(1)}, f32[128,8,32]{0,2,1:T(8,128)S(1)}, s32[1,128]{1,0:T(1,128)S(1)}, /*inde...) while((s32[]{:T(128)}, f32[8,128]{1,0:T(8,128)S(1)}, ...), condition=%wide.region_7.8_spmd.clone, body=%wide.region_4.7_spmd.clone.sunk | while | flops 395748864 | bytes 38985104 | solution.py:165
  325.1 7.8 %fusion.89 = f32[128,512,32]{1,2,0:T(8,128)S(1)} fusion(f32[4,128,512]{2,1,0:T(8,128)S(1)} %pad_maximum_fusion.2, f32[4,32]{1,0:T(4,128)S(1)} %get-tuple-element.738), kind=kOutput, calls=%fused_computation.22.clone.1 | convolution fusion | flops 100663296 | bytes 9437696 | tf_op jit(solution)/shard_map/while/body/eval_jaxpr/cqk,ch->hqk/dot_general | solution.py:51
  332.9 7.2 %fusion.90 = f32[128,512,8]{1,2,0:T(8,128)S(1)} fusion(f32[128,512,32]{1,2,0:T(8,128)S(1)} %fusion.89, f32[32]{0:T(128)S(1)} %get-tuple-element.739, f32[32,8]{0,1:T(8,128)S(1)} %get-tuple-element.740), kind=kOutput, calls=%fused_computation.8.clone.1 | convolution fusion | flops 220200960 | bytes 10486912 | tf_op jit(solution)/shard_map/while/body/eval_jaxpr/hqk,hn->nqk/dot_general | solution.py:54
  340.1 1.9 copy.56
  342.2 1.1 constant_dynamic-slice_fusion.6
  343.4 2.2 select_reduce_fusion.2
  347.5 7.8 %fusion.89 = f32[128,512,32]{1,2,0:T(8,128)S(1)} fusion(f32[4,128,512]{2,1,0:T(8,128)S(1)} %pad_maximum_fusion.2, f32[4,32]{1,0:T(4,128)S(1)} %get-tuple-element.738), kind=kOutput, calls=%fused_computation.22.clone.1 | convolution fusion | flops 100663296 | bytes 9437696 | tf_op jit(solution)/shard_map/while/body/eval_jaxpr/cqk,ch->hqk/dot_general | solution.py:51
  355.3 7.2 %fusion.90 = f32[128,512,8]{1,2,0:T(8,128)S(1)} fusion(f32[128,512,32]{1,2,0:T(8,128)S(1)} %fusion.89, f32[32]{0:T(128)S(1)} %get-tuple-element.739, f32[32,8]{0,1:T(8,128)S(1)} %get-tuple-element.740), kind=kOutput, calls=%fused_computation.8.clone.1 | convolution fusion | flops 220200960 | bytes 10486912 | tf_op jit(solution)/shard_map/while/body/eval_jaxpr/hqk,hn->nqk/dot_general | solution.py:54
  362.5 1.9 copy.56
  364.6 1.1 constant_dynamic-slice_fusion.6
  365.8 2.2 select_reduce_fusion.2
  369.9 7.8 %fusion.89 = f32[128,512,32]{1,2,0:T(8,128)S(1)} fusion(f32[4,128,512]{2,1,0:T(8,128)S(1)} %pad_maximum_fusion.2, f32[4,32]{1,0:T(4,128)S(1)} %get-tuple-element.738), kind=kOutput, calls=%fused_computation.22.clone.1 | convolution fusion | flops 100663296 | bytes 9437696 | tf_op jit(solution)/shard_map/while/body/eval_jaxpr/cqk,ch->hqk/dot_general | solution.py:51
  377.7 7.2 %fusion.90 = f32[128,512,8]{1,2,0:T(8,128)S(1)} fusion(f32[128,512,32]{1,2,0:T(8,128)S(1)} %fusion.89, f32[32]{0:T(128)S(1)} %get-tuple-element.739, f32[32,8]{0,1:T(8,128)S(1)} %get-tuple-element.740), kind=kOutput, calls=%fused_computation.8.clone.1 | convolution fusion | flops 220200960 | bytes 10486912 | tf_op jit(solution)/shard_map/while/body/eval_jaxpr/hqk,hn->nqk/dot_general | solution.py:54
  384.9 1.9 copy.56
  386.9 1.1 constant_dynamic-slice_fusion.6
  388.2 2.2 select_reduce_fusion.2
  392.3 7.8 %fusion.89 = f32[128,512,32]{1,2,0:T(8,128)S(1)} fusion(f32[4,128,512]{2,1,0:T(8,128)S(1)} %pad_maximum_fusion.2, f32[4,32]{1,0:T(4,128)S(1)} %get-tuple-element.738), kind=kOutput, calls=%fused_computation.22.clone.1 | convolution fusion | flops 100663296 | bytes 9437696 | tf_op jit(solution)/shard_map/while/body/eval_jaxpr/cqk,ch->hqk/dot_general | solution.py:51
  400.1 7.2 %fusion.90 = f32[128,512,8]{1,2,0:T(8,128)S(1)} fusion(f32[128,512,32]{1,2,0:T(8,128)S(1)} %fusion.89, f32[32]{0:T(128)S(1)} %get-tuple-element.739, f32[32,8]{0,1:T(8,128)S(1)} %get-tuple-element.740), kind=kOutput, calls=%fused_computation.8.clone.1 | convolution fusion | flops 220200960 | bytes 10486912 | tf_op jit(solution)/shard_map/while/body/eval_jaxpr/hqk,hn->nqk/dot_general | solution.py:54
  407.3 1.9 copy.56
  409.3 1.1 constant_dynamic-slice_fusion.6
  410.6 2.2 select_reduce_fusion.2
  414.7 7.8 %fusion.89 = f32[128,512,32]{1,2,0:T(8,128)S(1)} fusion(f32[4,128,512]{2,1,0:T(8,128)S(1)} %pad_maximum_fusion.2, f32[4,32]{1,0:T(4,128)S(1)} %get-tuple-element.738), kind=kOutput, calls=%fused_computation.22.clone.1 | convolution fusion | flops 100663296 | bytes 9437696 | tf_op jit(solution)/shard_map/while/body/eval_jaxpr/cqk,ch->hqk/dot_general | solution.py:51
  422.5 7.2 %fusion.90 = f32[128,512,8]{1,2,0:T(8,128)S(1)} fusion(f32[128,512,32]{1,2,0:T(8,128)S(1)} %fusion.89, f32[32]{0:T(128)S(1)} %get-tuple-element.739, f32[32,8]{0,1:T(8,128)S(1)} %get-tuple-element.740), kind=kOutput, calls=%fused_computation.8.clone.1 | convolution fusion | flops 220200960 | bytes 10486912 | tf_op jit(solution)/shard_map/while/body/eval_jaxpr/hqk,hn->nqk/dot_general | solution.py:54
  429.7 1.9 copy.56
  431.7 1.1 constant_dynamic-slice_fusion.6
  432.9 2.2 select_reduce_fusion.2
  437.0 7.8 %fusion.89 = f32[128,512,32]{1,2,0:T(8,128)S(1)} fusion(f32[4,128,512]{2,1,0:T(8,128)S(1)} %pad_maximum_fusion.2, f32[4,32]{1,0:T(4,128)S(1)} %get-tuple-element.738), kind=kOutput, calls=%fused_computation.22.clone.1 | convolution fusion | flops 100663296 | bytes 9437696 | tf_op jit(solution)/shard_map/while/body/eval_jaxpr/cqk,ch->hqk/dot_general | solution.py:51
  444.9 7.2 %fusion.90 = f32[128,512,8]{1,2,0:T(8,128)S(1)} fusion(f32[128,512,32]{1,2,0:T(8,128)S(1)} %fusion.89, f32[32]{0:T(128)S(1)} %get-tuple-element.739, f32[32,8]{0,1:T(8,128)S(1)} %get-tuple-element.740), kind=kOutput, calls=%fused_computation.8.clone.1 | convolution fusion | flops 220200960 | bytes 10486912 | tf_op jit(solution)/shard_map/while/body/eval_jaxpr/hqk,hn->nqk/dot_general | solution.py:54
  452.1 1.9 copy.56
  454.1 1.1 constant_dynamic-slice_fusion.6
  455.3 2.2 select_reduce_fusion.2
  459.4 7.8 %fusion.89 = f32[128,512,32]{1,2,0:T(8,128)S(1)} fusion(f32[4,128,512]{2,1,0:T(8,128)S(1)} %pad_maximum_fusion.2, f32[4,32]{1,0:T(4,128)S(1)} %get-tuple-element.738), kind=kOutput, calls=%fused_computation.22.clone.1 | convolution fusion | flops 100663296 | bytes 9437696 | tf_op jit(solution)/shard_map/while/body/eval_jaxpr/cqk,ch->hqk/dot_general | solution.py:51
  467.3 7.2 %fusion.90 = f32[128,512,8]{1,2,0:T(8,128)S(1)} fusion(f32[128,512,32]{1,2,0:T(8,128)S(1)} %fusion.89, f32[32]{0:T(128)S(1)} %get-tuple-element.739, f32[32,8]{0,1:T(8,128)S(1)} %get-tuple-element.740), kind=kOutput, calls=%fused_computation.8.clone.1 | convolution fusion | flops 220200960 | bytes 10486912 | tf_op jit(solution)/shard_map/while/body/eval_jaxpr/hqk,hn->nqk/dot_general | solution.py:54
  474.5 1.9 copy.56
  476.5 1.1 constant_dynamic-slice_fusion.6
  477.7 2.2 select_reduce_fusion.2
  481.8 7.8 %fusion.89 = f32[128,512,32]{1,2,0:T(8,128)S(1)} fusion(f32[4,128,512]{2,1,0:T(8,128)S(1)} %pad_maximum_fusion.2, f32[4,32]{1,0:T(4,128)S(1)} %get-tuple-element.738), kind=kOutput, calls=%fused_computation.22.clone.1 | convolution fusion | flops 100663296 | bytes 9437696 | tf_op jit(solution)/shard_map/while/body/eval_jaxpr/cqk,ch->hqk/dot_general | solution.py:51
  489.6 7.2 %fusion.90 = f32[128,512,8]{1,2,0:T(8,128)S(1)} fusion(f32[128,512,32]{1,2,0:T(8,128)S(1)} %fusion.89, f32[32]{0:T(128)S(1)} %get-tuple-element.739, f32[32,8]{0,1:T(8,128)S(1)} %get-tuple-element.740), kind=kOutput, calls=%fused_computation.8.clone.1 | convolution fusion | flops 220200960 | bytes 10486912 | tf_op jit(solution)/shard_map/while/body/eval_jaxpr/hqk,hn->nqk/dot_general | solution.py:54
  496.8 1.9 copy.56
  500.1 2.2 select_reduce_fusion.2
  (145 shorter events, 21.9 us)
Async XLA Ops:
  6.5 496.9 %copy-start = (bf16[256,256]{1,0:T(8,128)(2,1)S(1)}, bf16[256,256]{1,0:T(8,128)(2,1)}, u32[]{:S(2)}) copy-start(bf16[256,256]{1,0:T(8,128)(2,1)} %param.23) | copy-start | bytes 393220
  6.5 317.8 %copy-start.2 = (s32[1,128]{1,0:T(1,128)S(1)}, s32[1,128]{1,0:T(1,128)}, u32[]{:S(2)}) copy-start(s32[1,128]{1,0:T(1,128)} %param.18) | copy-start | bytes 1540
  6.5 317.8 %copy-start.1 = (f32[4,32]{1,0:T(4,128)S(1)}, f32[4,32]{1,0:T(4,128)}, u32[]{:S(2)}) copy-start(f32[4,32]{1,0:T(4,128)} %param.25) | copy-start | bytes 1540
  6.5 317.8 %copy-start.5 = (f32[32]{0:T(128)S(1)}, f32[32]{0:T(128)}, u32[]{:S(2)}) copy-start(f32[32]{0:T(128)} %param.26) | copy-start | bytes 388
  6.5 317.8 %copy-start.4 = (f32[32,8]{0,1:T(8,128)S(1)}, f32[32,8]{0,1:T(8,128)}, u32[]{:S(2)}) copy-start(f32[32,8]{0,1:T(8,128)} %param.27) | copy-start | bytes 3076
  6.5 12.8 %all-to-all-start = ((bf16[1,4,128,256]{3,2,0,1:T(8,128)(2,1)}), bf16[1,4,128,256]{3,2,0,1:T(8,128)(2,1)S(1)}, u32[]{:S(2)}, u32[]{:S(2)}) async-start(bf16[1,4,128,256]{3,2,0,1:T(8,128)(2,1)} %bitcast.120), calls=%async_computation | async-start | bytes 524288 | tf_op jit(solution)/shard_map/all_to_all | solution.py:109
  11.8 164.9 %all-gather.3.cloned.1.call-start = ((), (), s32[]{:S(2)}) async-start(), calls=%async_computation.2 | async-start | bytes 2162688 | tf_op jit(solution)/shard_map/all_gather | solution.py:142
  22.3 302.0 %all-gather.5.cloned.1.call-start = ((), (), s32[]{:S(2)}) async-start(), calls=%async_computation.3 | async-start | bytes 2162688 | tf_op jit(solution)/shard_map/all_gather | solution.py:143
  24.1 76.0 %all-to-all-start.1 = ((bf16[1,4,4,128]{3,2,0,1:T(4,128)(2,1)}), bf16[1,4,4,128]{3,2,0,1:T(4,128)(2,1)S(1)}, u32[]{:S(2)}, u32[]{:S(2)}) async-start(bf16[1,4,4,128]{3,2,0,1:T(4,128)(2,1)} %bitcast.132), calls=%async_computation.1 | async-start | bytes 8192 | tf_op jit(solution)/shard_map/all_to_all | solution.py:110
  324.3 179.6 %copy-start.3 = (f32[256]{0:T(256)S(1)}, f32[256]{0:T(256)}, u32[]{:S(2)}) copy-start(f32[256]{0:T(256)} %param.24) | copy-start | bytes 3076
Sparse Core Ops, SparseCore 0:
  22.5 146.8 all-gather.2
  171.0 153.2 all-gather.4
where the time goes:
time: 518 us; the launch traced here: 512 us
  waiting for transfers between devices  154 us (30%)
  blocking collectives  148 us (29%)
  matrix products  147 us (28%)
  local copies, waits for them, and re-layouts  26.1 us (5%)
  between operations  13.5 us (3%)
  other arithmetic  12.8 us (2%)
  starting transfers between devices  8.59 us (2%)
    all_gather x1, waiting for transfers between devices, shards(): consume_value_cols = lax.all_gather(value_cols, 'blk', axis=1, tiled=True)  148 us
    all_gather x1, blocking collectives, shards(): kin_piece = lax.all_gather(kin_rows, 'blk', axis=1, tiled=True)  75.3 us
    all_gather x1, blocking collectives, shards(): id_piece = lax.all_gather(event_id, 'blk', axis=1, tiled=True)  72.7 us
    dot_general x8, matrix products, pair_bias(): jnp.einsum('cqk,ch->hqk', features, pair_w1, precision=exact_mode)  62.5 us
    dot_general x8, matrix products, pair_bias(): return jnp.einsum('hqk,hn->nqk', hidden, pair_w2, precision=exact_mode)  57.6 us
    dot_general x8, matrix products, attend_block(): jnp.einsum('qhd,hdk->hqk', queries, key_heads, preferred_element_type=jnp...  17.9 us
    dot_general x8, local copies, waits for them, and re-layouts, pair_bias(): return jnp.einsum('hqk,hn->nqk', hidden, pair_w2, precision=exact_mode)  15.1 us
  transfers between devices with their start and end apart: 4, of which 2 were waited for; matrix products, arithmetic and copies ran while one was open for 1% of the time, Pallas kernels for 0%

commit v1 on v0

v1 whole, which is shorter than its diff:
```python
import functools
import math

import jax
import jax.numpy as jnp
from jax import lax
from jax.experimental import pallas as pl
from jax.experimental.pallas import tpu as pltpu
from jax.sharding import PartitionSpec as P

MESH = pl.DeviceIdType.MESH
F32 = jnp.float32
BF16 = jnp.bfloat16
HIGHEST = lax.Precision.HIGHEST

KIN_ROWS = 16
GROUP = 8
UNIT = 16
TILE = 256

GELU_A = math.sqrt(2.0 / math.pi)
GELU_B = GELU_A * 0.044715
GELU_S = GELU_B ** (-1.0 / 3.0)
ALPHA = GELU_A * GELU_S
LOG2E = 1.0 / math.log(2.0)


def layer_norm(rows, gain):
    center = rows - jnp.mean(rows, axis=-1, keepdims=True)
    spread = jnp.mean(center * center, axis=-1, keepdims=True)
    return center * lax.rsqrt(spread + 1e-05) * gain


def exchange_kernel(
    n_grp,
    n_blk,
    raw_ref,
    kin_ref,
    reader_ref,
    event_ref,
    gain_ref,
    out_ref,
    inbox,
    kin_send,
    kin_in,
    block,
    send_sem,
    recv_sem,
    kin_send_sem,
    kin_recv_sem,
    all_send_sem,
    all_recv_sem,
    own_sem,
):
    g = lax.axis_index("grp")
    b = lax.axis_index("blk")
    slots = raw_ref.shape[2]
    barrier = pltpu.get_barrier_semaphore()
    for k in range(1, n_grp):
        pl.semaphore_signal(
            barrier, inc=1, device_id={"grp": lax.rem(g + k, n_grp)}, device_id_type=MESH
        )
    for k in range(1, n_blk):
        pl.semaphore_signal(
            barrier, inc=1, device_id={"blk": lax.rem(b + k, n_blk)}, device_id_type=MESH
        )
    kin_send[...] = jnp.zeros_like(kin_send)
    for k in range(n_grp):
        kin_send[k, 0:4, :] = kin_ref[0, k].astype(F32)
    pl.semaphore_wait(barrier, n_grp + n_blk - 2)

    copies = []
    for k in range(1, n_grp):
        to = lax.rem(g + k, n_grp)
        copy = pltpu.make_async_remote_copy(
            src_ref=raw_ref.at[0, to],
            dst_ref=inbox.at[n_grp - k],
            send_sem=send_sem.at[k],
            recv_sem=recv_sem.at[n_grp - k],
            device_id={"grp": to},
            device_id_type=MESH,
        )
        kin_copy = pltpu.make_async_remote_copy(
            src_ref=kin_send.at[to],
            dst_ref=kin_in.at[n_grp - k],
            send_sem=kin_send_sem.at[k],
            recv_sem=kin_recv_sem.at[n_grp - k],
            device_id={"grp": to},
            device_id_type=MESH,
        )
        copy.start()
        kin_copy.start()
        copies += [copy, kin_copy]

    reader = reader_ref[...]
    wanted = lax.rem(reader - g + n_grp, n_grp)
    column = jnp.broadcast_to(wanted, (slots, slots)).T
    kin = jnp.where(wanted == 0, kin_send[g, 0:4, :], 0.0)
    halves = [
        jnp.where(column == 0, raw_ref[0, g][:, h : h + slots].astype(F32), 0.0)
        for h in range(0, raw_ref.shape[3], slots)
    ]
    for copy in copies:
        copy.wait()
    for k in range(1, n_grp):
        kin = kin + jnp.where(wanted == k, kin_in[k, 0:4, :], 0.0)
        halves = [
            half
            + jnp.where(column == k, inbox[k][:, i * slots : (i + 1) * slots].astype(F32), 0.0)
            for i, half in enumerate(halves)
        ]
    tokens = jnp.concatenate(halves, axis=1)
    block[0:slots, :] = layer_norm(tokens, gain_ref[...]).astype(BF16)
    tail = jnp.concatenate(
        [
            jnp.concatenate(
                [kin, event_ref[...].astype(F32), jnp.zeros((KIN_ROWS - 5, slots), F32)], axis=0
            ),
            jnp.zeros((KIN_ROWS, raw_ref.shape[3] - slots), F32),
        ],
        axis=1,
    )
    block[slots : slots + KIN_ROWS, :] = tail.astype(BF16)

    own = pltpu.make_async_copy(block, out_ref.at[b], own_sem)
    own.start()

    def send(k, carry):
        pltpu.make_async_remote_copy(
            src_ref=block,
            dst_ref=out_ref.at[b],
            send_sem=all_send_sem,
            recv_sem=all_recv_sem,
            device_id={"blk": lax.rem(b + k, n_blk)},
            device_id_type=MESH,
        ).start()
        return carry

    lax.fori_loop(1, n_blk, send, 0)
    own.wait()
    every = pltpu.make_async_remote_copy(
        src_ref=out_ref.at[pl.ds(0, n_blk - 1)],
        dst_ref=out_ref.at[pl.ds(0, n_blk - 1)],
        send_sem=all_send_sem,
        recv_sem=all_recv_sem,
        device_id={"blk": lax.rem(b + 1, n_blk)},
        device_id_type=MESH,
    )
    every.wait()


def split_two(value):
    high = value.astype(BF16)
    low = (value - high.astype(F32)).astype(BF16)
    return high, low


def spread_over(weight):
    m, c = weight.shape
    up = (
        lax.broadcasted_iota(jnp.int32, (m * GROUP, m), 0) // GROUP
        == lax.broadcasted_iota(jnp.int32, (m * GROUP, m), 1)
    ).astype(F32)
    across = (
        lax.broadcasted_iota(jnp.int32, (c, c * GROUP), 1) // GROUP
        == lax.broadcasted_iota(jnp.int32, (c, c * GROUP), 0)
    ).astype(F32)
    tall = jnp.dot(up, weight, precision=HIGHEST, preferred_element_type=F32)
    wide = jnp.dot(tall, across, precision=HIGHEST, preferred_element_type=F32)
    same = (
        lax.broadcasted_iota(jnp.int32, (m * GROUP, c * GROUP), 0) % GROUP
        == lax.broadcasted_iota(jnp.int32, (m * GROUP, c * GROUP), 1) % GROUP
    )
    return jnp.where(same, wide, 0.0)


def attend_kernel(
    heads,
    x_ref,
    wq_ref,
    wk_ref,
    wv_ref,
    wo_ref,
    gain_ref,
    w1_ref,
    b1_ref,
    w2_ref,
    out_ref,
    kt_ref,
    v_ref,
    terms,
    q_terms,
    q_ref,
    qm_ref,
    s_ref,
    acc_ref,
    att_ref,
    wfirst,
    wsecond,
):
    n_blk = x_ref.shape[0]
    own_rows = out_ref.shape[0]
    width = out_ref.shape[1]
    head_size = width // heads
    hid = w1_ref.shape[1]
    feats = w1_ref.shape[0]
    per_tile = TILE // own_rows
    b = lax.axis_index("blk")
    root = math.sqrt(head_size)

    w1 = w1_ref[...]
    b1 = b1_ref[...]
    w2 = w2_ref[...]
    first = jnp.concatenate([w1, b1, jnp.zeros((8 - feats - 1, hid), F32)], axis=0)
    line = jnp.dot(first, w2, precision=HIGHEST, preferred_element_type=F32) * (0.5 * root)
    stacked = jnp.concatenate([first.T * (1.0 / GELU_S), line.T], axis=0)
    big = spread_over(stacked)
    high, low = split_two(big)
    part = feats * GROUP
    wfirst[:, 0:part] = high[:, 0:part]
    wfirst[:, part : 2 * part] = high[:, 0:part]
    wfirst[:, 2 * part : 3 * part] = low[:, 0:part]
    wfirst[:, 3 * part : 3 * part + GROUP] = high[:, part : part + GROUP]
    wfirst[:, 3 * part + GROUP : 3 * part + 2 * GROUP] = low[:, part : part + GROUP]
    wsecond[...] = spread_over(w2.T * (0.5 * root * GELU_S)).astype(BF16)

    tab = x_ref[:, own_rows : own_rows + 8, 0:own_rows].astype(F32)
    mom, rap, azi, mass, ids = [tab[:, i, :] for i in range(5)]
    trans = jnp.sqrt(mom * mom + mass * mass)
    grow = jnp.exp(rap)
    shrink = jnp.exp(-rap)
    for i, term in enumerate(
        [mom, rap, jnp.cos(azi), jnp.sin(azi), trans * grow, trans * shrink, mass * mass, ids]
    ):
        terms[i] = term
    for i in range(8):
        q_terms[i] = jnp.broadcast_to(terms[i, pl.ds(b, 1), :], (own_rows, own_rows)).T

    q_ref[...] = jnp.dot(
        x_ref[b, 0:own_rows, :], wq_ref[...], preferred_element_type=F32
    )

    n_units = own_rows // UNIT
    lows = []
    ends = []
    for u in range(n_units):
        begin = q_terms[7, pl.ds(u * UNIT, 1), :]
        finish = q_terms[7, pl.ds(u * UNIT + UNIT - 1, 1), :]
        lows.append(jnp.sum((ids < begin).astype(jnp.int32)) // TILE)
        ends.append((jnp.sum((ids <= finish).astype(jnp.int32)) + TILE - 1) // TILE)

    wkt = wk_ref[...].astype(F32).T.astype(BF16)

    def project(t, carry):
        for i in range(per_tile):
            rows = x_ref[t * per_tile + i, 0:own_rows, :]
            start = pl.multiple_of(t * TILE + i * own_rows, own_rows)
            kt_ref[:, pl.ds(start, own_rows)] = lax.dot_general(
                wkt, rows, (((1,), (1,)), ((), ())), preferred_element_type=F32
            ).astype(BF16)
            v_ref[pl.ds(start, own_rows), :] = jnp.dot(
                rows, wv_ref[...], preferred_element_type=F32
            ).astype(BF16)
        return carry

    lax.fori_loop(lows[0], ends[-1], project, 0)

    lane_head = lax.broadcasted_iota(jnp.int32, (GROUP, width), 1) // head_size
    groups = UNIT // GROUP
    rows_g = heads * GROUP

    for u in range(n_units):
        for g in range(groups):
            base = u * UNIT + g * GROUP
            rows = q_ref[pl.ds(base, GROUP), :]
            qm_ref[g * rows_g : (g + 1) * rows_g, :] = jnp.concatenate(
                [jnp.where(lane_head == h, rows, 0.0) for h in range(heads)], axis=0
            ).astype(BF16)

        def score(t, run_max, u=u):
            start = pl.multiple_of(t * TILE, TILE)
            products = jnp.dot(
                qm_ref[...], kt_ref[:, pl.ds(start, TILE)], preferred_element_type=F32
            )
            parts = []
            for g in range(groups):
                base = u * UNIT + g * GROUP
                qt = [q_terms[i, pl.ds(base, GROUP), :] for i in range(8)]
                columns = []
                lives = []
                for i in range(per_tile):
                    kt = [terms[j, pl.ds(t * per_tile + i, 1), :] for j in range(8)]
                    gap = qt[1] - kt[1]
                    cos_gap = qt[2] * kt[2] + qt[3] * kt[3]
                    dist = gap * gap + (2.0 - 2.0 * cos_gap)
                    small = jnp.minimum(qt[0], kt[0])
                    msq = (
                        qt[6]
                        + kt[6]
                        + (qt[4] * kt[5] + qt[5] * kt[4] - 2.0 * (qt[0] * kt[0] * cos_gap))
                    )
                    f = [
                        jnp.log(1.0 + dist),
                        jnp.log(1.0 + small * small * dist),
                        small / (qt[0] + kt[0]),
                        jnp.log(1.0 + msq),
                    ]
                    f = jnp.concatenate(f, axis=0)
                    fh, fl = split_two(f)
                    columns.append(
                        jnp.concatenate([fh, fl, fh, jnp.ones((2 * GROUP, own_rows), BF16)], axis=0)
                    )
                    lives.append(qt[7] == kt[7])
                x = jnp.concatenate(columns, axis=1)
                z = jnp.dot(wfirst[...], x, preferred_element_type=F32)
                inner = z[0 : hid * GROUP].astype(BF16)
                turn = jnp.tanh(inner * (ALPHA + inner * inner))
                bias = (
                    jnp.dot(wsecond[...], inner * turn, preferred_element_type=F32)
                    + z[hid * GROUP :]
                )
                s = products[g * rows_g : (g + 1) * rows_g] + bias
                live = jnp.concatenate(lives, axis=1)
                s = jnp.where(live[None], s.reshape(heads, GROUP, TILE), -1e30)
                parts.append(s.reshape(rows_g, TILE))
            s = jnp.concatenate(parts, axis=0)
            s_ref[:, pl.ds(start, TILE)] = s
            for i in range(0, TILE, 128):
                run_max = jnp.maximum(run_max, s[:, i : i + 128])
            return run_max

        run_max = lax.fori_loop(
            lows[u], ends[u], score, jnp.full((groups * rows_g, 128), -1e30, F32)
        )
        top = jnp.max(run_max, axis=1, keepdims=True)
        acc_ref[...] = jnp.zeros_like(acc_ref)

        def gather(t, total):
            start = pl.multiple_of(t * TILE, TILE)
            weight = jnp.exp2((s_ref[:, pl.ds(start, TILE)] - top) * (LOG2E / root))
            acc_ref[...] += jnp.dot(
                weight.astype(BF16), v_ref[pl.ds(start, TILE), :], preferred_element_type=F32
            )
            for i in range(0, TILE, 128):
                total = total + weight[:, i : i + 128]
            return total

        total = lax.fori_loop(
            lows[u], ends[u], gather, jnp.zeros((groups * rows_g, 128), F32)
        )
        total = jnp.sum(total, axis=1, keepdims=True)
        for g in range(groups):
            out = jnp.zeros((GROUP, width), F32)
            for h in range(heads):
                at = g * rows_g + h * GROUP
                scaled = acc_ref[at : at + GROUP, :] / total[at : at + GROUP]
                out = jnp.where(lane_head == h, scaled, out)
            att_ref[u * UNIT + g * GROUP : u * UNIT + (g + 1) * GROUP, :] = out

    mixed = jnp.dot(att_ref[...].astype(BF16), wo_ref[...], preferred_element_type=F32)
    out_ref[...] = layer_norm(mixed, gain_ref[...]).astype(BF16)


def shards(
    n_grp,
    n_blk,
    raw,
    raw_kin,
    reader,
    event_id,
    pre_gain,
    w_query,
    w_key,
    w_value,
    w_out,
    post_gain,
    pair_w1,
    pair_b1,
    pair_w2,
):
    slots, width = raw.shape[2], raw.shape[3]
    heads = pair_w2.shape[1]
    vmem = pl.BlockSpec(memory_space=pltpu.VMEM)
    gathered = pl.pallas_call(
        functools.partial(exchange_kernel, n_grp, n_blk),
        out_shape=jax.ShapeDtypeStruct((n_blk, slots + KIN_ROWS, width), BF16),
        in_specs=[vmem] * 5,
        out_specs=pl.BlockSpec(memory_space=pl.ANY),
        scratch_shapes=[
            pltpu.VMEM((n_grp, slots, width), BF16),
            pltpu.VMEM((n_grp, 8, slots), F32),
            pltpu.VMEM((n_grp, 8, slots), F32),
            pltpu.VMEM((slots + KIN_ROWS, width), BF16),
            pltpu.SemaphoreType.DMA((n_grp,)),
            pltpu.SemaphoreType.DMA((n_grp,)),
            pltpu.SemaphoreType.DMA((n_grp,)),
            pltpu.SemaphoreType.DMA((n_grp,)),
            pltpu.SemaphoreType.DMA,
            pltpu.SemaphoreType.DMA,
            pltpu.SemaphoreType.DMA,
        ],
        compiler_params=pltpu.CompilerParams(collective_id=0, has_side_effects=True),
        name="exchange",
    )(raw, raw_kin, reader, event_id, pre_gain[None])

    keys = n_blk * slots
    feats, hid = pair_w1.shape
    rows_u = heads * UNIT
    encoded = pl.pallas_call(
        functools.partial(attend_kernel, heads),
        out_shape=jax.ShapeDtypeStruct((slots, width), BF16),
        in_specs=[vmem] * 9,
        out_specs=vmem,
        scratch_shapes=[
            pltpu.VMEM((width, keys), BF16),
            pltpu.VMEM((keys, width), BF16),
            pltpu.VMEM((8, n_blk, slots), F32),
            pltpu.VMEM((8, slots, slots), F32),
            pltpu.VMEM((slots, width), F32),
            pltpu.VMEM((rows_u, width), BF16),
            pltpu.VMEM((rows_u, keys), F32),
            pltpu.VMEM((rows_u, width), F32),
            pltpu.VMEM((slots, width), F32),
            pltpu.VMEM(((hid + heads) * GROUP, (3 * feats + 2) * GROUP), BF16),
            pltpu.VMEM((heads * GROUP, hid * GROUP), BF16),
        ],
        compiler_params=pltpu.CompilerParams(vmem_limit_bytes=40 * 1024 * 1024),
        name="attend",
    )(
        gathered,
        w_query,
        w_key,
        w_value,
        w_out,
        post_gain[None],
        pair_w1,
        pair_b1[None],
        pair_w2,
    )
    return encoded[None]


def solution(mesh):
    in_specs = (
        P("grp", None, "blk", None),
        P("grp", None, None, "blk"),
        P("grp", "blk"),
        P("grp", "blk"),
        P(),
        P(),
        P(),
        P(),
        P(),
        P(),
        P(),
        P(),
        P(),
    )
    out_specs = P("grp", "blk", None)
    body = functools.partial(shards, mesh.shape["grp"], mesh.shape["blk"])
    return jax.shard_map(body, mesh=mesh, in_specs=in_specs, out_specs=out_specs, check_vma=False)
```

time: 518 us -> 113 us (0.22)
  the two profiles are of different devices: /device:TPU:8 before, /device:TPU:32 now
where the time goes in v1:
time: 113 us
  Pallas kernels  111 us (98%)
  local copies, waits for them, and re-layouts  2.54 us (2%)
    pallas_call x1, Pallas kernels, shards(): pl.pallas_call(functools.partial(attend_kernel, heads), out_shape=jax.Sha...  59.7 us
    pallas_call x1, Pallas kernels, shards(): pl.pallas_call(functools.partial(exchange_kernel, n_grp, n_blk), out_shap...  50.9 us
    unnamed x17, local copies, waits for them, and re-layouts  2.54 us

profile of v1, /device:TPU:32, one launch (start us, length us, event | category | flops | bytes accessed | tf_op | source)
XLA Modules:
  0.0 113.2 jit_solution(12654949987551158522)
XLA Ops:
  0.0 0.0 copy-start.7
  0.0 0.0 copy-start.5
  0.0 0.0 copy-start.6
  0.0 0.0 copy-start.4
  0.0 0.0 copy-start.3
  0.0 0.0 copy-start.2
  0.0 0.0 copy-start.1
  0.0 0.9 copy.14.w2_ref
  0.9 50.9 %exchange.1.x_ref = bf16[32,144,256]{2,1,0:T(8,128)(2,1)} custom-call(bf16[1,4,128,256]{3,2,1,0:T(8,128)(2,1)} %raw_ref.1, bf16[1,4,4,128]{3,2,1,0:T(4,128)(2,1)} %kin_ref.1, s32[1,128]{1,0:T(1,128)} %reader_ref.1, s32[1,128]{1,0:T(1,128)} %event_ref.1, f32[1,256]{1,0:T(1,128)} %bitcast.6), custom_call_target="tpu_custom_call" | custom-call | tf_op jit(solution)/shard_map/exchange/pallas_call | solution.py:384
  51.8 0.0 copy-done.7
  51.8 0.0 copy-done.5
  51.8 0.0 copy-done.6
  51.8 0.0 copy-done.4
  51.8 0.0 copy-done.3
  51.8 0.0 copy-done.2
  51.9 0.0 copy-done.1
  51.9 0.0 copy-start
  51.9 1.7 %copy-done = bf16[32,144,256]{2,1,0:T(8,128)(2,1)S(1)} copy-done((bf16[32,144,256]{2,1,0:T(8,128)(2,1)S(1)}, bf16[32,144,256]{2,1,0:T(8,128)(2,1)}, u32[]{:S(2)}) %copy-start) | copy-done | bytes 2359320
  53.5 59.7 %attend.1 = bf16[128,256]{1,0:T(8,128)(2,1)} custom-call(bf16[32,144,256]{2,1,0:T(8,128)(2,1)S(1)} %copy-done, bf16[256,256]{1,0:T(8,128)(2,1)S(1)} %copy-done.1, bf16[256,256]{1,0:T(8,128)(2,1)S(1)} %copy-done.2, bf16[256,256]{1,0:T(8,128)(2,1)S(1)} %copy-done.3, bf16[256,256]{1,0:T(8,128)(2,1)S(1)} %copy-done.4, f32[1,256]{1,0:T(1,128)S(1)} %bitcast.4, ...), custom_call_target="tpu_custom_call" | custom-call | tf_op jit(solution)/shard_map/attend/pallas_call | solution.py:409
Async XLA Ops:
  0.0 51.8 %copy-start.7 = (f32[32]{0:T(128)S(1)}, f32[32]{0:T(128)}, u32[]{:S(2)}) copy-start(f32[32]{0:T(128)} %param.24) | copy-start | bytes 388
  0.0 51.8 %copy-start.5 = (f32[4,32]{1,0:T(4,128)S(1)}, f32[4,32]{1,0:T(4,128)}, u32[]{:S(2)}) copy-start(f32[4,32]{1,0:T(4,128)} %w1_ref.1) | copy-start | bytes 1540
  0.0 51.8 %copy-start.6 = (f32[256]{0:T(256)S(1)}, f32[256]{0:T(256)}, u32[]{:S(2)}) copy-start(f32[256]{0:T(256)} %param.22) | copy-start | bytes 3076
  0.0 51.8 %copy-start.4 = (bf16[256,256]{1,0:T(8,128)(2,1)S(1)}, bf16[256,256]{1,0:T(8,128)(2,1)}, u32[]{:S(2)}) copy-start(bf16[256,256]{1,0:T(8,128)(2,1)} %wo_ref.1) | copy-start | bytes 393220
  0.0 51.8 %copy-start.3 = (bf16[256,256]{1,0:T(8,128)(2,1)S(1)}, bf16[256,256]{1,0:T(8,128)(2,1)}, u32[]{:S(2)}) copy-start(bf16[256,256]{1,0:T(8,128)(2,1)} %wv_ref.1) | copy-start | bytes 393220
  0.0 51.8 %copy-start.2 = (bf16[256,256]{1,0:T(8,128)(2,1)S(1)}, bf16[256,256]{1,0:T(8,128)(2,1)}, u32[]{:S(2)}) copy-start(bf16[256,256]{1,0:T(8,128)(2,1)} %wk_ref.1) | copy-start | bytes 393220
  0.0 51.8 %copy-start.1 = (bf16[256,256]{1,0:T(8,128)(2,1)S(1)}, bf16[256,256]{1,0:T(8,128)(2,1)}, u32[]{:S(2)}) copy-start(bf16[256,256]{1,0:T(8,128)(2,1)} %wq_ref.1) | copy-start | bytes 393220
  51.9 1.7 %copy-start = (bf16[32,144,256]{2,1,0:T(8,128)(2,1)S(1)}, bf16[32,144,256]{2,1,0:T(8,128)(2,1)}, u32[]{:S(2)}) copy-start(bf16[32,144,256]{2,1,0:T(8,128)(2,1)} %exchange.1.x_ref) | copy-start | bytes 7077892

commit v2 on v1

--- a/solution.py
+++ b/solution.py
@@ -190,38 +190,49 @@
     v_ref,
     terms,
     q_terms,
-    q_ref,
     qm_ref,
     s_ref,
+    top_ref,
+    total_ref,
     acc_ref,
     att_ref,
     wfirst,
+    wline,
     wsecond,
+    fresh,
+    aged,
+    turned,
+    weight_ref,
+    limits,
 ):
-    n_blk = x_ref.shape[0]
-    own_rows = out_ref.shape[0]
-    width = out_ref.shape[1]
+    own_rows, width = out_ref.shape
     head_size = width // heads
-    hid = w1_ref.shape[1]
-    feats = w1_ref.shape[0]
+    feats, hid = w1_ref.shape
     per_tile = TILE // own_rows
     b = lax.axis_index("blk")
     root = math.sqrt(head_size)
+    groups = UNIT // GROUP
+    rows_g = heads * GROUP
+    rows_u = groups * rows_g
+    n_units = own_rows // UNIT
 
     w1 = w1_ref[...]
     b1 = b1_ref[...]
     w2 = w2_ref[...]
     first = jnp.concatenate([w1, b1, jnp.zeros((8 - feats - 1, hid), F32)], axis=0)
     line = jnp.dot(first, w2, precision=HIGHEST, preferred_element_type=F32) * (0.5 * root)
-    stacked = jnp.concatenate([first.T * (1.0 / GELU_S), line.T], axis=0)
-    big = spread_over(stacked)
-    high, low = split_two(big)
     part = feats * GROUP
-    wfirst[:, 0:part] = high[:, 0:part]
-    wfirst[:, part : 2 * part] = high[:, 0:part]
-    wfirst[:, 2 * part : 3 * part] = low[:, 0:part]
-    wfirst[:, 3 * part : 3 * part + GROUP] = high[:, part : part + GROUP]
-    wfirst[:, 3 * part + GROUP : 3 * part + 2 * GROUP] = low[:, part : part + GROUP]
+
+    def lay(ref, weight):
+        high, low = split_two(spread_over(weight))
+        ref[:, 0:part] = high[:, 0:part]
+        ref[:, part : 2 * part] = high[:, 0:part]
+        ref[:, 2 * part : 3 * part] = low[:, 0:part]
+        ref[:, 3 * part : 3 * part + GROUP] = high[:, part : part + GROUP]
+        ref[:, 3 * part + GROUP : 3 * part + 2 * GROUP] = low[:, part : part + GROUP]
+
+    lay(wfirst, first.T * (1.0 / GELU_S))
+    lay(wline, line.T)
     wsecond[...] = spread_over(w2.T * (0.5 * root * GELU_S)).astype(BF16)
 
     tab = x_ref[:, own_rows : own_rows + 8, 0:own_rows].astype(F32)
@@ -236,18 +247,11 @@
     for i in range(8):
         q_terms[i] = jnp.broadcast_to(terms[i, pl.ds(b, 1), :], (own_rows, own_rows)).T
 
-    q_ref[...] = jnp.dot(
-        x_ref[b, 0:own_rows, :], wq_ref[...], preferred_element_type=F32
-    )
-
-    n_units = own_rows // UNIT
-    lows = []
-    ends = []
     for u in range(n_units):
         begin = q_terms[7, pl.ds(u * UNIT, 1), :]
         finish = q_terms[7, pl.ds(u * UNIT + UNIT - 1, 1), :]
-        lows.append(jnp.sum((ids < begin).astype(jnp.int32)) // TILE)
-        ends.append((jnp.sum((ids <= finish).astype(jnp.int32)) + TILE - 1) // TILE)
+        limits[0, u] = jnp.sum((ids < begin).astype(jnp.int32)) // TILE
+        limits[1, u] = (jnp.sum((ids <= finish).astype(jnp.int32)) + TILE - 1) // TILE
 
     wkt = wk_ref[...].astype(F32).T.astype(BF16)
 
@@ -263,99 +267,151 @@
             ).astype(BF16)
         return carry
 
-    lax.fori_loop(lows[0], ends[-1], project, 0)
+    lax.fori_loop(limits[0, 0], limits[1, n_units - 1], project, 0)
 
     lane_head = lax.broadcasted_iota(jnp.int32, (GROUP, width), 1) // head_size
-    groups = UNIT // GROUP
-    rows_g = heads * GROUP
-
-    for u in range(n_units):
+    queries = jnp.dot(x_ref[b, 0:own_rows, :], wq_ref[...], preferred_element_type=F32)
+    for base in range(0, own_rows, GROUP):
+        rows = queries[base : base + GROUP]
+        qm_ref[base * heads : base * heads + rows_g, :] = jnp.concatenate(
+            [jnp.where(lane_head == h, rows, 0.0) for h in range(heads)], axis=0
+        ).astype(BF16)
+
+    top_ref[...] = jnp.full_like(top_ref, -1e30)
+    total_ref[...] = jnp.zeros_like(total_ref)
+    acc_ref[...] = jnp.zeros_like(acc_ref)
+
+    def following(u, t):
+        more = t + 1 < limits[1, u]
+        then = jnp.where(more, u, jnp.minimum(u + 1, n_units - 1))
+        return then, jnp.where(more, t + 1, limits[0, then])
+
+    steps = limits[1, 0] - limits[0, 0]
+    for u in range(1, n_units):
+        steps = steps + limits[1, u] - limits[0, u]
+
+    def features(u, t):
         for g in range(groups):
-            base = u * UNIT + g * GROUP
-            rows = q_ref[pl.ds(base, GROUP), :]
-            qm_ref[g * rows_g : (g + 1) * rows_g, :] = jnp.concatenate(
-                [jnp.where(lane_head == h, rows, 0.0) for h in range(heads)], axis=0
-            ).astype(BF16)
-
-        def score(t, run_max, u=u):
-            start = pl.multiple_of(t * TILE, TILE)
-            products = jnp.dot(
-                qm_ref[...], kt_ref[:, pl.ds(start, TILE)], preferred_element_type=F32
+            base = pl.multiple_of(u * UNIT + g * GROUP, GROUP)
+            qt = [q_terms[i, pl.ds(base, GROUP), :] for i in range(7)]
+            columns = []
+            for i in range(per_tile):
+                kt = [terms[j, pl.ds(t * per_tile + i, 1), :] for j in range(7)]
+                gap = qt[1] - kt[1]
+                cos_gap = qt[2] * kt[2] + qt[3] * kt[3]
+                dist = gap * gap + (2.0 - 2.0 * cos_gap)
+                small = jnp.minimum(qt[0], kt[0])
+                msq = (
+                    qt[6]
+                    + kt[6]
+                    + (qt[4] * kt[5] + qt[5] * kt[4] - 2.0 * (qt[0] * kt[0] * cos_gap))
+                )
+                f = [
+                    jnp.log(1.0 + dist),
+                    jnp.log(1.0 + small * small * dist),
+                    small / (qt[0] + kt[0]),
+                    jnp.log(1.0 + msq),
+                ]
+                fh, fl = split_two(jnp.concatenate(f, axis=0))
+                columns.append(
+                    jnp.concatenate([fh, fl, fh, jnp.ones((2 * GROUP, own_rows), BF16)], axis=0)
+                )
+            fresh[g] = jnp.concatenate(columns, axis=1)
+
+    def gelus():
+        for g in range(groups):
+            x = fresh[g]
+            aged[g] = x
+            inner = jnp.dot(wfirst[...], x, preferred_element_type=F32).astype(BF16)
+            turned[g] = inner * jnp.tanh(inner * (ALPHA + inner * inner))
+
+    def scores(u, t, away):
+        start = pl.multiple_of(t * TILE, TILE)
+        first_row = pl.multiple_of(u * rows_u, rows_u)
+        products = jnp.dot(
+            qm_ref[pl.ds(first_row, rows_u), :],
+            kt_ref[:, pl.ds(start, TILE)],
+            preferred_element_type=F32,
+        )
+        for g in range(groups):
+            base = pl.multiple_of(u * UNIT + g * GROUP, GROUP)
+            bias = jnp.dot(wsecond[...], turned[g], preferred_element_type=F32) + jnp.dot(
+                wline[...], aged[g], preferred_element_type=F32
             )
-            parts = []
-            for g in range(groups):
-                base = u * UNIT + g * GROUP
-                qt = [q_terms[i, pl.ds(base, GROUP), :] for i in range(8)]
-                columns = []
-                lives = []
-                for i in range(per_tile):
-                    kt = [terms[j, pl.ds(t * per_tile + i, 1), :] for j in range(8)]
-                    gap = qt[1] - kt[1]
-                    cos_gap = qt[2] * kt[2] + qt[3] * kt[3]
-                    dist = gap * gap + (2.0 - 2.0 * cos_gap)
-                    small = jnp.minimum(qt[0], kt[0])
-                    msq = (
-                        qt[6]
-                        + kt[6]
-                        + (qt[4] * kt[5] + qt[5] * kt[4] - 2.0 * (qt[0] * kt[0] * cos_gap))
-                    )
-                    f = [
-                        jnp.log(1.0 + dist),
-                        jnp.log(1.0 + small * small * dist),
-                        small / (qt[0] + kt[0]),
-                        jnp.log(1.0 + msq),
-                    ]
-                    f = jnp.concatenate(f, axis=0)
-                    fh, fl = split_two(f)
-                    columns.append(
-                        jnp.concatenate([fh, fl, fh, jnp.ones((2 * GROUP, own_rows), BF16)], axis=0)
-                    )
-                    lives.append(qt[7] == kt[7])
-                x = jnp.concatenate(columns, axis=1)
-                z = jnp.dot(wfirst[...], x, preferred_element_type=F32)
-                inner = z[0 : hid * GROUP].astype(BF16)
-                turn = jnp.tanh(inner * (ALPHA + inner * inner))
-                bias = (
-                    jnp.dot(wsecond[...], inner * turn, preferred_element_type=F32)
-                    + z[hid * GROUP :]
-                )
-                s = products[g * rows_g : (g + 1) * rows_g] + bias
-                live = jnp.concatenate(lives, axis=1)
-                s = jnp.where(live[None], s.reshape(heads, GROUP, TILE), -1e30)
-                parts.append(s.reshape(rows_g, TILE))
-            s = jnp.concatenate(parts, axis=0)
-            s_ref[:, pl.ds(start, TILE)] = s
+            s = products[g * rows_g : (g + 1) * rows_g] + bias
+            own = q_terms[7, pl.ds(base, GROUP), :] + away
+            live = jnp.concatenate(
+                [own == terms[7, pl.ds(t * per_tile + i, 1), :] for i in range(per_tile)], axis=1
+            )
+            s = jnp.where(live[None], s.reshape(heads, GROUP, TILE), -1e30).reshape(rows_g, TILE)
+            at = pl.ds(pl.multiple_of(first_row + g * rows_g, rows_g), rows_g)
+            s_ref[at, pl.ds(start, TILE)] = s
+            run_max = top_ref[at, :]
             for i in range(0, TILE, 128):
                 run_max = jnp.maximum(run_max, s[:, i : i + 128])
-            return run_max
-
-        run_max = lax.fori_loop(
-            lows[u], ends[u], score, jnp.full((groups * rows_g, 128), -1e30, F32)
-        )
-        top = jnp.max(run_max, axis=1, keepdims=True)
-        acc_ref[...] = jnp.zeros_like(acc_ref)
-
-        def gather(t, total):
-            start = pl.multiple_of(t * TILE, TILE)
-            weight = jnp.exp2((s_ref[:, pl.ds(start, TILE)] - top) * (LOG2E / root))
-            acc_ref[...] += jnp.dot(
-                weight.astype(BF16), v_ref[pl.ds(start, TILE), :], preferred_element_type=F32
-            )
-            for i in range(0, TILE, 128):
-                total = total + weight[:, i : i + 128]
-            return total
-
-        total = lax.fori_loop(
-            lows[u], ends[u], gather, jnp.zeros((groups * rows_g, 128), F32)
-        )
-        total = jnp.sum(total, axis=1, keepdims=True)
-        for g in range(groups):
-            out = jnp.zeros((GROUP, width), F32)
-            for h in range(heads):
-                at = g * rows_g + h * GROUP
-                scaled = acc_ref[at : at + GROUP, :] / total[at : at + GROUP]
-                out = jnp.where(lane_head == h, scaled, out)
-            att_ref[u * UNIT + g * GROUP : u * UNIT + (g + 1) * GROUP, :] = out
+            top_ref[at, :] = run_max
+
+    def score_step(i, carry):
+        u0, t0, u1, t1, u2, t2 = carry
+        scores(u2, t2, jnp.where(i >= 2, 0.0, 100.0))
+        gelus()
+        features(u0, t0)
+        return (*following(u0, t0), u0, t0, u1, t1)
+
+    zero = jnp.int32(0)
+    t_first = limits[0, 0]
+    _, _, u1, t1, u2, t2 = lax.fori_loop(
+        0, steps, score_step, (zero, t_first, zero, t_first, zero, t_first)
+    )
+    scores(u2, t2, jnp.where(steps >= 2, 0.0, 100.0))
+    gelus()
+    scores(u1, t1, 0.0)
+
+    for u in range(n_units):
+        at = slice(u * rows_u, (u + 1) * rows_u)
+        top_ref[at, :] = jnp.broadcast_to(
+            jnp.max(top_ref[at, :], axis=1, keepdims=True), (rows_u, 128)
+        )
+
+    weight_ref[...] = jnp.zeros_like(weight_ref)
+
+    def apply(u, t):
+        at = pl.ds(pl.multiple_of(u * rows_u, rows_u), rows_u)
+        acc_ref[at, :] += jnp.dot(
+            weight_ref[...],
+            v_ref[pl.ds(pl.multiple_of(t * TILE, TILE), TILE), :],
+            preferred_element_type=F32,
+        )
+
+    def weigh(u, t):
+        at = pl.ds(pl.multiple_of(u * rows_u, rows_u), rows_u)
+        top = top_ref[at, :]
+        total = total_ref[at, :]
+        for i in range(0, TILE, 128):
+            cols = pl.ds(pl.multiple_of(t * TILE + i, 128), 128)
+            weight = jnp.exp2((s_ref[at, cols] - top) * (LOG2E / root))
+            total = total + weight
+            weight_ref[:, i : i + 128] = weight.astype(BF16)
+        total_ref[at, :] = total
+
+    def value_step(i, carry):
+        u0, t0, u1, t1 = carry
+        apply(u1, t1)
+        weigh(u0, t0)
+        return (*following(u0, t0), u0, t0)
+
+    _, _, u1, t1 = lax.fori_loop(0, steps, value_step, (zero, t_first, zero, t_first))
+    apply(u1, t1)
+
+    for base in range(0, own_rows, GROUP):
+        at = base * heads
+        total = 1.0 / jnp.sum(total_ref[at : at + rows_g, :], axis=1, keepdims=True)
+        out = jnp.zeros((GROUP, width), F32)
+        for h in range(heads):
+            rows = slice(at + h * GROUP, at + (h + 1) * GROUP)
+            scaled = acc_ref[rows, :] * total[h * GROUP : (h + 1) * GROUP]
+            out = jnp.where(lane_head == h, scaled, out)
+        att_ref[base : base + GROUP, :] = out
 
     mixed = jnp.dot(att_ref[...].astype(BF16), wo_ref[...], preferred_element_type=F32)
     out_ref[...] = layer_norm(mixed, gain_ref[...]).astype(BF16)
@@ -405,7 +461,9 @@
 
     keys = n_blk * slots
     feats, hid = pair_w1.shape
-    rows_u = heads * UNIT
+    groups = UNIT // GROUP
+    rows_all = heads * slots
+    mixing = (3 * feats + 2) * GROUP
     encoded = pl.pallas_call(
         functools.partial(attend_kernel, heads),
         out_shape=jax.ShapeDtypeStruct((slots, width), BF16),
@@ -416,13 +474,20 @@
             pltpu.VMEM((keys, width), BF16),
             pltpu.VMEM((8, n_blk, slots), F32),
             pltpu.VMEM((8, slots, slots), F32),
+            pltpu.VMEM((rows_all, width), BF16),
+            pltpu.VMEM((rows_all, keys), F32),
+            pltpu.VMEM((rows_all, 128), F32),
+            pltpu.VMEM((rows_all, 128), F32),
+            pltpu.VMEM((rows_all, width), F32),
             pltpu.VMEM((slots, width), F32),
-            pltpu.VMEM((rows_u, width), BF16),
-            pltpu.VMEM((rows_u, keys), F32),
-            pltpu.VMEM((rows_u, width), F32),
-            pltpu.VMEM((slots, width), F32),
-            pltpu.VMEM(((hid + heads) * GROUP, (3 * feats + 2) * GROUP), BF16),
+            pltpu.VMEM((hid * GROUP, mixing), BF16),
+            pltpu.VMEM((heads * GROUP, mixing), BF16),
             pltpu.VMEM((heads * GROUP, hid * GROUP), BF16),
+            pltpu.VMEM((groups, mixing, TILE), BF16),
+            pltpu.VMEM((groups, mixing, TILE), BF16),
+            pltpu.VMEM((groups, hid * GROUP, TILE), BF16),
+            pltpu.VMEM((heads * UNIT, TILE), BF16),
+            pltpu.SMEM((2, slots // UNIT), jnp.int32),
         ],
         compiler_params=pltpu.CompilerParams(vmem_limit_bytes=40 * 1024 * 1024),
         name="attend",

time: 113 us -> 94.5 us (0.84)
  the two profiles are of different devices: /device:TPU:32 before, /device:TPU:8 now
where the time goes in v2:
time: 94.5 us; the launch traced here: 94.1 us
  Pallas kernels  91.4 us (97%)
  local copies, waits for them, and re-layouts  2.54 us (3%)
    pallas_call x1, Pallas kernels, shards(): pl.pallas_call(functools.partial(exchange_kernel, n_grp, n_blk), out_shap...  51.1 us
    pallas_call x1, Pallas kernels, shards(): pl.pallas_call(functools.partial(attend_kernel, heads), out_shape=jax.Sha...  40.3 us
    unnamed x17, local copies, waits for them, and re-layouts  2.54 us

profile of v2, /device:TPU:8, one launch (start us, length us, event | category | flops | bytes accessed | tf_op | source)
XLA Modules:
  0.0 94.1 jit_solution(4578956287080021491)
XLA Ops:
  0.0 0.0 copy-start.7
  0.0 0.0 copy-start.5
  0.0 0.0 copy-start.6
  0.0 0.0 copy-start.4
  0.0 0.0 copy-start.3
  0.0 0.0 copy-start.2
  0.0 0.0 copy-start.1
  0.0 0.9 copy.14.w2_ref
  0.9 51.1 %exchange.1.x_ref = bf16[32,144,256]{2,1,0:T(8,128)(2,1)} custom-call(bf16[1,4,128,256]{3,2,1,0:T(8,128)(2,1)} %raw_ref.1, bf16[1,4,4,128]{3,2,1,0:T(4,128)(2,1)} %kin_ref.1, s32[1,128]{1,0:T(1,128)} %reader_ref.1, s32[1,128]{1,0:T(1,128)} %event_ref.1, f32[1,256]{1,0:T(1,128)} %bitcast.6), custom_call_target="tpu_custom_call" | custom-call | tf_op jit(solution)/shard_map/exchange/pallas_call | solution.py:440
  52.0 0.0 copy-done.7
  52.0 0.0 copy-done.5
  52.0 0.0 copy-done.6
  52.0 0.0 copy-done.4
  52.0 0.0 copy-done.3
  52.1 0.0 copy-done.2
  52.1 0.0 copy-done.1
  52.1 0.0 copy-start
  52.1 1.7 %copy-done = bf16[32,144,256]{2,1,0:T(8,128)(2,1)S(1)} copy-done((bf16[32,144,256]{2,1,0:T(8,128)(2,1)S(1)}, bf16[32,144,256]{2,1,0:T(8,128)(2,1)}, u32[]{:S(2)}) %copy-start) | copy-done | bytes 2359320
  53.7 40.3 %attend.1 = bf16[128,256]{1,0:T(8,128)(2,1)} custom-call(bf16[32,144,256]{2,1,0:T(8,128)(2,1)S(1)} %copy-done, bf16[256,256]{1,0:T(8,128)(2,1)S(1)} %copy-done.1, bf16[256,256]{1,0:T(8,128)(2,1)S(1)} %copy-done.2, bf16[256,256]{1,0:T(8,128)(2,1)S(1)} %copy-done.3, bf16[256,256]{1,0:T(8,128)(2,1)S(1)} %copy-done.4, f32[1,256]{1,0:T(1,128)S(1)} %bitcast.4, ...), custom_call_target="tpu_custom_call" | custom-call | tf_op jit(solution)/shard_map/attend/pallas_call | solution.py:467
Async XLA Ops:
  0.0 52.0 %copy-start.7 = (f32[32]{0:T(128)S(1)}, f32[32]{0:T(128)}, u32[]{:S(2)}) copy-start(f32[32]{0:T(128)} %param.24) | copy-start | bytes 388
  0.0 52.0 %copy-start.5 = (f32[4,32]{1,0:T(4,128)S(1)}, f32[4,32]{1,0:T(4,128)}, u32[]{:S(2)}) copy-start(f32[4,32]{1,0:T(4,128)} %w1_ref.1) | copy-start | bytes 1540
  0.0 52.0 %copy-start.6 = (f32[256]{0:T(256)S(1)}, f32[256]{0:T(256)}, u32[]{:S(2)}) copy-start(f32[256]{0:T(256)} %param.22) | copy-start | bytes 3076
  0.0 52.0 %copy-start.4 = (bf16[256,256]{1,0:T(8,128)(2,1)S(1)}, bf16[256,256]{1,0:T(8,128)(2,1)}, u32[]{:S(2)}) copy-start(bf16[256,256]{1,0:T(8,128)(2,1)} %wo_ref.1) | copy-start | bytes 393220
  0.0 52.0 %copy-start.3 = (bf16[256,256]{1,0:T(8,128)(2,1)S(1)}, bf16[256,256]{1,0:T(8,128)(2,1)}, u32[]{:S(2)}) copy-start(bf16[256,256]{1,0:T(8,128)(2,1)} %wv_ref.1) | copy-start | bytes 393220
  0.0 52.0 %copy-start.2 = (bf16[256,256]{1,0:T(8,128)(2,1)S(1)}, bf16[256,256]{1,0:T(8,128)(2,1)}, u32[]{:S(2)}) copy-start(bf16[256,256]{1,0:T(8,128)(2,1)} %wk_ref.1) | copy-start | bytes 393220
  0.0 52.0 %copy-start.1 = (bf16[256,256]{1,0:T(8,128)(2,1)S(1)}, bf16[256,256]{1,0:T(8,128)(2,1)}, u32[]{:S(2)}) copy-start(bf16[256,256]{1,0:T(8,128)(2,1)} %wq_ref.1) | copy-start | bytes 393220
  52.1 1.7 %copy-start = (bf16[32,144,256]{2,1,0:T(8,128)(2,1)S(1)}, bf16[32,144,256]{2,1,0:T(8,128)(2,1)}, u32[]{:S(2)}) copy-start(bf16[32,144,256]{2,1,0:T(8,128)(2,1)} %exchange.1.x_ref) | copy-start | bytes 7077892

commit v3 on v2

v3 whole, which is shorter than its diff:
```python
import functools
import math

import jax
import jax.numpy as jnp
from jax import lax
from jax.experimental import pallas as pl
from jax.experimental.pallas import tpu as pltpu
from jax.sharding import PartitionSpec as P

MESH = pl.DeviceIdType.MESH
F32 = jnp.float32
BF16 = jnp.bfloat16
HIGHEST = lax.Precision.HIGHEST

KIN_ROWS = 16
GROUP = 8
UNIT = 16
TILE = 256
STRIDE = 3

GELU_A = math.sqrt(2.0 / math.pi)
GELU_B = GELU_A * 0.044715
GELU_S = GELU_B ** (-1.0 / 3.0)
ALPHA = GELU_A * GELU_S
LOG2E = 1.0 / math.log(2.0)


def layer_norm(rows, gain):
    center = rows - jnp.mean(rows, axis=-1, keepdims=True)
    spread = jnp.mean(center * center, axis=-1, keepdims=True)
    return center * lax.rsqrt(spread + 1e-05) * gain


def mesh_place(cube):
    _, ny, nx = cube
    b = lax.axis_index("blk")
    return b // (ny * nx), lax.rem(b // nx, ny), lax.rem(b, nx)


def exchange_kernel(
    n_grp,
    cube,
    raw_ref,
    kin_ref,
    reader_ref,
    event_ref,
    gain_ref,
    pair_ref,
    keys_ref,
    inbox,
    kin_send,
    kin_in,
    block,
    other,
    payload,
    send_sem,
    recv_sem,
    kin_send_sem,
    kin_recv_sem,
    link_send,
    link_recv,
    own_sem,
):
    nz, ny, nx = cube
    g = lax.axis_index("grp")
    z, y, x = mesh_place(cube)
    slots = raw_ref.shape[2]
    width = raw_ref.shape[3]
    half = slots // nz

    def blk(z, y, x):
        return {"blk": (z * ny + y) * nx + x}

    partners = [{"grp": lax.rem(g + k, n_grp)} for k in range(1, n_grp)]
    partners.append(blk(1 - z, y, x))
    partners += [blk(z, lax.rem(y + k, ny), x) for k in range(1, ny)]
    partners += [blk(z, y, lax.rem(x + k, nx)) for k in range(1, nx)]
    barrier = pltpu.get_barrier_semaphore()
    for partner in partners:
        pl.semaphore_signal(barrier, inc=1, device_id=partner, device_id_type=MESH)
    kin_send[...] = jnp.zeros_like(kin_send)
    for k in range(n_grp):
        kin_send[k, 0:4, :] = kin_ref[0, k].astype(F32)
    pl.semaphore_wait(barrier, len(partners))

    copies = []
    for k in range(1, n_grp):
        to = lax.rem(g + k, n_grp)
        for src, dst, ssem, rsem in (
            (raw_ref.at[0, to], inbox.at[n_grp - k], send_sem, recv_sem),
            (kin_send.at[to], kin_in.at[n_grp - k], kin_send_sem, kin_recv_sem),
        ):
            copy = pltpu.make_async_remote_copy(
                src_ref=src,
                dst_ref=dst,
                send_sem=ssem.at[k],
                recv_sem=rsem.at[n_grp - k],
                device_id={"grp": to},
                device_id_type=MESH,
            )
            copy.start()
            copies.append(copy)

    wanted = lax.rem(reader_ref[...] - g + n_grp, n_grp)
    column = jnp.broadcast_to(wanted, (slots, slots)).T
    kin = jnp.where(wanted == 0, kin_send[g, 0:4, :], 0.0)
    sides = [
        jnp.where(column == 0, raw_ref[0, g][:, h : h + slots].astype(F32), 0.0)
        for h in range(0, width, slots)
    ]
    for copy in copies:
        copy.wait()
    for k in range(1, n_grp):
        kin = kin + jnp.where(wanted == k, kin_in[k, 0:4, :], 0.0)
        sides = [
            side
            + jnp.where(column == k, inbox[k][:, i * slots : (i + 1) * slots].astype(F32), 0.0)
            for i, side in enumerate(sides)
        ]
    tokens = jnp.concatenate(sides, axis=1)
    block[0:slots, :] = layer_norm(tokens, gain_ref[...]).astype(BF16)
    tail = jnp.concatenate(
        [kin, event_ref[...].astype(F32), jnp.zeros((8 - 5, slots), F32)], axis=0
    )
    tail = jnp.concatenate([tail, tail], axis=0)
    block[slots : slots + KIN_ROWS, :] = jnp.concatenate([tail, tail], axis=1).astype(BF16)

    def push(slot, src, dst, to):
        copy = pltpu.make_async_remote_copy(
            src_ref=src,
            dst_ref=dst,
            send_sem=link_send.at[slot],
            recv_sem=link_recv.at[slot],
            device_id=to,
            device_id_type=MESH,
        )
        copy.start()
        return copy

    mine = pl.ds(pl.multiple_of(z * half, half), half)
    theirs = pl.ds(pl.multiple_of((1 - z) * half, half), half)
    ends = pl.ds(slots, KIN_ROWS)
    near = blk(1 - z, y, x)
    first = [
        push(0, block.at[theirs], other.at[theirs], near),
        push(1, block.at[ends], other.at[ends], near),
    ]
    rest = push(2, block.at[mine], other.at[mine], near)
    for copy in first:
        copy.wait()

    mine_own = block[mine, :]
    mine_other = other[mine, :]
    payload[0:half, :] = jnp.where(z == 0, mine_own, mine_other)
    payload[half : 2 * half, :] = jnp.where(z == 0, mine_other, mine_own)
    ends_own = block[ends, :].astype(F32)
    ends_other = other[ends, :].astype(F32)
    part = lax.broadcasted_iota(jnp.int32, (KIN_ROWS, width), 0) // 8
    lane = lax.broadcasted_iota(jnp.int32, (KIN_ROWS, width), 1) // half
    both = jnp.where(part == z, ends_own, ends_other)
    swapped = jnp.concatenate([both[:, half:], both[:, :half]], axis=1)
    both = jnp.where(lax.rem(lane, 2) == z, both, swapped)
    payload[slots : slots + KIN_ROWS, :] = jnp.where(lane == x, both, 0.0).astype(BF16)

    own = pltpu.make_async_copy(payload, keys_ref.at[y, x], own_sem.at[0])
    own.start()
    rows = (pl.ds(0, half), pl.ds(half, half + KIN_ROWS))
    along = []
    for i, k in enumerate((1, 3, 2)):
        along.append(
            push(
                3 + i,
                payload.at[rows[0]],
                keys_ref.at[y, x, rows[0]],
                blk(z, y, lax.rem(x + k, nx)),
            )
        )
        along.append(
            push(
                6 + i,
                payload.at[rows[1]],
                keys_ref.at[y, x, rows[1]],
                blk(z, lax.rem(y + k, ny), x),
            )
        )
    own.wait()
    for copy in along:
        copy.wait()
    line_x = keys_ref.at[y, :, rows[0]]
    line_y = keys_ref.at[:, x, rows[1]]
    last = []
    for i, k in enumerate((1, 3, 2)):
        last.append(push(9 + i, line_x, line_x, blk(z, lax.rem(y + k, ny), x)))
        last.append(push(12 + i, line_y, line_y, blk(z, y, lax.rem(x + k, nx))))
    rest.wait()
    pair = [
        pltpu.make_async_copy(block, pair_ref.at[z], own_sem.at[1]),
        pltpu.make_async_copy(other, pair_ref.at[1 - z], own_sem.at[2]),
    ]
    for copy in pair:
        copy.start()
    for copy in pair + last:
        copy.wait()


def split_two(value):
    high = value.astype(BF16)
    low = (value - high.astype(F32)).astype(BF16)
    return high, low


def spread_over(weight):
    m, c = weight.shape
    up = (
        lax.broadcasted_iota(jnp.int32, (m * GROUP, m), 0) // GROUP
        == lax.broadcasted_iota(jnp.int32, (m * GROUP, m), 1)
    ).astype(F32)
    across = (
        lax.broadcasted_iota(jnp.int32, (c, c * GROUP), 1) // GROUP
        == lax.broadcasted_iota(jnp.int32, (c, c * GROUP), 0)
    ).astype(F32)
    tall = jnp.dot(up, weight, precision=HIGHEST, preferred_element_type=F32)
    wide = jnp.dot(tall, across, precision=HIGHEST, preferred_element_type=F32)
    same = (
        lax.broadcasted_iota(jnp.int32, (m * GROUP, c * GROUP), 0) % GROUP
        == lax.broadcasted_iota(jnp.int32, (m * GROUP, c * GROUP), 1) % GROUP
    )
    return jnp.where(same, wide, 0.0)


def attend_kernel(
    heads,
    pair_hbm,
    keys_hbm,
    wq_ref,
    wk_ref,
    wv_ref,
    w1_ref,
    b1_ref,
    w2_ref,
    out_ref,
    level_ref,
    pair_ref,
    keys_ref,
    load_sem,
    kt_ref,
    v_ref,
    terms,
    q_terms,
    qm_ref,
    s_ref,
    top_ref,
    total_ref,
    acc_ref,
    wfirst,
    wsecond,
    fresh,
    hidden,
    linear,
    turned,
    weight_ref,
    held_ref,
    limits,
):
    loads = [
        pltpu.make_async_copy(pair_hbm, pair_ref, load_sem.at[0]),
        pltpu.make_async_copy(keys_hbm, keys_ref, load_sem.at[1]),
    ]
    for load in loads:
        load.start()
    nz, slots, width = out_ref.shape
    ny, nx = keys_ref.shape[0:2]
    half = slots // nz
    own_rows = nz * slots
    head_size = width // heads
    feats, hid = w1_ref.shape
    root = math.sqrt(head_size)
    groups = UNIT // GROUP
    rows_g = heads * GROUP
    rows_u = groups * rows_g
    n_units = own_rows // UNIT
    n_tiles = nz * ny

    w1 = w1_ref[...]
    b1 = b1_ref[...]
    w2 = w2_ref[...]
    first = jnp.concatenate([w1, b1, jnp.zeros((8 - feats - 1, hid), F32)], axis=0)
    line = jnp.dot(first, w2, precision=HIGHEST, preferred_element_type=F32) * (0.5 * root)
    part = feats * GROUP

    stacked = jnp.concatenate([first.T * (1.0 / GELU_S), line.T], axis=0)
    high, low = split_two(spread_over(stacked))
    wfirst[:, 0:part] = high[:, 0:part]
    wfirst[:, part : 2 * part] = high[:, 0:part]
    wfirst[:, 2 * part : 3 * part] = low[:, 0:part]
    wfirst[:, 3 * part : 3 * part + GROUP] = high[:, part : part + GROUP]
    wfirst[:, 3 * part + GROUP : 3 * part + 2 * GROUP] = low[:, part : part + GROUP]
    wsecond[...] = spread_over(w2.T * (0.5 * root * GELU_S)).astype(BF16)

    for load in loads:
        load.wait()

    def terms_of(mom, rap, azi, mass, ids):
        trans = jnp.sqrt(mom * mom + mass * mass)
        return (
            mom,
            rap,
            jnp.cos(azi),
            jnp.sin(azi),
            trans * jnp.exp(rap),
            trans * jnp.exp(-rap),
            mass * mass,
            ids,
        )

    ends = []
    for yy in range(ny):
        end = keys_ref[yy, 0, slots : slots + KIN_ROWS, :].astype(F32)
        for xx in range(1, nx):
            end = end + keys_ref[yy, xx, slots : slots + KIN_ROWS, :].astype(F32)
        ends.append(end)
    raw_terms = [
        jnp.concatenate(
            [ends[yy][zz * 8 + i : zz * 8 + i + 1] for zz in range(nz) for yy in range(ny)], axis=0
        )
        for i in range(5)
    ]
    ids = raw_terms[4]
    for i, term in enumerate(terms_of(*raw_terms)):
        for k in range(TILE // 128):
            terms[i, k] = term[:, k * 128 : (k + 1) * 128]
    ends = [pair_ref[zz, slots : slots + KIN_ROWS, 0:slots].astype(F32) for zz in range(nz)]
    raw_terms = [
        jnp.concatenate([ends[zz][i : i + 1] for zz in range(nz)], axis=0) for i in range(5)
    ]
    for i, term in enumerate(terms_of(*raw_terms)):
        for zz in range(nz):
            q_terms[i, zz * slots : (zz + 1) * slots, :] = jnp.broadcast_to(
                term[zz : zz + 1], (slots, slots)
            ).T

    for u in range(n_units):
        begin = q_terms[7, u * UNIT : u * UNIT + 1, 0:1]
        finish = q_terms[7, u * UNIT + UNIT - 1 : u * UNIT + UNIT, 0:1]
        start = jnp.minimum(jnp.sum((ids < begin).astype(jnp.int32)) // TILE, n_tiles - 1)
        limits[0, u] = start
        limits[1, u] = jnp.maximum(
            (jnp.sum((ids <= finish).astype(jnp.int32)) + TILE - 1) // TILE, start + 1
        )

    wkt = wk_ref[...].astype(F32).T.astype(BF16)
    for yy in range(ny):
        for zz in range(nz):
            rows = jnp.concatenate(
                [keys_ref[yy, xx, zz * half : (zz + 1) * half, :] for xx in range(nx)], axis=0
            )
            at = slice((zz * ny + yy) * TILE, (zz * ny + yy + 1) * TILE)
            kt_ref[:, at] = lax.dot_general(
                wkt, rows, (((1,), (1,)), ((), ())), preferred_element_type=F32
            ).astype(BF16)
            v_ref[at, :] = jnp.dot(rows, wv_ref[...], preferred_element_type=F32).astype(BF16)
    for k in range(STRIDE - 1):
        v_ref[(n_tiles + k) * TILE : (n_tiles + k + 1) * TILE, :] = jnp.zeros((TILE, width), BF16)

    lane_head = lax.broadcasted_iota(jnp.int32, (GROUP, width), 1) // head_size
    for zz in range(nz):
        queries = jnp.dot(pair_ref[zz, 0:slots, :], wq_ref[...], preferred_element_type=F32)
        for base in range(0, slots, GROUP):
            rows = queries[base : base + GROUP]
            at = (zz * slots + base) * heads
            qm_ref[at : at + rows_g, :] = jnp.concatenate(
                [jnp.where(lane_head == h, rows, 0.0) for h in range(heads)], axis=0
            ).astype(BF16)

    top_ref[...] = jnp.full_like(top_ref, -1e30)
    total_ref[...] = jnp.zeros_like(total_ref)
    acc_ref[...] = jnp.zeros_like(acc_ref)

    def following(u, t):
        more = t + 1 < limits[1, u]
        then = jnp.where(more, u, jnp.minimum(u + 1, n_units - 1))
        return then, jnp.where(more, t + 1, limits[0, then])

    steps = limits[1, 0] - limits[0, 0]
    for u in range(1, n_units):
        steps = steps + limits[1, u] - limits[0, u]

    def features(p, u, t):
        for g in range(groups):
            base = pl.multiple_of(u * UNIT + g * GROUP, GROUP)
            qt = [q_terms[i, pl.ds(base, GROUP), :] for i in range(7)]
            columns = []
            for i in range(TILE // 128):
                kt = [terms[j, i, pl.ds(t, 1), :] for j in range(7)]
                gap = qt[1] - kt[1]
                cos_gap = qt[2] * kt[2] + qt[3] * kt[3]
                dist = gap * gap + (2.0 - 2.0 * cos_gap)
                small = jnp.minimum(qt[0], kt[0])
                msq = (
                    qt[6]
                    + kt[6]
                    + (qt[4] * kt[5] + qt[5] * kt[4] - 2.0 * (qt[0] * kt[0] * cos_gap))
                )
                f = [
                    jnp.log(1.0 + dist),
                    jnp.log(1.0 + small * small * dist),
                    small / (qt[0] + kt[0]),
                    jnp.log(1.0 + msq),
                ]
                fh, fl = split_two(jnp.concatenate(f, axis=0))
                columns.append(
                    jnp.concatenate([fh, fl, fh, jnp.ones((2 * GROUP, 128), BF16)], axis=0)
                )
            fresh[p, g] = jnp.concatenate(columns, axis=1)

    def hiddens(p):
        for g in range(groups):
            z = jnp.dot(wfirst[...], fresh[p, g], preferred_element_type=F32)
            hidden[p, g] = z[0 : hid * GROUP].astype(BF16)
            linear[p, g] = z[hid * GROUP :]

    def gelus(p):
        for g in range(groups):
            inner = hidden[p, g]
            turned[p, g] = inner * jnp.tanh(inner * (ALPHA + inner * inner))

    def scores(p, u, t, away):
        start = pl.multiple_of(t * TILE, TILE)
        first_row = pl.multiple_of(u * rows_u, rows_u)
        products = jnp.dot(
            qm_ref[pl.ds(first_row, rows_u), :],
            kt_ref[:, pl.ds(start, TILE)],
            preferred_element_type=F32,
        )
        for g in range(groups):
            base = pl.multiple_of(u * UNIT + g * GROUP, GROUP)
            bias = jnp.dot(wsecond[...], turned[p, g], preferred_element_type=F32)
            s = products[g * rows_g : (g + 1) * rows_g] + (bias + linear[p, g])
            own = q_terms[7, pl.ds(base, GROUP), :] + away
            live = jnp.concatenate(
                [own == terms[7, i, pl.ds(t, 1), :] for i in range(TILE // 128)], axis=1
            )
            s = jnp.where(live[None], s.reshape(heads, GROUP, TILE), -1e30).reshape(rows_g, TILE)
            at = pl.ds(pl.multiple_of(first_row + g * rows_g, rows_g), rows_g)
            s_ref[at, pl.ds(start, TILE)] = s
            run_max = top_ref[at, :]
            for i in range(0, TILE, 128):
                run_max = jnp.maximum(run_max, s[:, i : i + 128])
            top_ref[at, :] = run_max

    def score_steps(i, carry):
        for p in range(2):
            u0, t0, u1, t1, u2, t2, u3, t3 = carry
            scores(1 - p, u3, t3, jnp.where(2 * i + p >= 3, 0.0, 100.0))
            hiddens(1 - p)
            gelus(p)
            features(p, u0, t0)
            carry = (*following(u0, t0), u0, t0, u1, t1, u2, t2)
        return carry

    zero = jnp.int32(0)
    t_first = limits[0, 0]
    lax.fori_loop(0, (steps + 4) // 2, score_steps, (zero, t_first) * 4)

    for u in range(n_units):
        at = slice(u * rows_u, (u + 1) * rows_u)
        top_ref[at, :] = jnp.broadcast_to(
            jnp.max(top_ref[at, :], axis=1, keepdims=True), (rows_u, 128)
        )

    for u in range(n_units):
        for k in range(STRIDE - 1):
            start = pl.multiple_of((limits[1, u] + k) * TILE, TILE)
            s_ref[u * rows_u : (u + 1) * rows_u, pl.ds(start, TILE)] = jnp.full(
                (rows_u, TILE), -1e30, F32
            )
    weight_ref[...] = jnp.zeros_like(weight_ref)
    span = STRIDE * TILE

    def stride_on(u, t):
        more = t + STRIDE < limits[1, u]
        then = jnp.where(more, u, jnp.minimum(u + 1, n_units - 1))
        return then, jnp.where(more, t + STRIDE, limits[0, then])

    def apply(u, t):
        at = pl.ds(pl.multiple_of(u * rows_u, rows_u), rows_u)
        acc_ref[at, :] += jnp.dot(
            weight_ref[...],
            v_ref[pl.ds(pl.multiple_of(t * TILE, TILE), span), :],
            preferred_element_type=F32,
        )

    def weigh(u, t):
        at = pl.ds(pl.multiple_of(u * rows_u, rows_u), rows_u)
        top = top_ref[at, :]
        total = total_ref[at, :]
        for i in range(0, span, 128):
            cols = pl.ds(pl.multiple_of(t * TILE + i, 128), 128)
            weight = jnp.exp2((s_ref[at, cols] - top) * (LOG2E / root))
            total = total + weight
            weight_ref[:, i : i + 128] = weight.astype(BF16)
        total_ref[at, :] = total

    def value_step(i, carry):
        u0, t0, u1, t1 = carry
        apply(u1, t1)
        weigh(u0, t0)
        return (*stride_on(u0, t0), u0, t0)

    strides = zero
    for u in range(n_units):
        strides = strides + (limits[1, u] - limits[0, u] + STRIDE - 1) // STRIDE
    _, _, u1, t1 = lax.fori_loop(0, strides, value_step, (zero, t_first, zero, t_first))
    apply(u1, t1)

    lane = lax.broadcasted_iota(jnp.int32, (rows_g, slots), 1)
    row = lax.rem(lax.broadcasted_iota(jnp.int32, (rows_g, slots), 0), GROUP)
    for zz in range(nz):
        level = jnp.zeros((rows_g, slots), F32)
        for base in range(0, slots, GROUP):
            at = (zz * slots + base) * heads
            total = jnp.sum(total_ref[at : at + rows_g, :], axis=1, keepdims=True)
            level = jnp.where(
                lane == base + row,
                top_ref[at : at + rows_g, :] * (LOG2E / root) + jnp.log(total) * LOG2E,
                level,
            )
            total = 1.0 / total
            out = jnp.zeros((GROUP, width), F32)
            for h in range(heads):
                rows = slice(at + h * GROUP, at + (h + 1) * GROUP)
                scaled = acc_ref[rows, :] * total[h * GROUP : (h + 1) * GROUP]
                out = jnp.where(lane_head == h, scaled, out)
            held_ref[base : base + GROUP, :] = out
        out_ref[zz] = held_ref[...].astype(BF16)
        level_ref[zz] = jnp.sum(level.reshape(heads, GROUP, slots), axis=1)


def finish_kernel(
    cube,
    part_ref,
    level_ref,
    wo_ref,
    gain_ref,
    out_ref,
    part_in,
    level_in,
    send_sem,
    recv_sem,
):
    _, ny, nx = cube
    z, y, x = mesh_place(cube)
    near = {"blk": ((1 - z) * ny + y) * nx + x}
    heads = level_ref.shape[1]
    width = part_ref.shape[2]
    barrier = pltpu.get_barrier_semaphore()
    pl.semaphore_signal(barrier, inc=1, device_id=near, device_id_type=MESH)
    pl.semaphore_wait(barrier, 1)
    copies = [
        pltpu.make_async_remote_copy(
            src_ref=src,
            dst_ref=dst,
            send_sem=send_sem.at[i],
            recv_sem=recv_sem.at[i],
            device_id=near,
            device_id_type=MESH,
        )
        for i, (src, dst) in enumerate(
            [(part_ref.at[1 - z], part_in), (level_ref.at[1 - z], level_in)]
        )
    ]
    for copy in copies:
        copy.start()
    spread = (
        lax.broadcasted_iota(jnp.int32, (heads, width), 1) // (width // heads)
        == lax.broadcasted_iota(jnp.int32, (heads, width), 0)
    ).astype(F32)
    for copy in copies:
        copy.wait()
    share = 1.0 / (1.0 + jnp.exp2(level_in[...] - level_ref[z]))
    share = jnp.dot(share.T, spread, precision=HIGHEST, preferred_element_type=F32)
    theirs = part_in[...].astype(F32)
    attended = theirs + share * (part_ref[z].astype(F32) - theirs)
    mixed = jnp.dot(attended.astype(BF16), wo_ref[...], preferred_element_type=F32)
    out_ref[...] = layer_norm(mixed, gain_ref[...]).astype(BF16)


def shards(
    n_grp,
    cube,
    raw,
    raw_kin,
    reader,
    event_id,
    pre_gain,
    w_query,
    w_key,
    w_value,
    w_out,
    post_gain,
    pair_w1,
    pair_b1,
    pair_w2,
):
    slots, width = raw.shape[2], raw.shape[3]
    heads = pair_w2.shape[1]
    nz, ny, nx = cube
    vmem = pl.BlockSpec(memory_space=pltpu.VMEM)
    free = pl.BlockSpec(memory_space=pl.ANY)
    dma = pltpu.SemaphoreType.DMA
    tall = slots + KIN_ROWS
    pair, keys = pl.pallas_call(
        functools.partial(exchange_kernel, n_grp, cube),
        out_shape=(
            jax.ShapeDtypeStruct((nz, tall, width), BF16),
            jax.ShapeDtypeStruct((ny, nx, tall, width), BF16),
        ),
        in_specs=[vmem] * 5,
        out_specs=(free, free),
        scratch_shapes=[
            pltpu.VMEM((n_grp, slots, width), BF16),
            pltpu.VMEM((n_grp, 8, slots), F32),
            pltpu.VMEM((n_grp, 8, slots), F32),
            pltpu.VMEM((tall, width), BF16),
            pltpu.VMEM((tall, width), BF16),
            pltpu.VMEM((tall, width), BF16),
            dma((n_grp,)),
            dma((n_grp,)),
            dma((n_grp,)),
            dma((n_grp,)),
            dma((15,)),
            dma((15,)),
            dma((3,)),
        ],
        compiler_params=pltpu.CompilerParams(collective_id=0, has_side_effects=True),
        name="exchange",
    )(raw, raw_kin, reader, event_id, pre_gain[None])

    own_rows = nz * slots
    n_tiles = nz * ny
    feats, hid = pair_w1.shape
    groups = UNIT // GROUP
    rows_all = heads * own_rows
    mixing = (3 * feats + 2) * GROUP
    part, level = pl.pallas_call(
        functools.partial(attend_kernel, heads),
        out_shape=(
            jax.ShapeDtypeStruct((nz, slots, width), BF16),
            jax.ShapeDtypeStruct((nz, heads, slots), F32),
        ),
        in_specs=[free, free] + [vmem] * 6,
        out_specs=(vmem, vmem),
        scratch_shapes=[
            pltpu.VMEM((nz, tall, width), BF16),
            pltpu.VMEM((ny, nx, tall, width), BF16),
            dma((2,)),
            pltpu.VMEM((width, n_tiles * TILE), BF16),
            pltpu.VMEM(((n_tiles + STRIDE - 1) * TILE, width), BF16),
            pltpu.VMEM((8, TILE // 128, n_tiles, 128), F32),
            pltpu.VMEM((8, own_rows, slots), F32),
            pltpu.VMEM((rows_all, width), BF16),
            pltpu.VMEM((rows_all, (n_tiles + STRIDE - 1) * TILE), F32),
            pltpu.VMEM((rows_all, 128), F32),
            pltpu.VMEM((rows_all, 128), F32),
            pltpu.VMEM((rows_all, width), F32),
            pltpu.VMEM(((hid + heads) * GROUP, mixing), BF16),
            pltpu.VMEM((heads * GROUP, hid * GROUP), BF16),
            pltpu.VMEM((2, groups, mixing, TILE), BF16),
            pltpu.VMEM((2, groups, hid * GROUP, TILE), BF16),
            pltpu.VMEM((2, groups, heads * GROUP, TILE), F32),
            pltpu.VMEM((2, groups, hid * GROUP, TILE), BF16),
            pltpu.VMEM((heads * UNIT, STRIDE * TILE), BF16),
            pltpu.VMEM((slots, width), F32),
            pltpu.SMEM((2, own_rows // UNIT), jnp.int32),
        ],
        compiler_params=pltpu.CompilerParams(vmem_limit_bytes=52 * 1024 * 1024),
        name="attend",
    )(pair, keys, w_query, w_key, w_value, pair_w1, pair_b1[None], pair_w2)

    encoded = pl.pallas_call(
        functools.partial(finish_kernel, cube),
        out_shape=jax.ShapeDtypeStruct((slots, width), BF16),
        in_specs=[vmem] * 4,
        out_specs=vmem,
        scratch_shapes=[
            pltpu.VMEM((slots, width), BF16),
            pltpu.VMEM((heads, slots), F32),
            dma((2,)),
            dma((2,)),
        ],
        compiler_params=pltpu.CompilerParams(collective_id=1, has_side_effects=True),
        name="finish",
    )(part, level, w_out, post_gain[None])
    return encoded[None]


def solution(mesh):
    in_specs = (
        P("grp", None, "blk", None),
        P("grp", None, None, "blk"),
        P("grp", "blk"),
        P("grp", "blk"),
        P(),
        P(),
        P(),
        P(),
        P(),
        P(),
        P(),
        P(),
        P(),
    )
    out_specs = P("grp", "blk", None)
    cube = (2, 4, mesh.shape["blk"] // 8)
    body = functools.partial(shards, mesh.shape["grp"], cube)
    return jax.shard_map(body, mesh=mesh, in_specs=in_specs, out_specs=out_specs, check_vma=False)
```

time: 94.5 us -> 72.9 us (0.77)
  the two profiles are of different devices: /device:TPU:8 before, /device:TPU:16 now
where the time goes in v3:
time: 72.9 us; the launch traced here: 72.5 us
  Pallas kernels  62.8 us (86%)
  local copies, waits for them, and re-layouts  9.69 us (13%)
    pallas_call x1, Pallas kernels, shards(): pl.pallas_call(functools.partial(attend_kernel, heads), out_shape=(jax.Sh...  28.1 us
    pallas_call x1, Pallas kernels, shards(): pl.pallas_call(functools.partial(exchange_kernel, n_grp, cube), out_shape...  28 us
    unnamed x20, local copies, waits for them, and re-layouts  9.69 us
    pallas_call x1, Pallas kernels, shards(): pl.pallas_call(functools.partial(finish_kernel, cube), out_shape=jax.Shap...  6.62 us

profile of v3, /device:TPU:16, one launch (start us, length us, event | category | flops | bytes accessed | tf_op | source)
XLA Modules:
  0.0 72.5 jit_solution(7692473670165990730)
XLA Ops:
  0.0 0.8 %copy.14.w2_ref = f32[32,8]{1,0:T(8,128)S(1)} copy(f32[32,8]{0,1:T(8,128)} %param.25) | data formatting | bytes 2048 | tf_op args[12]
  0.8 28.0 %exchange.1 = (bf16[2,144,256]{2,1,0:T(8,128)(2,1)}, bf16[4,4,144,256]{3,2,1,0:T(8,128)(2,1)}) custom-call(bf16[1,4,128,256]{3,2,1,0:T(8,128)(2,1)} %raw_ref.1, bf16[1,4,4,128]{3,2,1,0:T(4,128)(2,1)} %kin_ref.1, s32[1,128]{1,0:T(1,128)} %reader_ref.1, s32[1,128]{1,0:T(1,128)} %event_ref.1, f32[1,256]{1,0:T(1,128)} %bitcast.6), custom_call_target="tpu_custom_call" | custom-call | tf_op jit(solution)/shard_map/exchange/pallas_call | solution.py:613
  28.8 0.0 copy-start
  28.8 1.3 %copy-done = bf16[4,4,144,256]{3,2,1,0:T(8,128)(2,1)S(1)} copy-done((bf16[4,4,144,256]{3,2,1,0:T(8,128)(2,1)S(1)}, bf16[4,4,144,256]{3,2,1,0:T(8,128)(2,1)}, u32[]{:S(2)}) %copy-start) | copy-done | bytes 1179672
  30.1 0.0 copy-start.1
  30.1 0.9 %copy-done.1 = bf16[2,144,256]{2,1,0:T(8,128)(2,1)S(1)} copy-done((bf16[2,144,256]{2,1,0:T(8,128)(2,1)S(1)}, bf16[2,144,256]{2,1,0:T(8,128)(2,1)}, u32[]{:S(2)}) %copy-start.1) | copy-done | bytes 147480
  31.0 0.0 copy-start.2
  31.0 0.9 %copy-done.2 = bf16[256,256]{1,0:T(8,128)(2,1)S(1)} copy-done((bf16[256,256]{1,0:T(8,128)(2,1)S(1)}, bf16[256,256]{1,0:T(8,128)(2,1)}, u32[]{:S(2)}) %copy-start.2) | copy-done | bytes 131096
  31.9 0.0 copy-start.3
  31.9 0.9 %copy-done.3 = bf16[256,256]{1,0:T(8,128)(2,1)S(1)} copy-done((bf16[256,256]{1,0:T(8,128)(2,1)S(1)}, bf16[256,256]{1,0:T(8,128)(2,1)}, u32[]{:S(2)}) %copy-start.3) | copy-done | bytes 131096
  32.8 0.0 copy-start.4
  32.8 0.9 %copy-done.4 = bf16[256,256]{1,0:T(8,128)(2,1)S(1)} copy-done((bf16[256,256]{1,0:T(8,128)(2,1)S(1)}, bf16[256,256]{1,0:T(8,128)(2,1)}, u32[]{:S(2)}) %copy-start.4) | copy-done | bytes 131096
  33.7 0.0 copy-start.7
  33.7 0.7 copy-done.7
  34.4 0.0 copy-start.8
  34.4 0.7 copy-done.8
  35.0 28.1 %attend.1 = (bf16[2,128,256]{2,1,0:T(8,128)(2,1)S(1)}, f32[2,8,128]{2,1,0:T(8,128)S(1)}) custom-call(bf16[2,144,256]{2,1,0:T(8,128)(2,1)S(1)} %copy-done.1, bf16[4,4,144,256]{3,2,1,0:T(8,128)(2,1)S(1)} %copy-done, bf16[256,256]{1,0:T(8,128)(2,1)S(1)} %copy-done.2, bf16[256,256]{1,0:T(8,128)(2,1)S(1)} %copy-done.3, bf16[256,256]{1,0:T(8,128)(2,1)S(1)} %copy-done.4, ...), custom_call_target="tpu_custom_call" | custom-call | tf_op jit(solution)/shard_map/attend/pallas_call | solution.py:646
  63.2 0.0 copy-start.5
  63.2 0.6 copy-done.5
  63.8 0.0 copy-start.6
  63.8 0.6 copy-done.6
  64.4 6.6 %finish.1 = bf16[128,256]{1,0:T(8,128)(2,1)} custom-call(bf16[2,128,256]{2,1,0:T(8,128)(2,1)} %copy-done.5, f32[2,8,128]{2,1,0:T(8,128)} %copy-done.6, bf16[256,256]{1,0:T(8,128)(2,1)} %wo_ref.1, f32[1,256]{1,0:T(1,128)} %bitcast.7), custom_call_target="tpu_custom_call" | custom-call | tf_op jit(solution)/shard_map/finish/pallas_call | solution.py:681
  71.0 1.5 %copy.16 = bf16[1,128,256]{2,1,0:T(8,128)(2,1)} copy(bf16[1,128,256]{2,1,0:T(8,128)(2,1)} %bitcast.5) | data formatting | bytes 131072
Async XLA Ops:
  28.8 1.3 %copy-start = (bf16[4,4,144,256]{3,2,1,0:T(8,128)(2,1)S(1)}, bf16[4,4,144,256]{3,2,1,0:T(8,128)(2,1)}, u32[]{:S(2)}) copy-start(bf16[4,4,144,256]{3,2,1,0:T(8,128)(2,1)} %get-tuple-element.10.keys_hbm) | copy-start | bytes 3538948
  30.1 0.9 %copy-start.1 = (bf16[2,144,256]{2,1,0:T(8,128)(2,1)S(1)}, bf16[2,144,256]{2,1,0:T(8,128)(2,1)}, u32[]{:S(2)}) copy-start(bf16[2,144,256]{2,1,0:T(8,128)(2,1)} %get-tuple-element.9.pair_hbm) | copy-start | bytes 442372
  31.0 0.9 %copy-start.2 = (bf16[256,256]{1,0:T(8,128)(2,1)S(1)}, bf16[256,256]{1,0:T(8,128)(2,1)}, u32[]{:S(2)}) copy-start(bf16[256,256]{1,0:T(8,128)(2,1)} %wq_ref.1) | copy-start | bytes 393220
  31.9 0.9 %copy-start.3 = (bf16[256,256]{1,0:T(8,128)(2,1)S(1)}, bf16[256,256]{1,0:T(8,128)(2,1)}, u32[]{:S(2)}) copy-start(bf16[256,256]{1,0:T(8,128)(2,1)} %wk_ref.1) | copy-start | bytes 393220
  32.8 0.9 %copy-start.4 = (bf16[256,256]{1,0:T(8,128)(2,1)S(1)}, bf16[256,256]{1,0:T(8,128)(2,1)}, u32[]{:S(2)}) copy-start(bf16[256,256]{1,0:T(8,128)(2,1)} %wv_ref.1) | copy-start | bytes 393220
  33.7 0.7 copy-start.7
  34.4 0.7 copy-start.8
  63.2 0.6 copy-start.5
  63.8 0.6 copy-start.6

commit v4 on v3

--- a/solution.py
+++ b/solution.py
@@ -238,7 +238,7 @@
     wv_ref,
     w1_ref,
     b1_ref,
-    w2_ref,
+    w2t_ref,
     out_ref,
     level_ref,
     pair_ref,
@@ -261,6 +261,7 @@
     turned,
     weight_ref,
     held_ref,
+    ranges,
     limits,
 ):
     loads = [
@@ -284,19 +285,21 @@
 
     w1 = w1_ref[...]
     b1 = b1_ref[...]
-    w2 = w2_ref[...]
+    w2t = w2t_ref[...]
     first = jnp.concatenate([w1, b1, jnp.zeros((8 - feats - 1, hid), F32)], axis=0)
-    line = jnp.dot(first, w2, precision=HIGHEST, preferred_element_type=F32) * (0.5 * root)
+    line = lax.dot_general(
+        w2t, first, (((1,), (1,)), ((), ())), precision=HIGHEST, preferred_element_type=F32
+    ) * (0.5 * root)
     part = feats * GROUP
 
-    stacked = jnp.concatenate([first.T * (1.0 / GELU_S), line.T], axis=0)
+    stacked = jnp.concatenate([first.T * (1.0 / GELU_S), line], axis=0)
     high, low = split_two(spread_over(stacked))
     wfirst[:, 0:part] = high[:, 0:part]
     wfirst[:, part : 2 * part] = high[:, 0:part]
     wfirst[:, 2 * part : 3 * part] = low[:, 0:part]
     wfirst[:, 3 * part : 3 * part + GROUP] = high[:, part : part + GROUP]
     wfirst[:, 3 * part + GROUP : 3 * part + 2 * GROUP] = low[:, part : part + GROUP]
-    wsecond[...] = spread_over(w2.T * (0.5 * root * GELU_S)).astype(BF16)
+    wsecond[...] = spread_over(w2t * (0.5 * root * GELU_S)).astype(BF16)
 
     for load in loads:
         load.wait()
@@ -340,14 +343,21 @@
                 term[zz : zz + 1], (slots, slots)
             ).T
 
-    for u in range(n_units):
-        begin = q_terms[7, u * UNIT : u * UNIT + 1, 0:1]
-        finish = q_terms[7, u * UNIT + UNIT - 1 : u * UNIT + UNIT, 0:1]
-        start = jnp.minimum(jnp.sum((ids < begin).astype(jnp.int32)) // TILE, n_tiles - 1)
-        limits[0, u] = start
-        limits[1, u] = jnp.maximum(
-            (jnp.sum((ids <= finish).astype(jnp.int32)) + TILE - 1) // TILE, start + 1
-        )
+    counts = []
+    for row in (0, UNIT - 1):
+        bound = q_terms[7, pl.ds(row, n_units, stride=UNIT), :]
+        count = jnp.zeros((n_units, 128), F32)
+        for t in range(n_tiles):
+            for k in range(TILE // 128):
+                key = terms[7, k, t : t + 1, :]
+                count = count + jnp.where(key < bound if row == 0 else key <= bound, 1.0, 0.0)
+        counts.append(jnp.sum(count, axis=1, keepdims=True).astype(jnp.int32))
+    start = jnp.minimum(counts[0] // TILE, n_tiles - 1)
+    stop = jnp.maximum((counts[1] + (TILE - 1)) // TILE, start + 1)
+    ranges[0] = jnp.broadcast_to(start, (n_units, 128))
+    ranges[1] = jnp.broadcast_to(stop, (n_units, 128))
+    to_scalars = pltpu.make_async_copy(ranges, limits, load_sem.at[2])
+    to_scalars.start()
 
     wkt = wk_ref[...].astype(F32).T.astype(BF16)
     for yy in range(ny):
@@ -377,14 +387,16 @@
     total_ref[...] = jnp.zeros_like(total_ref)
     acc_ref[...] = jnp.zeros_like(acc_ref)
 
+    to_scalars.wait()
+
     def following(u, t):
-        more = t + 1 < limits[1, u]
+        more = t + 1 < limits[1, u, 0]
         then = jnp.where(more, u, jnp.minimum(u + 1, n_units - 1))
-        return then, jnp.where(more, t + 1, limits[0, then])
-
-    steps = limits[1, 0] - limits[0, 0]
+        return then, jnp.where(more, t + 1, limits[0, then, 0])
+
+    steps = limits[1, 0, 0] - limits[0, 0, 0]
     for u in range(1, n_units):
-        steps = steps + limits[1, u] - limits[0, u]
+        steps = steps + limits[1, u, 0] - limits[0, u, 0]
 
     def features(p, u, t):
         for g in range(groups):
@@ -460,7 +472,7 @@
         return carry
 
     zero = jnp.int32(0)
-    t_first = limits[0, 0]
+    t_first = limits[0, 0, 0]
     lax.fori_loop(0, (steps + 4) // 2, score_steps, (zero, t_first) * 4)
 
     for u in range(n_units):
@@ -471,7 +483,7 @@
 
     for u in range(n_units):
         for k in range(STRIDE - 1):
-            start = pl.multiple_of((limits[1, u] + k) * TILE, TILE)
+            start = pl.multiple_of((limits[1, u, 0] + k) * TILE, TILE)
             s_ref[u * rows_u : (u + 1) * rows_u, pl.ds(start, TILE)] = jnp.full(
                 (rows_u, TILE), -1e30, F32
             )
@@ -479,9 +491,9 @@
     span = STRIDE * TILE
 
     def stride_on(u, t):
-        more = t + STRIDE < limits[1, u]
+        more = t + STRIDE < limits[1, u, 0]
         then = jnp.where(more, u, jnp.minimum(u + 1, n_units - 1))
-        return then, jnp.where(more, t + STRIDE, limits[0, then])
+        return then, jnp.where(more, t + STRIDE, limits[0, then, 0])
 
     def apply(u, t):
         at = pl.ds(pl.multiple_of(u * rows_u, rows_u), rows_u)
@@ -510,7 +522,7 @@
 
     strides = zero
     for u in range(n_units):
-        strides = strides + (limits[1, u] - limits[0, u] + STRIDE - 1) // STRIDE
+        strides = strides + (limits[1, u, 0] - limits[0, u, 0] + STRIDE - 1) // STRIDE
     _, _, u1, t1 = lax.fori_loop(0, strides, value_step, (zero, t_first, zero, t_first))
     apply(u1, t1)
 
@@ -654,7 +666,7 @@
         scratch_shapes=[
             pltpu.VMEM((nz, tall, width), BF16),
             pltpu.VMEM((ny, nx, tall, width), BF16),
-            dma((2,)),
+            dma((3,)),
             pltpu.VMEM((width, n_tiles * TILE), BF16),
             pltpu.VMEM(((n_tiles + STRIDE - 1) * TILE, width), BF16),
             pltpu.VMEM((8, TILE // 128, n_tiles, 128), F32),
@@ -672,11 +684,12 @@
             pltpu.VMEM((2, groups, hid * GROUP, TILE), BF16),
             pltpu.VMEM((heads * UNIT, STRIDE * TILE), BF16),
             pltpu.VMEM((slots, width), F32),
-            pltpu.SMEM((2, own_rows // UNIT), jnp.int32),
+            pltpu.VMEM((2, own_rows // UNIT, 128), jnp.int32),
+            pltpu.SMEM((2, own_rows // UNIT, 128), jnp.int32),
         ],
-        compiler_params=pltpu.CompilerParams(vmem_limit_bytes=52 * 1024 * 1024),
+        compiler_params=pltpu.CompilerParams(vmem_limit_bytes=63 * 1024 * 1024),
         name="attend",
-    )(pair, keys, w_query, w_key, w_value, pair_w1, pair_b1[None], pair_w2)
+    )(pair, keys, w_query, w_key, w_value, pair_w1, pair_b1[None], pair_w2.T)
 
     encoded = pl.pallas_call(
         functools.partial(finish_kernel, cube),

time: 72.9 us -> 62.2 us (0.85)
  the two profiles are of different devices: /device:TPU:16 before, /device:TPU:8 now
where the time goes in v4:
time: 62.2 us; the launch traced here: 61.9 us
  Pallas kernels  60.4 us (97%)
  local copies, waits for them, and re-layouts  1.47 us (2%)
    pallas_call x1, Pallas kernels, shards(): pl.pallas_call(functools.partial(exchange_kernel, n_grp, cube), out_shape...  28.2 us
    pallas_call x1, Pallas kernels, shards(): pl.pallas_call(functools.partial(attend_kernel, heads), out_shape=(jax.Sh...  25.5 us
    pallas_call x1, Pallas kernels, shards(): pl.pallas_call(functools.partial(finish_kernel, cube), out_shape=jax.Shap...  6.66 us
    unnamed x1, local copies, waits for them, and re-layouts  1.47 us

profile of v4, /device:TPU:8, one launch (start us, length us, event | category | flops | bytes accessed | tf_op | source)
XLA Modules:
  0.0 61.9 jit_solution(16512626651166106565)
XLA Ops:
  0.0 28.2 %exchange.1 = (bf16[2,144,256]{2,1,0:T(8,128)(2,1)}, bf16[4,4,144,256]{3,2,1,0:T(8,128)(2,1)}) custom-call(bf16[1,4,128,256]{3,2,1,0:T(8,128)(2,1)} %raw_ref.1, bf16[1,4,4,128]{3,2,1,0:T(4,128)(2,1)} %kin_ref.1, s32[1,128]{1,0:T(1,128)} %reader_ref.1, s32[1,128]{1,0:T(1,128)} %event_ref.1, f32[1,256]{1,0:T(1,128)} %bitcast.7), custom_call_target="tpu_custom_call" | custom-call | tf_op jit(solution)/shard_map/exchange/pallas_call | solution.py:625
  28.2 25.5 %attend.1 = (bf16[2,128,256]{2,1,0:T(8,128)(2,1)}, f32[2,8,128]{2,1,0:T(8,128)}) custom-call(bf16[2,144,256]{2,1,0:T(8,128)(2,1)} %get-tuple-element.9.pair_hbm, bf16[4,4,144,256]{3,2,1,0:T(8,128)(2,1)} %get-tuple-element.10.keys_hbm, bf16[256,256]{1,0:T(8,128)(2,1)} %wq_ref.1, bf16[256,256]{1,0:T(8,128)(2,1)} %wk_ref.1, bf16[256,256]{1,0:T(8,128)(2,1)} %wv_ref.1, ...), custom_call_target="tpu_custom_call" | custom-call | tf_op jit(solution)/shard_map/attend/pallas_call | solution.py:658
  53.8 6.7 %finish.1 = bf16[128,256]{1,0:T(8,128)(2,1)} custom-call(bf16[2,128,256]{2,1,0:T(8,128)(2,1)} %get-tuple-element.11.part_ref, f32[2,8,128]{2,1,0:T(8,128)} %get-tuple-element.12.level_ref, bf16[256,256]{1,0:T(8,128)(2,1)} %wo_ref.1, f32[1,256]{1,0:T(1,128)} %bitcast.8), custom_call_target="tpu_custom_call" | custom-call | tf_op jit(solution)/shard_map/finish/pallas_call | solution.py:694
  60.4 1.5 %copy.15 = bf16[1,128,256]{2,1,0:T(8,128)(2,1)} copy(bf16[1,128,256]{2,1,0:T(8,128)(2,1)} %bitcast.5) | data formatting | bytes 131072

commit v5 on v4

--- a/solution.py
+++ b/solution.py
@@ -17,7 +17,8 @@
 GROUP = 8
 UNIT = 16
 TILE = 256
-STRIDE = 3
+SCORE_STEPS = 6
+VALUE_STEPS = 8
 
 GELU_A = math.sqrt(2.0 / math.pi)
 GELU_B = GELU_A * 0.044715
@@ -46,8 +47,13 @@
     reader_ref,
     event_ref,
     gain_ref,
+    w1_ref,
+    b1_ref,
+    w2t_ref,
     pair_ref,
     keys_ref,
+    wfirst,
+    wsecond,
     inbox,
     kin_send,
     kin_in,
@@ -79,6 +85,8 @@
     barrier = pltpu.get_barrier_semaphore()
     for partner in partners:
         pl.semaphore_signal(barrier, inc=1, device_id=partner, device_id_type=MESH)
+    load = pltpu.make_async_copy(raw_ref.at[0, g], inbox.at[0], own_sem.at[0])
+    load.start()
     kin_send[...] = jnp.zeros_like(kin_send)
     for k in range(n_grp):
         kin_send[k, 0:4, :] = kin_ref[0, k].astype(F32)
@@ -102,11 +110,13 @@
             copy.start()
             copies.append(copy)
 
+    pair_weights(w1_ref[...], b1_ref[...], w2t_ref[...], width // w2t_ref.shape[0], wfirst, wsecond)
     wanted = lax.rem(reader_ref[...] - g + n_grp, n_grp)
+    load.wait()
     column = jnp.broadcast_to(wanted, (slots, slots)).T
     kin = jnp.where(wanted == 0, kin_send[g, 0:4, :], 0.0)
     sides = [
-        jnp.where(column == 0, raw_ref[0, g][:, h : h + slots].astype(F32), 0.0)
+        jnp.where(column == 0, inbox[0][:, h : h + slots].astype(F32), 0.0)
         for h in range(0, width, slots)
     ]
     for copy in copies:
@@ -146,14 +156,19 @@
         push(0, block.at[theirs], other.at[theirs], near),
         push(1, block.at[ends], other.at[ends], near),
     ]
-    rest = push(2, block.at[mine], other.at[mine], near)
+    rows_own = pl.ds(pl.multiple_of(z * (half + KIN_ROWS), 16), half)
+    rows_other = pl.ds(pl.multiple_of((1 - z) * half, 16), half + KIN_ROWS)
+    x_peers = [blk(z, y, lax.rem(x + k, nx)) for k in (1, nx - 1, 2)]
+    y_peers = [blk(z, lax.rem(y + k, ny), x) for k in (1, ny - 1, 2)]
+    own_x = [
+        push(3 + i, block.at[mine], keys_ref.at[y, x, rows_own], peer)
+        for i, peer in enumerate(x_peers)
+    ]
+    own_here = pltpu.make_async_copy(block.at[mine], keys_ref.at[y, x, rows_own], own_sem.at[0])
+    own_here.start()
     for copy in first:
         copy.wait()
 
-    mine_own = block[mine, :]
-    mine_other = other[mine, :]
-    payload[0:half, :] = jnp.where(z == 0, mine_own, mine_other)
-    payload[half : 2 * half, :] = jnp.where(z == 0, mine_other, mine_own)
     ends_own = block[ends, :].astype(F32)
     ends_other = other[ends, :].astype(F32)
     part = lax.broadcasted_iota(jnp.int32, (KIN_ROWS, width), 0) // 8
@@ -161,46 +176,58 @@
     both = jnp.where(part == z, ends_own, ends_other)
     swapped = jnp.concatenate([both[:, half:], both[:, :half]], axis=1)
     both = jnp.where(lax.rem(lane, 2) == z, both, swapped)
-    payload[slots : slots + KIN_ROWS, :] = jnp.where(lane == x, both, 0.0).astype(BF16)
-
-    own = pltpu.make_async_copy(payload, keys_ref.at[y, x], own_sem.at[0])
-    own.start()
-    rows = (pl.ds(0, half), pl.ds(half, half + KIN_ROWS))
-    along = []
-    for i, k in enumerate((1, 3, 2)):
-        along.append(
-            push(
-                3 + i,
-                payload.at[rows[0]],
-                keys_ref.at[y, x, rows[0]],
-                blk(z, y, lax.rem(x + k, nx)),
-            )
-        )
-        along.append(
-            push(
-                6 + i,
-                payload.at[rows[1]],
-                keys_ref.at[y, x, rows[1]],
-                blk(z, lax.rem(y + k, ny), x),
-            )
-        )
-    own.wait()
-    for copy in along:
+    payload[pl.ds(pl.multiple_of(z * half, 16), KIN_ROWS), :] = jnp.where(
+        lane == x, both, 0.0
+    ).astype(BF16)
+    payload[pl.ds(pl.multiple_of((1 - z) * KIN_ROWS, 16), half), :] = other[mine, :]
+    other_y = [
+        push(6 + i, payload, keys_ref.at[y, x, rows_other], peer)
+        for i, peer in enumerate(y_peers)
+    ]
+    other_here = pltpu.make_async_copy(payload, keys_ref.at[y, x, rows_other], own_sem.at[1])
+    other_here.start()
+    rest = push(2, block.at[mine], other.at[mine], near)
+
+    def line(slot, view, peers):
+        lower, upper = view(0), view(1)
+        right, left = peers[0], peers[1]
+        return (
+            [push(slot, lower, lower, right), push(slot + 1, upper, upper, left)],
+            [push(slot + 2, upper, upper, right), push(slot + 3, lower, lower, left)],
+        )
+
+    def view_x(yy):
+        return lambda part: keys_ref.at[yy, pl.ds(part * (nx // 2), nx // 2), rows_own]
+
+    def view_y(xx):
+        return lambda part: keys_ref.at[pl.ds(part * (ny // 2), ny // 2), xx, rows_other]
+
+    own_here.wait()
+    for copy in own_x:
         copy.wait()
-    line_x = keys_ref.at[y, :, rows[0]]
-    line_y = keys_ref.at[:, x, rows[1]]
-    last = []
-    for i, k in enumerate((1, 3, 2)):
-        last.append(push(9 + i, line_x, line_x, blk(z, lax.rem(y + k, ny), x)))
-        last.append(push(12 + i, line_y, line_y, blk(z, y, lax.rem(x + k, nx))))
+    lines_x = line(9, view_x(y), y_peers)
+    other_here.wait()
+    for copy in other_y:
+        copy.wait()
+    lines_y = line(15, view_y(x), x_peers)
+    onward = []
+    for slot, lines, view, place, size, peers in (
+        (13, lines_x, view_x, y, ny, y_peers),
+        (19, lines_y, view_y, x, nx, x_peers),
+    ):
+        for copy in lines[0]:
+            copy.wait()
+        lower = view(lax.rem(place + size - 1, size))(0)
+        upper = view(lax.rem(place + 1, size))(1)
+        onward += [push(slot, lower, lower, peers[0]), push(slot + 1, upper, upper, peers[1])]
     rest.wait()
     pair = [
-        pltpu.make_async_copy(block, pair_ref.at[z], own_sem.at[1]),
-        pltpu.make_async_copy(other, pair_ref.at[1 - z], own_sem.at[2]),
+        pltpu.make_async_copy(block, pair_ref.at[z], own_sem.at[0]),
+        pltpu.make_async_copy(other, pair_ref.at[1 - z], own_sem.at[1]),
     ]
     for copy in pair:
         copy.start()
-    for copy in pair + last:
+    for copy in pair + lines_x[1] + lines_y[1] + onward:
         copy.wait()
 
 
@@ -229,6 +256,25 @@
     return jnp.where(same, wide, 0.0)
 
 
+def pair_weights(w1, b1, w2t, head_size, wfirst, wsecond):
+    feats, hid = w1.shape
+    root = math.sqrt(head_size)
+    first = jnp.concatenate([w1, b1, jnp.zeros((8 - feats - 1, hid), F32)], axis=0)
+    line = lax.dot_general(
+        w2t, first, (((1,), (1,)), ((), ())), precision=HIGHEST, preferred_element_type=F32
+    ) * (0.5 * root)
+    part = feats * GROUP
+
+    stacked = jnp.concatenate([first.T * (1.0 / GELU_S), line], axis=0)
+    high, low = split_two(spread_over(stacked))
+    wfirst[:, 0:part] = high[:, 0:part]
+    wfirst[:, part : 2 * part] = high[:, 0:part]
+    wfirst[:, 2 * part : 3 * part] = low[:, 0:part]
+    wfirst[:, 3 * part : 3 * part + GROUP] = high[:, part : part + GROUP]
+    wfirst[:, 3 * part + GROUP : 3 * part + 2 * GROUP] = low[:, part : part + GROUP]
+    wsecond[...] = spread_over(w2t * (0.5 * root * GELU_S)).astype(BF16)
+
+
 def attend_kernel(
     heads,
     pair_hbm,
@@ -236,9 +282,8 @@
     wq_ref,
     wk_ref,
     wv_ref,
-    w1_ref,
-    b1_ref,
-    w2t_ref,
+    wfirst,
+    wsecond,
     out_ref,
     level_ref,
     pair_ref,
@@ -253,8 +298,6 @@
     top_ref,
     total_ref,
     acc_ref,
-    wfirst,
-    wsecond,
     fresh,
     hidden,
     linear,
@@ -275,31 +318,13 @@
     half = slots // nz
     own_rows = nz * slots
     head_size = width // heads
-    feats, hid = w1_ref.shape
+    hid = wsecond.shape[1] // GROUP
     root = math.sqrt(head_size)
     groups = UNIT // GROUP
     rows_g = heads * GROUP
     rows_u = groups * rows_g
     n_units = own_rows // UNIT
     n_tiles = nz * ny
-
-    w1 = w1_ref[...]
-    b1 = b1_ref[...]
-    w2t = w2t_ref[...]
-    first = jnp.concatenate([w1, b1, jnp.zeros((8 - feats - 1, hid), F32)], axis=0)
-    line = lax.dot_general(
-        w2t, first, (((1,), (1,)), ((), ())), precision=HIGHEST, preferred_element_type=F32
-    ) * (0.5 * root)
-    part = feats * GROUP
-
-    stacked = jnp.concatenate([first.T * (1.0 / GELU_S), line], axis=0)
-    high, low = split_two(spread_over(stacked))
-    wfirst[:, 0:part] = high[:, 0:part]
-    wfirst[:, part : 2 * part] = high[:, 0:part]
-    wfirst[:, 2 * part : 3 * part] = low[:, 0:part]
-    wfirst[:, 3 * part : 3 * part + GROUP] = high[:, part : part + GROUP]
-    wfirst[:, 3 * part + GROUP : 3 * part + 2 * GROUP] = low[:, part : part + GROUP]
-    wsecond[...] = spread_over(w2t * (0.5 * root * GELU_S)).astype(BF16)
 
     for load in loads:
         load.wait()
@@ -319,9 +344,9 @@
 
     ends = []
     for yy in range(ny):
-        end = keys_ref[yy, 0, slots : slots + KIN_ROWS, :].astype(F32)
+        end = keys_ref[yy, 0, half : half + KIN_ROWS, :].astype(F32)
         for xx in range(1, nx):
-            end = end + keys_ref[yy, xx, slots : slots + KIN_ROWS, :].astype(F32)
+            end = end + keys_ref[yy, xx, half : half + KIN_ROWS, :].astype(F32)
         ends.append(end)
     raw_terms = [
         jnp.concatenate(
@@ -363,15 +388,17 @@
     for yy in range(ny):
         for zz in range(nz):
             rows = jnp.concatenate(
-                [keys_ref[yy, xx, zz * half : (zz + 1) * half, :] for xx in range(nx)], axis=0
+                [
+                    keys_ref[yy, xx, zz * (half + KIN_ROWS) : zz * (half + KIN_ROWS) + half, :]
+                    for xx in range(nx)
+                ],
+                axis=0,
             )
             at = slice((zz * ny + yy) * TILE, (zz * ny + yy + 1) * TILE)
             kt_ref[:, at] = lax.dot_general(
                 wkt, rows, (((1,), (1,)), ((), ())), preferred_element_type=F32
             ).astype(BF16)
             v_ref[at, :] = jnp.dot(rows, wv_ref[...], preferred_element_type=F32).astype(BF16)
-    for k in range(STRIDE - 1):
-        v_ref[(n_tiles + k) * TILE : (n_tiles + k + 1) * TILE, :] = jnp.zeros((TILE, width), BF16)
 
     lane_head = lax.broadcasted_iota(jnp.int32, (GROUP, width), 1) // head_size
     for zz in range(nz):
@@ -462,9 +489,10 @@
             top_ref[at, :] = run_max
 
     def score_steps(i, carry):
-        for p in range(2):
+        for k in range(SCORE_STEPS):
+            p = k % 2
             u0, t0, u1, t1, u2, t2, u3, t3 = carry
-            scores(1 - p, u3, t3, jnp.where(2 * i + p >= 3, 0.0, 100.0))
+            scores(1 - p, u3, t3, jnp.where(SCORE_STEPS * i + k >= 3, 0.0, 100.0))
             hiddens(1 - p)
             gelus(p)
             features(p, u0, t0)
@@ -473,7 +501,7 @@
 
     zero = jnp.int32(0)
     t_first = limits[0, 0, 0]
-    lax.fori_loop(0, (steps + 4) // 2, score_steps, (zero, t_first) * 4)
+    lax.fori_loop(0, (steps + SCORE_STEPS + 2) // SCORE_STEPS, score_steps, (zero, t_first) * 4)
 
     for u in range(n_units):
         at = slice(u * rows_u, (u + 1) * rows_u)
@@ -481,50 +509,36 @@
             jnp.max(top_ref[at, :], axis=1, keepdims=True), (rows_u, 128)
         )
 
-    for u in range(n_units):
-        for k in range(STRIDE - 1):
-            start = pl.multiple_of((limits[1, u, 0] + k) * TILE, TILE)
-            s_ref[u * rows_u : (u + 1) * rows_u, pl.ds(start, TILE)] = jnp.full(
-                (rows_u, TILE), -1e30, F32
-            )
     weight_ref[...] = jnp.zeros_like(weight_ref)
-    span = STRIDE * TILE
-
-    def stride_on(u, t):
-        more = t + STRIDE < limits[1, u, 0]
-        then = jnp.where(more, u, jnp.minimum(u + 1, n_units - 1))
-        return then, jnp.where(more, t + STRIDE, limits[0, then, 0])
-
-    def apply(u, t):
+
+    def apply(p, u, t):
         at = pl.ds(pl.multiple_of(u * rows_u, rows_u), rows_u)
         acc_ref[at, :] += jnp.dot(
-            weight_ref[...],
-            v_ref[pl.ds(pl.multiple_of(t * TILE, TILE), span), :],
+            weight_ref[p],
+            v_ref[pl.ds(pl.multiple_of(t * TILE, TILE), TILE), :],
             preferred_element_type=F32,
         )
 
-    def weigh(u, t):
+    def weigh(p, u, t, above):
         at = pl.ds(pl.multiple_of(u * rows_u, rows_u), rows_u)
-        top = top_ref[at, :]
+        top = top_ref[at, :] + above
         total = total_ref[at, :]
-        for i in range(0, span, 128):
+        for i in range(0, TILE, 128):
             cols = pl.ds(pl.multiple_of(t * TILE + i, 128), 128)
             weight = jnp.exp2((s_ref[at, cols] - top) * (LOG2E / root))
             total = total + weight
-            weight_ref[:, i : i + 128] = weight.astype(BF16)
+            weight_ref[p, :, i : i + 128] = weight.astype(BF16)
         total_ref[at, :] = total
 
-    def value_step(i, carry):
-        u0, t0, u1, t1 = carry
-        apply(u1, t1)
-        weigh(u0, t0)
-        return (*stride_on(u0, t0), u0, t0)
-
-    strides = zero
-    for u in range(n_units):
-        strides = strides + (limits[1, u, 0] - limits[0, u, 0] + STRIDE - 1) // STRIDE
-    _, _, u1, t1 = lax.fori_loop(0, strides, value_step, (zero, t_first, zero, t_first))
-    apply(u1, t1)
+    def value_steps(i, carry):
+        for k in range(VALUE_STEPS):
+            u0, t0, u1, t1 = carry
+            apply(1 - k % 2, u1, t1)
+            weigh(k % 2, u0, t0, jnp.where(VALUE_STEPS * i + k < steps, 0.0, 1e32))
+            carry = (*following(u0, t0), u0, t0)
+        return carry
+
+    lax.fori_loop(0, (steps + VALUE_STEPS) // VALUE_STEPS, value_steps, (zero, t_first) * 2)
 
     lane = lax.broadcasted_iota(jnp.int32, (rows_g, slots), 1)
     row = lax.rem(lax.broadcasted_iota(jnp.int32, (rows_g, slots), 0), GROUP)
@@ -558,8 +572,11 @@
     out_ref,
     part_in,
     level_in,
+    part_own,
+    wo_own,
     send_sem,
     recv_sem,
+    load_sem,
 ):
     _, ny, nx = cube
     z, y, x = mesh_place(cube)
@@ -568,6 +585,12 @@
     width = part_ref.shape[2]
     barrier = pltpu.get_barrier_semaphore()
     pl.semaphore_signal(barrier, inc=1, device_id=near, device_id_type=MESH)
+    loads = [
+        pltpu.make_async_copy(part_ref.at[z], part_own, load_sem.at[0]),
+        pltpu.make_async_copy(wo_ref, wo_own, load_sem.at[1]),
+    ]
+    for load in loads:
+        load.start()
     pl.semaphore_wait(barrier, 1)
     copies = [
         pltpu.make_async_remote_copy(
@@ -588,13 +611,13 @@
         lax.broadcasted_iota(jnp.int32, (heads, width), 1) // (width // heads)
         == lax.broadcasted_iota(jnp.int32, (heads, width), 0)
     ).astype(F32)
-    for copy in copies:
+    for copy in loads + copies:
         copy.wait()
     share = 1.0 / (1.0 + jnp.exp2(level_in[...] - level_ref[z]))
     share = jnp.dot(share.T, spread, precision=HIGHEST, preferred_element_type=F32)
     theirs = part_in[...].astype(F32)
-    attended = theirs + share * (part_ref[z].astype(F32) - theirs)
-    mixed = jnp.dot(attended.astype(BF16), wo_ref[...], preferred_element_type=F32)
+    attended = theirs + share * (part_own[...].astype(F32) - theirs)
+    mixed = jnp.dot(attended.astype(BF16), wo_own[...], preferred_element_type=F32)
     out_ref[...] = layer_norm(mixed, gain_ref[...]).astype(BF16)
 
 
@@ -622,83 +645,95 @@
     free = pl.BlockSpec(memory_space=pl.ANY)
     dma = pltpu.SemaphoreType.DMA
     tall = slots + KIN_ROWS
-    pair, keys = pl.pallas_call(
+    feats, hid = pair_w1.shape
+    mixing = (3 * feats + 2) * GROUP
+    pair, keys, first, second = pl.pallas_call(
         functools.partial(exchange_kernel, n_grp, cube),
         out_shape=(
             jax.ShapeDtypeStruct((nz, tall, width), BF16),
             jax.ShapeDtypeStruct((ny, nx, tall, width), BF16),
+            jax.ShapeDtypeStruct(((hid + heads) * GROUP, mixing), BF16),
+            jax.ShapeDtypeStruct((heads * GROUP, hid * GROUP), BF16),
         ),
-        in_specs=[vmem] * 5,
-        out_specs=(free, free),
+        in_specs=[free] + [vmem] * 7,
+        out_specs=(free, free, vmem, vmem),
         scratch_shapes=[
             pltpu.VMEM((n_grp, slots, width), BF16),
             pltpu.VMEM((n_grp, 8, slots), F32),
             pltpu.VMEM((n_grp, 8, slots), F32),
             pltpu.VMEM((tall, width), BF16),
             pltpu.VMEM((tall, width), BF16),
-            pltpu.VMEM((tall, width), BF16),
+            pltpu.VMEM((slots // nz + KIN_ROWS, width), BF16),
             dma((n_grp,)),
             dma((n_grp,)),
             dma((n_grp,)),
             dma((n_grp,)),
-            dma((15,)),
-            dma((15,)),
-            dma((3,)),
+            dma((21,)),
+            dma((21,)),
+            dma((2,)),
         ],
         compiler_params=pltpu.CompilerParams(collective_id=0, has_side_effects=True),
         name="exchange",
-    )(raw, raw_kin, reader, event_id, pre_gain[None])
+    )(
+        raw,
+        raw_kin,
+        reader,
+        event_id,
+        pre_gain[None],
+        pair_w1,
+        pair_b1[None],
+        pair_w2.T,
+    )
 
     own_rows = nz * slots
     n_tiles = nz * ny
-    feats, hid = pair_w1.shape
     groups = UNIT // GROUP
     rows_all = heads * own_rows
-    mixing = (3 * feats + 2) * GROUP
     part, level = pl.pallas_call(
         functools.partial(attend_kernel, heads),
         out_shape=(
             jax.ShapeDtypeStruct((nz, slots, width), BF16),
             jax.ShapeDtypeStruct((nz, heads, slots), F32),
         ),
-        in_specs=[free, free] + [vmem] * 6,
+        in_specs=[free, free] + [vmem] * 5,
         out_specs=(vmem, vmem),
         scratch_shapes=[
             pltpu.VMEM((nz, tall, width), BF16),
             pltpu.VMEM((ny, nx, tall, width), BF16),
             dma((3,)),
             pltpu.VMEM((width, n_tiles * TILE), BF16),
-            pltpu.VMEM(((n_tiles + STRIDE - 1) * TILE, width), BF16),
+            pltpu.VMEM((n_tiles * TILE, width), BF16),
             pltpu.VMEM((8, TILE // 128, n_tiles, 128), F32),
             pltpu.VMEM((8, own_rows, slots), F32),
             pltpu.VMEM((rows_all, width), BF16),
-            pltpu.VMEM((rows_all, (n_tiles + STRIDE - 1) * TILE), F32),
+            pltpu.VMEM((rows_all, n_tiles * TILE), F32),
             pltpu.VMEM((rows_all, 128), F32),
             pltpu.VMEM((rows_all, 128), F32),
             pltpu.VMEM((rows_all, width), F32),
-            pltpu.VMEM(((hid + heads) * GROUP, mixing), BF16),
-            pltpu.VMEM((heads * GROUP, hid * GROUP), BF16),
             pltpu.VMEM((2, groups, mixing, TILE), BF16),
             pltpu.VMEM((2, groups, hid * GROUP, TILE), BF16),
             pltpu.VMEM((2, groups, heads * GROUP, TILE), F32),
             pltpu.VMEM((2, groups, hid * GROUP, TILE), BF16),
-            pltpu.VMEM((heads * UNIT, STRIDE * TILE), BF16),
+            pltpu.VMEM((2, heads * UNIT, TILE), BF16),
             pltpu.VMEM((slots, width), F32),
             pltpu.VMEM((2, own_rows // UNIT, 128), jnp.int32),
             pltpu.SMEM((2, own_rows // UNIT, 128), jnp.int32),
         ],
         compiler_params=pltpu.CompilerParams(vmem_limit_bytes=63 * 1024 * 1024),
         name="attend",
-    )(pair, keys, w_query, w_key, w_value, pair_w1, pair_b1[None], pair_w2.T)
+    )(pair, keys, w_query, w_key, w_value, first, second)
 
     encoded = pl.pallas_call(
         functools.partial(finish_kernel, cube),
         out_shape=jax.ShapeDtypeStruct((slots, width), BF16),
-        in_specs=[vmem] * 4,
+        in_specs=[free, vmem, free, vmem],
         out_specs=vmem,
         scratch_shapes=[
             pltpu.VMEM((slots, width), BF16),
             pltpu.VMEM((heads, slots), F32),
+            pltpu.VMEM((slots, width), BF16),
+            pltpu.VMEM((width, width), BF16),
+            dma((2,)),
             dma((2,)),
             dma((2,)),
         ],

time: 62.2 us -> 59.2 us (0.952)
  the two profiles are of different devices: /device:TPU:8 before, /device:TPU:78 now
where the time goes in v5:
time: 59.2 us; the launch traced here: 59 us
  Pallas kernels  57.5 us (97%)
  local copies, waits for them, and re-layouts  1.47 us (2%)
    pallas_call x1, Pallas kernels, shards(): pl.pallas_call(functools.partial(exchange_kernel, n_grp, cube), out_shape...  28.2 us
    pallas_call x1, Pallas kernels, shards(): pl.pallas_call(functools.partial(attend_kernel, heads), out_shape=(jax.Sh...  22.7 us
    pallas_call x1, Pallas kernels, shards(): pl.pallas_call(functools.partial(finish_kernel, cube), out_shape=jax.Shap...  6.61 us
    unnamed x1, local copies, waits for them, and re-layouts  1.47 us

profile of v5, /device:TPU:78, one launch (start us, length us, event | category | flops | bytes accessed | tf_op | source)
XLA Modules:
  0.0 59.0 jit_solution(10175441320633790335)
XLA Ops:
  0.0 28.2 %exchange.1 = (bf16[2,144,256]{2,1,0:T(8,128)(2,1)}, bf16[4,4,144,256]{3,2,1,0:T(8,128)(2,1)}, bf16[320,112]{1,0:T(8,128)(2,1)}, bf16[64,256]{1,0:T(8,128)(2,1)}) custom-call(bf16[1,4,128,256]{3,2,1,0:T(8,128)(2,1)} %raw_ref.1, bf16[1,4,4,128]{3,2,1,0:T(4,128)(2,1)} %kin_ref.1, s32[1,128]{1,0:T(1,128)} %reader_ref.1, s32[1,128]{1,0:T(1,128)} %event_ref.1, ...), custom_call_target="tpu_custom_call" | custom-call | tf_op jit(solution)/shard_map/exchange/pallas_call | solution.py:650
  28.2 22.7 %attend.1 = (bf16[2,128,256]{2,1,0:T(8,128)(2,1)}, f32[2,8,128]{2,1,0:T(8,128)}) custom-call(bf16[2,144,256]{2,1,0:T(8,128)(2,1)} %get-tuple-element.11.pair_hbm, bf16[4,4,144,256]{3,2,1,0:T(8,128)(2,1)} %get-tuple-element.12.keys_hbm, bf16[256,256]{1,0:T(8,128)(2,1)} %wq_ref.1, bf16[256,256]{1,0:T(8,128)(2,1)} %wk_ref.1, bf16[256,256]{1,0:T(8,128)(2,1)} %wv_ref.1, ...), custom_call_target="tpu_custom_call" | custom-call | tf_op jit(solution)/shard_map/attend/pallas_call | solution.py:692
  50.9 6.6 %finish.1 = bf16[128,256]{1,0:T(8,128)(2,1)} custom-call(bf16[2,128,256]{2,1,0:T(8,128)(2,1)} %get-tuple-element.15.part_ref, f32[2,8,128]{2,1,0:T(8,128)} %get-tuple-element.16.level_ref, bf16[256,256]{1,0:T(8,128)(2,1)} %wo_ref.1, f32[1,256]{1,0:T(1,128)} %bitcast.8), custom_call_target="tpu_custom_call" | custom-call | tf_op jit(solution)/shard_map/finish/pallas_call | solution.py:726
  57.5 1.5 %copy.15 = bf16[1,128,256]{2,1,0:T(8,128)(2,1)} copy(bf16[1,128,256]{2,1,0:T(8,128)(2,1)} %bitcast.5) | data formatting | bytes 131072

commit v6 on v5

--- a/solution.py
+++ b/solution.py
@@ -43,6 +43,17 @@
     n_grp,
     cube,
     raw_ref,
+    kin_hbm,
+    reader_hbm,
+    event_hbm,
+    gain_hbm,
+    w1_hbm,
+    b1_hbm,
+    w2t_hbm,
+    pair_ref,
+    keys_ref,
+    first_hbm,
+    second_hbm,
     kin_ref,
     reader_ref,
     event_ref,
@@ -50,16 +61,15 @@
     w1_ref,
     b1_ref,
     w2t_ref,
-    pair_ref,
-    keys_ref,
     wfirst,
     wsecond,
+    load_sem,
     inbox,
     kin_send,
     kin_in,
     block,
-    other,
-    payload,
+    mine,
+    theirs,
     send_sem,
     recv_sem,
     kin_send_sem,
@@ -79,14 +89,31 @@
         return {"blk": (z * ny + y) * nx + x}
 
     partners = [{"grp": lax.rem(g + k, n_grp)} for k in range(1, n_grp)]
-    partners.append(blk(1 - z, y, x))
-    partners += [blk(z, lax.rem(y + k, ny), x) for k in range(1, ny)]
-    partners += [blk(z, y, lax.rem(x + k, nx)) for k in range(1, nx)]
+    x_peers = [blk(z, y, lax.rem(x + k, nx)) for k in range(1, nx)]
+    y_peers = [blk(z, lax.rem(y + k, ny), x) for k in range(1, ny)]
+    across = [blk(1 - z, lax.rem(y + k, ny), x) for k in range(ny)]
+    partners += x_peers + y_peers + across
     barrier = pltpu.get_barrier_semaphore()
     for partner in partners:
         pl.semaphore_signal(barrier, inc=1, device_id=partner, device_id_type=MESH)
-    load = pltpu.make_async_copy(raw_ref.at[0, g], inbox.at[0], own_sem.at[0])
-    load.start()
+    loads = [
+        pltpu.make_async_copy(src, dst, load_sem.at[i])
+        for i, (src, dst) in enumerate(
+            [
+                (kin_hbm, kin_ref),
+                (reader_hbm, reader_ref),
+                (event_hbm, event_ref),
+                (gain_hbm, gain_ref),
+                (w1_hbm, w1_ref),
+                (b1_hbm, b1_ref),
+                (w2t_hbm, w2t_ref),
+                (raw_ref.at[0, g], inbox.at[0]),
+            ]
+        )
+    ]
+    for load in loads:
+        load.start()
+    loads[0].wait()
     kin_send[...] = jnp.zeros_like(kin_send)
     for k in range(n_grp):
         kin_send[k, 0:4, :] = kin_ref[0, k].astype(F32)
@@ -110,9 +137,16 @@
             copy.start()
             copies.append(copy)
 
+    for load in loads[1:]:
+        load.wait()
     pair_weights(w1_ref[...], b1_ref[...], w2t_ref[...], width // w2t_ref.shape[0], wfirst, wsecond)
     wanted = lax.rem(reader_ref[...] - g + n_grp, n_grp)
-    load.wait()
+    stores = [
+        pltpu.make_async_copy(wfirst, first_hbm, load_sem.at[0]),
+        pltpu.make_async_copy(wsecond, second_hbm, load_sem.at[1]),
+    ]
+    for store in stores:
+        store.start()
     column = jnp.broadcast_to(wanted, (slots, slots)).T
     kin = jnp.where(wanted == 0, kin_send[g, 0:4, :], 0.0)
     sides = [
@@ -129,12 +163,22 @@
             for i, side in enumerate(sides)
         ]
     tokens = jnp.concatenate(sides, axis=1)
-    block[0:slots, :] = layer_norm(tokens, gain_ref[...]).astype(BF16)
+    normed = layer_norm(tokens, gain_ref[...]).astype(BF16)
+    block[0:slots, :] = normed
     tail = jnp.concatenate(
-        [kin, event_ref[...].astype(F32), jnp.zeros((8 - 5, slots), F32)], axis=0
+        [kin, event_ref[...].astype(F32), jnp.zeros((KIN_ROWS - 5, slots), F32)], axis=0
     )
-    tail = jnp.concatenate([tail, tail], axis=0)
-    block[slots : slots + KIN_ROWS, :] = jnp.concatenate([tail, tail], axis=1).astype(BF16)
+    double = jnp.concatenate([tail, tail], axis=1)
+    swapped = jnp.concatenate([double[:, half:], double[:, :half]], axis=1)
+    block[slots : slots + KIN_ROWS, :] = double.astype(BF16)
+    lane = lax.broadcasted_iota(jnp.int32, (KIN_ROWS, width), 1) // half
+    even = lax.rem(lane, 2)
+    rows_z = jnp.where(z == 0, normed[0:half], normed[half : 2 * half])
+    rows_not = jnp.where(z == 0, normed[half : 2 * half], normed[0:half])
+    for ref, rows, side in ((mine, rows_z, z), (theirs, rows_not, 1 - z)):
+        ref[0:half, :] = rows
+        placed = jnp.where(even == side, double, swapped)
+        ref[half : half + KIN_ROWS, :] = jnp.where(lane == x, placed, 0.0).astype(BF16)
 
     def push(slot, src, dst, to):
         copy = pltpu.make_async_remote_copy(
@@ -148,86 +192,29 @@
         copy.start()
         return copy
 
-    mine = pl.ds(pl.multiple_of(z * half, half), half)
-    theirs = pl.ds(pl.multiple_of((1 - z) * half, half), half)
-    ends = pl.ds(slots, KIN_ROWS)
-    near = blk(1 - z, y, x)
-    first = [
-        push(0, block.at[theirs], other.at[theirs], near),
-        push(1, block.at[ends], other.at[ends], near),
+    other_y = [push(k, theirs, keys_ref.at[y, x, z], peer) for k, peer in enumerate(across)]
+    own_x = [push(4 + k, mine, keys_ref.at[y, x, z], peer) for k, peer in enumerate(x_peers)]
+    moves = [push(7 + k, mine, keys_ref.at[y, x, z], peer) for k, peer in enumerate(y_peers)]
+    moves.append(push(10, block, pair_ref.at[z], across[0]))
+    own_here = pltpu.make_async_copy(mine, keys_ref.at[y, x, z], own_sem.at[0])
+    own_here.start()
+    pair_here = pltpu.make_async_copy(block, pair_ref.at[z], own_sem.at[1])
+    pair_here.start()
+    slot = 11
+    near_x = [(own_x[k - 1], keys_ref.at[y, lax.rem(x - k + nx, nx), z], y_peers) for k in (1, 3, 2)]
+    near_y = [
+        (other_y[k], keys_ref.at[lax.rem(y - k + ny, ny), x, 1 - z], x_peers) for k in (0, 1, 3, 2)
     ]
-    rows_own = pl.ds(pl.multiple_of(z * (half + KIN_ROWS), 16), half)
-    rows_other = pl.ds(pl.multiple_of((1 - z) * half, 16), half + KIN_ROWS)
-    x_peers = [blk(z, y, lax.rem(x + k, nx)) for k in (1, nx - 1, 2)]
-    y_peers = [blk(z, lax.rem(y + k, ny), x) for k in (1, ny - 1, 2)]
-    own_x = [
-        push(3 + i, block.at[mine], keys_ref.at[y, x, rows_own], peer)
-        for i, peer in enumerate(x_peers)
-    ]
-    own_here = pltpu.make_async_copy(block.at[mine], keys_ref.at[y, x, rows_own], own_sem.at[0])
-    own_here.start()
-    for copy in first:
+    for copy, piece, peers in near_x[0:2] + near_y[0:3] + near_x[2:] + near_y[3:]:
+        copy.wait_recv()
+        for peer in peers:
+            moves.append(push(slot, piece, piece, peer))
+            slot += 1
+    for copy in [own_here, pair_here] + stores:
         copy.wait()
-
-    ends_own = block[ends, :].astype(F32)
-    ends_other = other[ends, :].astype(F32)
-    part = lax.broadcasted_iota(jnp.int32, (KIN_ROWS, width), 0) // 8
-    lane = lax.broadcasted_iota(jnp.int32, (KIN_ROWS, width), 1) // half
-    both = jnp.where(part == z, ends_own, ends_other)
-    swapped = jnp.concatenate([both[:, half:], both[:, :half]], axis=1)
-    both = jnp.where(lax.rem(lane, 2) == z, both, swapped)
-    payload[pl.ds(pl.multiple_of(z * half, 16), KIN_ROWS), :] = jnp.where(
-        lane == x, both, 0.0
-    ).astype(BF16)
-    payload[pl.ds(pl.multiple_of((1 - z) * KIN_ROWS, 16), half), :] = other[mine, :]
-    other_y = [
-        push(6 + i, payload, keys_ref.at[y, x, rows_other], peer)
-        for i, peer in enumerate(y_peers)
-    ]
-    other_here = pltpu.make_async_copy(payload, keys_ref.at[y, x, rows_other], own_sem.at[1])
-    other_here.start()
-    rest = push(2, block.at[mine], other.at[mine], near)
-
-    def line(slot, view, peers):
-        lower, upper = view(0), view(1)
-        right, left = peers[0], peers[1]
-        return (
-            [push(slot, lower, lower, right), push(slot + 1, upper, upper, left)],
-            [push(slot + 2, upper, upper, right), push(slot + 3, lower, lower, left)],
-        )
-
-    def view_x(yy):
-        return lambda part: keys_ref.at[yy, pl.ds(part * (nx // 2), nx // 2), rows_own]
-
-    def view_y(xx):
-        return lambda part: keys_ref.at[pl.ds(part * (ny // 2), ny // 2), xx, rows_other]
-
-    own_here.wait()
-    for copy in own_x:
-        copy.wait()
-    lines_x = line(9, view_x(y), y_peers)
-    other_here.wait()
-    for copy in other_y:
-        copy.wait()
-    lines_y = line(15, view_y(x), x_peers)
-    onward = []
-    for slot, lines, view, place, size, peers in (
-        (13, lines_x, view_x, y, ny, y_peers),
-        (19, lines_y, view_y, x, nx, x_peers),
-    ):
-        for copy in lines[0]:
-            copy.wait()
-        lower = view(lax.rem(place + size - 1, size))(0)
-        upper = view(lax.rem(place + 1, size))(1)
-        onward += [push(slot, lower, lower, peers[0]), push(slot + 1, upper, upper, peers[1])]
-    rest.wait()
-    pair = [
-        pltpu.make_async_copy(block, pair_ref.at[z], own_sem.at[0]),
-        pltpu.make_async_copy(other, pair_ref.at[1 - z], own_sem.at[1]),
-    ]
-    for copy in pair:
-        copy.start()
-    for copy in pair + lines_x[1] + lines_y[1] + onward:
+    for copy in other_y + own_x:
+        copy.wait_send()
+    for copy in moves:
         copy.wait()
 
 
@@ -279,15 +266,20 @@
     heads,
     pair_hbm,
     keys_hbm,
+    wq_hbm,
+    wk_hbm,
+    wv_hbm,
+    first_hbm,
+    second_hbm,
+    out_ref,
+    level_ref,
+    pair_ref,
+    keys_ref,
     wq_ref,
     wk_ref,
     wv_ref,
     wfirst,
     wsecond,
-    out_ref,
-    level_ref,
-    pair_ref,
-    keys_ref,
     load_sem,
     kt_ref,
     v_ref,
@@ -308,8 +300,18 @@
     limits,
 ):
     loads = [
-        pltpu.make_async_copy(pair_hbm, pair_ref, load_sem.at[0]),
-        pltpu.make_async_copy(keys_hbm, keys_ref, load_sem.at[1]),
+        pltpu.make_async_copy(src, dst, load_sem.at[i])
+        for i, (src, dst) in enumerate(
+            [
+                (keys_hbm, keys_ref),
+                (pair_hbm, pair_ref),
+                (wk_hbm, wk_ref),
+                (wv_hbm, wv_ref),
+                (wq_hbm, wq_ref),
+                (first_hbm, wfirst),
+                (second_hbm, wsecond),
+            ]
+        )
     ]
     for load in loads:
         load.start()
@@ -343,17 +345,13 @@
         )
 
     ends = []
-    for yy in range(ny):
-        end = keys_ref[yy, 0, half : half + KIN_ROWS, :].astype(F32)
-        for xx in range(1, nx):
-            end = end + keys_ref[yy, xx, half : half + KIN_ROWS, :].astype(F32)
-        ends.append(end)
-    raw_terms = [
-        jnp.concatenate(
-            [ends[yy][zz * 8 + i : zz * 8 + i + 1] for zz in range(nz) for yy in range(ny)], axis=0
-        )
-        for i in range(5)
-    ]
+    for zz in range(nz):
+        for yy in range(ny):
+            end = keys_ref[yy, 0, zz, half : half + KIN_ROWS, :].astype(F32)
+            for xx in range(1, nx):
+                end = end + keys_ref[yy, xx, zz, half : half + KIN_ROWS, :].astype(F32)
+            ends.append(end)
+    raw_terms = [jnp.concatenate([end[i : i + 1] for end in ends], axis=0) for i in range(5)]
     ids = raw_terms[4]
     for i, term in enumerate(terms_of(*raw_terms)):
         for k in range(TILE // 128):
@@ -381,18 +379,14 @@
     stop = jnp.maximum((counts[1] + (TILE - 1)) // TILE, start + 1)
     ranges[0] = jnp.broadcast_to(start, (n_units, 128))
     ranges[1] = jnp.broadcast_to(stop, (n_units, 128))
-    to_scalars = pltpu.make_async_copy(ranges, limits, load_sem.at[2])
+    to_scalars = pltpu.make_async_copy(ranges, limits, load_sem.at[7])
     to_scalars.start()
 
     wkt = wk_ref[...].astype(F32).T.astype(BF16)
     for yy in range(ny):
         for zz in range(nz):
             rows = jnp.concatenate(
-                [
-                    keys_ref[yy, xx, zz * (half + KIN_ROWS) : zz * (half + KIN_ROWS) + half, :]
-                    for xx in range(nx)
-                ],
-                axis=0,
+                [keys_ref[yy, xx, zz, 0:half, :] for xx in range(nx)], axis=0
             )
             at = slice((zz * ny + yy) * TILE, (zz * ny + yy + 1) * TILE)
             kt_ref[:, at] = lax.dot_general(
@@ -573,7 +567,9 @@
     part_in,
     level_in,
     part_own,
+    level_own,
     wo_own,
+    gain_own,
     send_sem,
     recv_sem,
     load_sem,
@@ -587,7 +583,9 @@
     pl.semaphore_signal(barrier, inc=1, device_id=near, device_id_type=MESH)
     loads = [
         pltpu.make_async_copy(part_ref.at[z], part_own, load_sem.at[0]),
-        pltpu.make_async_copy(wo_ref, wo_own, load_sem.at[1]),
+        pltpu.make_async_copy(level_ref.at[z], level_own, load_sem.at[1]),
+        pltpu.make_async_copy(wo_ref, wo_own, load_sem.at[2]),
+        pltpu.make_async_copy(gain_ref, gain_own, load_sem.at[3]),
     ]
     for load in loads:
         load.start()
@@ -613,12 +611,12 @@
     ).astype(F32)
     for copy in loads + copies:
         copy.wait()
-    share = 1.0 / (1.0 + jnp.exp2(level_in[...] - level_ref[z]))
+    share = 1.0 / (1.0 + jnp.exp2(level_in[...] - level_own[...]))
     share = jnp.dot(share.T, spread, precision=HIGHEST, preferred_element_type=F32)
     theirs = part_in[...].astype(F32)
     attended = theirs + share * (part_own[...].astype(F32) - theirs)
     mixed = jnp.dot(attended.astype(BF16), wo_own[...], preferred_element_type=F32)
-    out_ref[...] = layer_norm(mixed, gain_ref[...]).astype(BF16)
+    out_ref[...] = layer_norm(mixed, gain_own[...]).astype(BF16)
 
 
 def shards(
@@ -645,31 +643,42 @@
     free = pl.BlockSpec(memory_space=pl.ANY)
     dma = pltpu.SemaphoreType.DMA
     tall = slots + KIN_ROWS
+    part_rows = slots // nz + KIN_ROWS
     feats, hid = pair_w1.shape
     mixing = (3 * feats + 2) * GROUP
     pair, keys, first, second = pl.pallas_call(
         functools.partial(exchange_kernel, n_grp, cube),
         out_shape=(
             jax.ShapeDtypeStruct((nz, tall, width), BF16),
-            jax.ShapeDtypeStruct((ny, nx, tall, width), BF16),
+            jax.ShapeDtypeStruct((ny, nx, nz, part_rows, width), BF16),
             jax.ShapeDtypeStruct(((hid + heads) * GROUP, mixing), BF16),
             jax.ShapeDtypeStruct((heads * GROUP, hid * GROUP), BF16),
         ),
-        in_specs=[free] + [vmem] * 7,
-        out_specs=(free, free, vmem, vmem),
+        in_specs=[free] * 8,
+        out_specs=(free,) * 4,
         scratch_shapes=[
+            pltpu.VMEM(raw_kin.shape, BF16),
+            pltpu.VMEM(reader.shape, jnp.int32),
+            pltpu.VMEM(event_id.shape, jnp.int32),
+            pltpu.VMEM((1, width), F32),
+            pltpu.VMEM((feats, hid), F32),
+            pltpu.VMEM((1, hid), F32),
+            pltpu.VMEM((heads, hid), F32),
+            pltpu.VMEM(((hid + heads) * GROUP, mixing), BF16),
+            pltpu.VMEM((heads * GROUP, hid * GROUP), BF16),
+            dma((8,)),
             pltpu.VMEM((n_grp, slots, width), BF16),
             pltpu.VMEM((n_grp, 8, slots), F32),
             pltpu.VMEM((n_grp, 8, slots), F32),
             pltpu.VMEM((tall, width), BF16),
-            pltpu.VMEM((tall, width), BF16),
-            pltpu.VMEM((slots // nz + KIN_ROWS, width), BF16),
+            pltpu.VMEM((part_rows, width), BF16),
+            pltpu.VMEM((part_rows, width), BF16),
             dma((n_grp,)),
             dma((n_grp,)),
             dma((n_grp,)),
             dma((n_grp,)),
-            dma((21,)),
-            dma((21,)),
+            dma((32,)),
+            dma((32,)),
             dma((2,)),
         ],
         compiler_params=pltpu.CompilerParams(collective_id=0, has_side_effects=True),
@@ -695,12 +704,17 @@
             jax.ShapeDtypeStruct((nz, slots, width), BF16),
             jax.ShapeDtypeStruct((nz, heads, slots), F32),
         ),
-        in_specs=[free, free] + [vmem] * 5,
+        in_specs=[free] * 7,
         out_specs=(vmem, vmem),
         scratch_shapes=[
             pltpu.VMEM((nz, tall, width), BF16),
-            pltpu.VMEM((ny, nx, tall, width), BF16),
-            dma((3,)),
+            pltpu.VMEM((ny, nx, nz, part_rows, width), BF16),
+            pltpu.VMEM((width, width), BF16),
+            pltpu.VMEM((width, width), BF16),
+            pltpu.VMEM((width, width), BF16),
+            pltpu.VMEM(((hid + heads) * GROUP, mixing), BF16),
+            pltpu.VMEM((heads * GROUP, hid * GROUP), BF16),
+            dma((8,)),
             pltpu.VMEM((width, n_tiles * TILE), BF16),
             pltpu.VMEM((n_tiles * TILE, width), BF16),
             pltpu.VMEM((8, TILE // 128, n_tiles, 128), F32),
@@ -726,16 +740,18 @@
     encoded = pl.pallas_call(
         functools.partial(finish_kernel, cube),
         out_shape=jax.ShapeDtypeStruct((slots, width), BF16),
-        in_specs=[free, vmem, free, vmem],
+        in_specs=[free] * 4,
         out_specs=vmem,
         scratch_shapes=[
             pltpu.VMEM((slots, width), BF16),
             pltpu.VMEM((heads, slots), F32),
             pltpu.VMEM((slots, width), BF16),
+            pltpu.VMEM((heads, slots), F32),
             pltpu.VMEM((width, width), BF16),
+            pltpu.VMEM((1, width), F32),
             dma((2,)),
             dma((2,)),
-            dma((2,)),
+            dma((4,)),
         ],
         compiler_params=pltpu.CompilerParams(collective_id=1, has_side_effects=True),
         name="finish",

time: 59.2 us -> 56.7 us (0.958)
  the two profiles are of different devices: /device:TPU:78 before, /device:TPU:8 now
where the time goes in v6:
time: 56.7 us; the launch traced here: 56.3 us
  Pallas kernels  54.8 us (97%)
  local copies, waits for them, and re-layouts  1.47 us (3%)
    pallas_call x1, Pallas kernels, shards(): pl.pallas_call(functools.partial(exchange_kernel, n_grp, cube), out_shape...  27.3 us
    pallas_call x1, Pallas kernels, shards(): pl.pallas_call(functools.partial(attend_kernel, heads), out_shape=(jax.Sh...  19 us
    pallas_call x1, Pallas kernels, shards(): pl.pallas_call(functools.partial(finish_kernel, cube), out_shape=jax.Shap...  8.5 us
    unnamed x1, local copies, waits for them, and re-layouts  1.47 us

profile of v6, /device:TPU:8, one launch (start us, length us, event | category | flops | bytes accessed | tf_op | source)
XLA Modules:
  0.0 56.3 jit_solution(18064763000134834897)
XLA Ops:
  0.0 27.3 %exchange.1 = (bf16[2,144,256]{2,1,0:T(8,128)(2,1)}, bf16[4,4,2,80,256]{4,3,2,1,0:T(8,128)(2,1)}, bf16[320,112]{1,0:T(8,128)(2,1)}, bf16[64,256]{1,0:T(8,128)(2,1)}) custom-call(bf16[1,4,128,256]{3,2,1,0:T(8,128)(2,1)} %raw_ref.1, bf16[1,4,4,128]{3,2,1,0:T(4,128)(2,1)} %kin_hbm.1, s32[1,128]{1,0:T(1,128)} %reader_hbm.1, s32[1,128]{1,0:T(1,128)} %event_hbm.1, ...), custom_call_target="tpu_custom_call" | custom-call | tf_op jit(solution)/shard_map/exchange/pallas_call | solution.py:649
  27.3 19.0 %attend.1 = (bf16[2,128,256]{2,1,0:T(8,128)(2,1)}, f32[2,8,128]{2,1,0:T(8,128)}) custom-call(bf16[2,144,256]{2,1,0:T(8,128)(2,1)} %get-tuple-element.11.pair_hbm, bf16[4,4,2,80,256]{4,3,2,1,0:T(8,128)(2,1)} %get-tuple-element.12.keys_hbm, bf16[256,256]{1,0:T(8,128)(2,1)} %wq_hbm.1, bf16[256,256]{1,0:T(8,128)(2,1)} %wk_hbm.1, bf16[256,256]{1,0:T(8,128)(2,1)} %wv_hbm.1, ...), custom_call_target="tpu_custom_call" | custom-call | tf_op jit(solution)/shard_map/attend/pallas_call | solution.py:701
  46.4 8.5 %finish.1 = bf16[128,256]{1,0:T(8,128)(2,1)} custom-call(bf16[2,128,256]{2,1,0:T(8,128)(2,1)} %get-tuple-element.15.part_ref, f32[2,8,128]{2,1,0:T(8,128)} %get-tuple-element.16.level_ref, bf16[256,256]{1,0:T(8,128)(2,1)} %wo_ref.1, f32[1,256]{1,0:T(1,128)} %bitcast.8), custom_call_target="tpu_custom_call" | custom-call | tf_op jit(solution)/shard_map/finish/pallas_call | solution.py:740
  54.9 1.5 %copy.15 = bf16[1,128,256]{2,1,0:T(8,128)(2,1)} copy(bf16[1,128,256]{2,1,0:T(8,128)(2,1)} %bitcast.5) | data formatting | bytes 131072

commit v7 on v6

--- a/solution.py
+++ b/solution.py
@@ -70,6 +70,7 @@
     block,
     mine,
     theirs,
+    got,
     send_sem,
     recv_sem,
     kin_send_sem,
@@ -84,15 +85,17 @@
     slots = raw_ref.shape[2]
     width = raw_ref.shape[3]
     half = slots // nz
+    body = half * (width // 128)
 
     def blk(z, y, x):
         return {"blk": (z * ny + y) * nx + x}
 
     partners = [{"grp": lax.rem(g + k, n_grp)} for k in range(1, n_grp)]
-    x_peers = [blk(z, y, lax.rem(x + k, nx)) for k in range(1, nx)]
-    y_peers = [blk(z, lax.rem(y + k, ny), x) for k in range(1, ny)]
-    across = [blk(1 - z, lax.rem(y + k, ny), x) for k in range(ny)]
-    partners += x_peers + y_peers + across
+    turns = (1, nx - 1, 2)
+    x_peers = [blk(z, y, lax.rem(x + k, nx)) for k in turns]
+    y_peers = [blk(z, lax.rem(y + k, ny), x) for k in turns]
+    near = blk(1 - z, y, x)
+    partners += [near] + x_peers + y_peers
     barrier = pltpu.get_barrier_semaphore()
     for partner in partners:
         pl.semaphore_signal(barrier, inc=1, device_id=partner, device_id_type=MESH)
@@ -168,17 +171,14 @@
     tail = jnp.concatenate(
         [kin, event_ref[...].astype(F32), jnp.zeros((KIN_ROWS - 5, slots), F32)], axis=0
     )
-    double = jnp.concatenate([tail, tail], axis=1)
-    swapped = jnp.concatenate([double[:, half:], double[:, :half]], axis=1)
-    block[slots : slots + KIN_ROWS, :] = double.astype(BF16)
-    lane = lax.broadcasted_iota(jnp.int32, (KIN_ROWS, width), 1) // half
-    even = lax.rem(lane, 2)
-    rows_z = jnp.where(z == 0, normed[0:half], normed[half : 2 * half])
-    rows_not = jnp.where(z == 0, normed[half : 2 * half], normed[0:half])
-    for ref, rows, side in ((mine, rows_z, z), (theirs, rows_not, 1 - z)):
-        ref[0:half, :] = rows
-        placed = jnp.where(even == side, double, swapped)
-        ref[half : half + KIN_ROWS, :] = jnp.where(lane == x, placed, 0.0).astype(BF16)
+    block[slots : slots + KIN_ROWS, :] = jnp.concatenate([tail, tail], axis=1).astype(BF16)
+    for ref, low in ((mine, z == 0), (theirs, z == 1)):
+        for i in range(width // 128):
+            cols = slice(i * 128, (i + 1) * 128)
+            ref[i * half : (i + 1) * half, :] = jnp.where(
+                low, normed[0:half, cols], normed[half : 2 * half, cols]
+            )
+    theirs[body : body + KIN_ROWS, :] = tail.astype(BF16)
 
     def push(slot, src, dst, to):
         copy = pltpu.make_async_remote_copy(
@@ -192,27 +192,42 @@
         copy.start()
         return copy
 
-    other_y = [push(k, theirs, keys_ref.at[y, x, z], peer) for k, peer in enumerate(across)]
-    own_x = [push(4 + k, mine, keys_ref.at[y, x, z], peer) for k, peer in enumerate(x_peers)]
-    moves = [push(7 + k, mine, keys_ref.at[y, x, z], peer) for k, peer in enumerate(y_peers)]
-    moves.append(push(10, block, pair_ref.at[z], across[0]))
-    own_here = pltpu.make_async_copy(mine, keys_ref.at[y, x, z], own_sem.at[0])
-    own_here.start()
-    pair_here = pltpu.make_async_copy(block, pair_ref.at[z], own_sem.at[1])
-    pair_here.start()
-    slot = 11
-    near_x = [(own_x[k - 1], keys_ref.at[y, lax.rem(x - k + nx, nx), z], y_peers) for k in (1, 3, 2)]
-    near_y = [
-        (other_y[k], keys_ref.at[lax.rem(y - k + ny, ny), x, 1 - z], x_peers) for k in (0, 1, 3, 2)
+    rows = pl.ds(0, body)
+    swap = push(0, theirs, got, near)
+    own_x = [push(1 + i, mine, keys_ref.at[y, x, z, rows], to) for i, to in enumerate(x_peers)]
+    moves = [push(4 + i, mine, keys_ref.at[y, x, z, rows], to) for i, to in enumerate(y_peers)]
+    here = [
+        pltpu.make_async_copy(mine, keys_ref.at[y, x, z, rows], own_sem.at[0]),
+        pltpu.make_async_copy(block, pair_ref.at[z], own_sem.at[1]),
     ]
-    for copy, piece, peers in near_x[0:2] + near_y[0:3] + near_x[2:] + near_y[3:]:
-        copy.wait_recv()
-        for peer in peers:
-            moves.append(push(slot, piece, piece, peer))
+    for copy in here:
+        copy.start()
+    swap.wait_recv()
+    ends = got[body : body + KIN_ROWS, :].astype(F32)
+    ends = jnp.concatenate([ends[:, half:], ends[:, :half]], axis=1)
+    side = lax.broadcasted_iota(jnp.int32, (KIN_ROWS, slots), 1) // half
+    got[body : body + KIN_ROWS, :] = jnp.where(side == z, tail, ends).astype(BF16)
+    other_y = [push(7 + i, got, keys_ref.at[y, x, 1 - z], to) for i, to in enumerate(y_peers)]
+    moves += [push(10 + i, got, keys_ref.at[y, x, 1 - z], to) for i, to in enumerate(x_peers)]
+    here.append(pltpu.make_async_copy(got, keys_ref.at[y, x, 1 - z], own_sem.at[2]))
+    here[-1].start()
+    moves.append(push(13, block, pair_ref.at[z], near))
+    slot = 14
+    for i, k in enumerate(turns):
+        own_x[i].wait_recv()
+        piece = keys_ref.at[y, lax.rem(x - k + nx, nx), z, rows]
+        for to in y_peers:
+            moves.append(push(slot, piece, piece, to))
             slot += 1
-    for copy in [own_here, pair_here] + stores:
+    for i, k in enumerate(turns):
+        other_y[i].wait_recv()
+        piece = keys_ref.at[lax.rem(y - k + ny, ny), x, 1 - z]
+        for to in x_peers:
+            moves.append(push(slot, piece, piece, to))
+            slot += 1
+    for copy in here + stores:
         copy.wait()
-    for copy in other_y + own_x:
+    for copy in [swap] + own_x + other_y:
         copy.wait_send()
     for copy in moves:
         copy.wait()
@@ -327,6 +342,7 @@
     rows_u = groups * rows_g
     n_units = own_rows // UNIT
     n_tiles = nz * ny
+    z = lax.axis_index("blk") // (ny * nx)
 
     for load in loads:
         load.wait()
@@ -344,13 +360,21 @@
             ids,
         )
 
-    ends = []
-    for zz in range(nz):
-        for yy in range(ny):
-            end = keys_ref[yy, 0, zz, half : half + KIN_ROWS, :].astype(F32)
-            for xx in range(1, nx):
-                end = end + keys_ref[yy, xx, zz, half : half + KIN_ROWS, :].astype(F32)
-            ends.append(end)
+    body = half * (width // 128)
+    lower = lax.broadcasted_iota(jnp.int32, (KIN_ROWS, 128), 1) < half
+    ends = [[] for _ in range(nz)]
+    for yy in range(ny):
+        tails = [
+            keys_ref[yy, xx, 1 - z, body : body + KIN_ROWS, :].astype(F32) for xx in range(nx)
+        ]
+        turned_tails = [jnp.concatenate([e[:, half:], e[:, :half]], axis=1) for e in tails]
+        ends[0].append(
+            [jnp.where(lower, tails[k], turned_tails[k + 1]) for k in range(0, nx, 2)]
+        )
+        ends[1].append(
+            [jnp.where(lower, turned_tails[k], tails[k + 1]) for k in range(0, nx, 2)]
+        )
+    ends = [jnp.concatenate(end, axis=1) for zz in range(nz) for end in ends[zz]]
     raw_terms = [jnp.concatenate([end[i : i + 1] for end in ends], axis=0) for i in range(5)]
     ids = raw_terms[4]
     for i, term in enumerate(terms_of(*raw_terms)):
@@ -386,7 +410,14 @@
     for yy in range(ny):
         for zz in range(nz):
             rows = jnp.concatenate(
-                [keys_ref[yy, xx, zz, 0:half, :] for xx in range(nx)], axis=0
+                [
+                    jnp.concatenate(
+                        [keys_ref[yy, xx, zz, i : i + half, :] for i in range(0, body, half)],
+                        axis=1,
+                    )
+                    for xx in range(nx)
+                ],
+                axis=0,
             )
             at = slice((zz * ny + yy) * TILE, (zz * ny + yy + 1) * TILE)
             kt_ref[:, at] = lax.dot_general(
@@ -643,14 +674,14 @@
     free = pl.BlockSpec(memory_space=pl.ANY)
     dma = pltpu.SemaphoreType.DMA
     tall = slots + KIN_ROWS
-    part_rows = slots // nz + KIN_ROWS
+    part_rows = slots // nz * (width // 128) + KIN_ROWS
     feats, hid = pair_w1.shape
     mixing = (3 * feats + 2) * GROUP
     pair, keys, first, second = pl.pallas_call(
         functools.partial(exchange_kernel, n_grp, cube),
         out_shape=(
             jax.ShapeDtypeStruct((nz, tall, width), BF16),
-            jax.ShapeDtypeStruct((ny, nx, nz, part_rows, width), BF16),
+            jax.ShapeDtypeStruct((ny, nx, nz, part_rows, 128), BF16),
             jax.ShapeDtypeStruct(((hid + heads) * GROUP, mixing), BF16),
             jax.ShapeDtypeStruct((heads * GROUP, hid * GROUP), BF16),
         ),
@@ -671,15 +702,16 @@
             pltpu.VMEM((n_grp, 8, slots), F32),
             pltpu.VMEM((n_grp, 8, slots), F32),
             pltpu.VMEM((tall, width), BF16),
-            pltpu.VMEM((part_rows, width), BF16),
-            pltpu.VMEM((part_rows, width), BF16),
+            pltpu.VMEM((part_rows - KIN_ROWS, 128), BF16),
+            pltpu.VMEM((part_rows, 128), BF16),
+            pltpu.VMEM((part_rows, 128), BF16),
             dma((n_grp,)),
             dma((n_grp,)),
             dma((n_grp,)),
             dma((n_grp,)),
             dma((32,)),
             dma((32,)),
-            dma((2,)),
+            dma((3,)),
         ],
         compiler_params=pltpu.CompilerParams(collective_id=0, has_side_effects=True),
         name="exchange",
@@ -708,7 +740,7 @@
         out_specs=(vmem, vmem),
         scratch_shapes=[
             pltpu.VMEM((nz, tall, width), BF16),
-            pltpu.VMEM((ny, nx, nz, part_rows, width), BF16),
+            pltpu.VMEM((ny, nx, nz, part_rows, 128), BF16),
             pltpu.VMEM((width, width), BF16),
             pltpu.VMEM((width, width), BF16),
             pltpu.VMEM((width, width), BF16),

time: 56.7 us -> 50.7 us (0.89)
  the two profiles are of different devices: /device:TPU:8 before, /device:TPU:64 now
where the time goes in v7:
time: 50.7 us; the launch traced here: 50.5 us
  Pallas kernels  49 us (97%)
  local copies, waits for them, and re-layouts  1.47 us (3%)
    pallas_call x1, Pallas kernels, shards(): pl.pallas_call(functools.partial(exchange_kernel, n_grp, cube), out_shape...  25.7 us
    pallas_call x1, Pallas kernels, shards(): pl.pallas_call(functools.partial(attend_kernel, heads), out_shape=(jax.Sh...  17.3 us
    pallas_call x1, Pallas kernels, shards(): pl.pallas_call(functools.partial(finish_kernel, cube), out_shape=jax.Shap...  5.95 us
    unnamed x1, local copies, waits for them, and re-layouts  1.47 us

profile of v7, /device:TPU:64, one launch (start us, length us, event | category | flops | bytes accessed | tf_op | source)
XLA Modules:
  0.0 50.5 jit_solution(13840506929373953193)
XLA Ops:
  0.0 25.7 %exchange.1 = (bf16[2,144,256]{2,1,0:T(8,128)(2,1)}, bf16[4,4,2,144,128]{4,3,2,1,0:T(8,128)(2,1)}, bf16[320,112]{1,0:T(8,128)(2,1)}, bf16[64,256]{1,0:T(8,128)(2,1)}) custom-call(bf16[1,4,128,256]{3,2,1,0:T(8,128)(2,1)} %raw_ref.1, bf16[1,4,4,128]{3,2,1,0:T(4,128)(2,1)} %kin_hbm.1, s32[1,128]{1,0:T(1,128)} %reader_hbm.1, s32[1,128]{1,0:T(1,128)} %event_hbm.1, ...), custom_call_target="tpu_custom_call" | custom-call | tf_op jit(solution)/shard_map/exchange/pallas_call | solution.py:680
  25.7 17.3 %attend.1 = (bf16[2,128,256]{2,1,0:T(8,128)(2,1)}, f32[2,8,128]{2,1,0:T(8,128)}) custom-call(bf16[2,144,256]{2,1,0:T(8,128)(2,1)} %get-tuple-element.11.pair_hbm, bf16[4,4,2,144,128]{4,3,2,1,0:T(8,128)(2,1)} %get-tuple-element.12.keys_hbm, bf16[256,256]{1,0:T(8,128)(2,1)} %wq_hbm.1, bf16[256,256]{1,0:T(8,128)(2,1)} %wk_hbm.1, bf16[256,256]{1,0:T(8,128)(2,1)} %wv_hbm.1, ...), custom_call_target="tpu_custom_call" | custom-call | tf_op jit(solution)/shard_map/attend/pallas_call | solution.py:733
  43.1 6.0 %finish.1 = bf16[128,256]{1,0:T(8,128)(2,1)} custom-call(bf16[2,128,256]{2,1,0:T(8,128)(2,1)} %get-tuple-element.15.part_ref, f32[2,8,128]{2,1,0:T(8,128)} %get-tuple-element.16.level_ref, bf16[256,256]{1,0:T(8,128)(2,1)} %wo_ref.1, f32[1,256]{1,0:T(1,128)} %bitcast.8), custom_call_target="tpu_custom_call" | custom-call | tf_op jit(solution)/shard_map/finish/pallas_call | solution.py:772
  49.0 1.5 %copy.15 = bf16[1,128,256]{2,1,0:T(8,128)(2,1)} copy(bf16[1,128,256]{2,1,0:T(8,128)(2,1)} %bitcast.5) | data formatting | bytes 131072

commit v8 on v7

--- a/solution.py
+++ b/solution.py
@@ -17,6 +17,7 @@
 GROUP = 8
 UNIT = 16
 TILE = 256
+LANES = 128
 SCORE_STEPS = 6
 VALUE_STEPS = 8
 
@@ -342,6 +343,7 @@
     rows_u = groups * rows_g
     n_units = own_rows // UNIT
     n_tiles = nz * ny
+    per_step = TILE // LANES
     z = lax.axis_index("blk") // (ny * nx)
 
     for load in loads:
@@ -376,10 +378,21 @@
         )
     ends = [jnp.concatenate(end, axis=1) for zz in range(nz) for end in ends[zz]]
     raw_terms = [jnp.concatenate([end[i : i + 1] for end in ends], axis=0) for i in range(5)]
-    ids = raw_terms[4]
+    n_rows = n_tiles * TILE // LANES
+    raw_terms = [
+        jnp.concatenate(
+            [
+                term[t : t + 1, k : k + LANES]
+                for t in range(n_tiles)
+                for k in range(0, TILE, LANES)
+            ],
+            axis=0,
+        )
+        for term in raw_terms
+    ]
     for i, term in enumerate(terms_of(*raw_terms)):
-        for k in range(TILE // 128):
-            terms[i, k] = term[:, k * 128 : (k + 1) * 128]
+        terms[i, 0:n_rows, :] = term
+        terms[i, n_rows : n_rows + 8, :] = jnp.full((8, LANES), -1.0 if i == 7 else 1.0, F32)
     ends = [pair_ref[zz, slots : slots + KIN_ROWS, 0:slots].astype(F32) for zz in range(nz)]
     raw_terms = [
         jnp.concatenate([ends[zz][i : i + 1] for zz in range(nz)], axis=0) for i in range(5)
@@ -394,15 +407,14 @@
     for row in (0, UNIT - 1):
         bound = q_terms[7, pl.ds(row, n_units, stride=UNIT), :]
         count = jnp.zeros((n_units, 128), F32)
-        for t in range(n_tiles):
-            for k in range(TILE // 128):
-                key = terms[7, k, t : t + 1, :]
-                count = count + jnp.where(key < bound if row == 0 else key <= bound, 1.0, 0.0)
+        for t in range(n_rows):
+            key = terms[7, t : t + 1, :]
+            count = count + jnp.where(key < bound if row == 0 else key <= bound, 1.0, 0.0)
         counts.append(jnp.sum(count, axis=1, keepdims=True).astype(jnp.int32))
-    start = jnp.minimum(counts[0] // TILE, n_tiles - 1)
-    stop = jnp.maximum((counts[1] + (TILE - 1)) // TILE, start + 1)
-    ranges[0] = jnp.broadcast_to(start, (n_units, 128))
-    ranges[1] = jnp.broadcast_to(stop, (n_units, 128))
+    start = jnp.minimum(counts[0] // LANES, n_rows - 1)
+    stop = jnp.maximum((counts[1] + (LANES - 1)) // LANES, start + 1)
+    ranges[0] = start + jnp.zeros((n_units, 128), jnp.int32)
+    ranges[1] = (stop - start + (per_step - 1)) // per_step + jnp.zeros((n_units, 128), jnp.int32)
     to_scalars = pltpu.make_async_copy(ranges, limits, load_sem.at[7])
     to_scalars.start()
 
@@ -425,6 +437,9 @@
             ).astype(BF16)
             v_ref[at, :] = jnp.dot(rows, wv_ref[...], preferred_element_type=F32).astype(BF16)
 
+    kt_ref[:, n_tiles * TILE :] = jnp.zeros((width, LANES), BF16)
+    v_ref[n_tiles * TILE :, :] = jnp.zeros((LANES, width), BF16)
+
     lane_head = lax.broadcasted_iota(jnp.int32, (GROUP, width), 1) // head_size
     for zz in range(nz):
         queries = jnp.dot(pair_ref[zz, 0:slots, :], wq_ref[...], preferred_element_type=F32)
@@ -441,22 +456,25 @@
 
     to_scalars.wait()
 
-    def following(u, t):
-        more = t + 1 < limits[1, u, 0]
-        then = jnp.where(more, u, jnp.minimum(u + 1, n_units - 1))
-        return then, jnp.where(more, t + 1, limits[0, then, 0])
-
-    steps = limits[1, 0, 0] - limits[0, 0, 0]
+    def following(u, k):
+        more = k + 1 < limits[1, u, 0]
+        return jnp.where(more, u, jnp.minimum(u + 1, n_units - 1)), jnp.where(more, k + 1, 0)
+
+    steps = limits[1, 0, 0]
     for u in range(1, n_units):
-        steps = steps + limits[1, u, 0] - limits[0, u, 0]
-
-    def features(p, u, t):
+        steps = steps + limits[1, u, 0]
+
+    def place(u, k):
+        return limits[0, u, 0] + k * per_step
+
+    def features(p, u, k):
+        t = place(u, k)
         for g in range(groups):
             base = pl.multiple_of(u * UNIT + g * GROUP, GROUP)
             qt = [q_terms[i, pl.ds(base, GROUP), :] for i in range(7)]
             columns = []
-            for i in range(TILE // 128):
-                kt = [terms[j, i, pl.ds(t, 1), :] for j in range(7)]
+            for i in range(per_step):
+                kt = [terms[j, pl.ds(t + i, 1), :] for j in range(7)]
                 gap = qt[1] - kt[1]
                 cos_gap = qt[2] * kt[2] + qt[3] * kt[3]
                 dist = gap * gap + (2.0 - 2.0 * cos_gap)
@@ -489,8 +507,9 @@
             inner = hidden[p, g]
             turned[p, g] = inner * jnp.tanh(inner * (ALPHA + inner * inner))
 
-    def scores(p, u, t, away):
-        start = pl.multiple_of(t * TILE, TILE)
+    def scores(p, u, k, away):
+        t = place(u, k)
+        start = pl.multiple_of(t * LANES, LANES)
         first_row = pl.multiple_of(u * rows_u, rows_u)
         products = jnp.dot(
             qm_ref[pl.ds(first_row, rows_u), :],
@@ -503,7 +522,7 @@
             s = products[g * rows_g : (g + 1) * rows_g] + (bias + linear[p, g])
             own = q_terms[7, pl.ds(base, GROUP), :] + away
             live = jnp.concatenate(
-                [own == terms[7, i, pl.ds(t, 1), :] for i in range(TILE // 128)], axis=1
+                [own == terms[7, pl.ds(t + i, 1), :] for i in range(per_step)], axis=1
             )
             s = jnp.where(live[None], s.reshape(heads, GROUP, TILE), -1e30).reshape(rows_g, TILE)
             at = pl.ds(pl.multiple_of(first_row + g * rows_g, rows_g), rows_g)
@@ -525,8 +544,7 @@
         return carry
 
     zero = jnp.int32(0)
-    t_first = limits[0, 0, 0]
-    lax.fori_loop(0, (steps + SCORE_STEPS + 2) // SCORE_STEPS, score_steps, (zero, t_first) * 4)
+    lax.fori_loop(0, (steps + SCORE_STEPS + 2) // SCORE_STEPS, score_steps, (zero,) * 8)
 
     for u in range(n_units):
         at = slice(u * rows_u, (u + 1) * rows_u)
@@ -536,20 +554,21 @@
 
     weight_ref[...] = jnp.zeros_like(weight_ref)
 
-    def apply(p, u, t):
+    def apply(p, u, k):
         at = pl.ds(pl.multiple_of(u * rows_u, rows_u), rows_u)
         acc_ref[at, :] += jnp.dot(
             weight_ref[p],
-            v_ref[pl.ds(pl.multiple_of(t * TILE, TILE), TILE), :],
+            v_ref[pl.ds(pl.multiple_of(place(u, k) * LANES, LANES), TILE), :],
             preferred_element_type=F32,
         )
 
-    def weigh(p, u, t, above):
+    def weigh(p, u, k, above):
+        t = place(u, k)
         at = pl.ds(pl.multiple_of(u * rows_u, rows_u), rows_u)
         top = top_ref[at, :] + above
         total = total_ref[at, :]
         for i in range(0, TILE, 128):
-            cols = pl.ds(pl.multiple_of(t * TILE + i, 128), 128)
+            cols = pl.ds(pl.multiple_of(t * LANES + i, 128), 128)
             weight = jnp.exp2((s_ref[at, cols] - top) * (LOG2E / root))
             total = total + weight
             weight_ref[p, :, i : i + 128] = weight.astype(BF16)
@@ -563,7 +582,7 @@
             carry = (*following(u0, t0), u0, t0)
         return carry
 
-    lax.fori_loop(0, (steps + VALUE_STEPS) // VALUE_STEPS, value_steps, (zero, t_first) * 2)
+    lax.fori_loop(0, (steps + VALUE_STEPS) // VALUE_STEPS, value_steps, (zero,) * 4)
 
     lane = lax.broadcasted_iota(jnp.int32, (rows_g, slots), 1)
     row = lax.rem(lax.broadcasted_iota(jnp.int32, (rows_g, slots), 0), GROUP)
@@ -747,12 +766,12 @@
             pltpu.VMEM(((hid + heads) * GROUP, mixing), BF16),
             pltpu.VMEM((heads * GROUP, hid * GROUP), BF16),
             dma((8,)),
-            pltpu.VMEM((width, n_tiles * TILE), BF16),
-            pltpu.VMEM((n_tiles * TILE, width), BF16),
-            pltpu.VMEM((8, TILE // 128, n_tiles, 128), F32),
+            pltpu.VMEM((width, n_tiles * TILE + LANES), BF16),
+            pltpu.VMEM((n_tiles * TILE + LANES, width), BF16),
+            pltpu.VMEM((8, n_tiles * TILE // LANES + 8, LANES), F32),
             pltpu.VMEM((8, own_rows, slots), F32),
             pltpu.VMEM((rows_all, width), BF16),
-            pltpu.VMEM((rows_all, n_tiles * TILE), F32),
+            pltpu.VMEM((rows_all, n_tiles * TILE + LANES), F32),
             pltpu.VMEM((rows_all, 128), F32),
             pltpu.VMEM((rows_all, 128), F32),
             pltpu.VMEM((rows_all, width), F32),

time: 50.7 us -> 50.9 us (level)
  the two profiles are of different devices: /device:TPU:64 before, /device:TPU:8 now
where the time goes in v8:
time: 50.9 us; the launch traced here: 50 us
  Pallas kernels  48.5 us (95%)
  local copies, waits for them, and re-layouts  1.47 us (3%)
    pallas_call x1, Pallas kernels, shards(): pl.pallas_call(functools.partial(exchange_kernel, n_grp, cube), out_shape...  25.2 us
    pallas_call x1, Pallas kernels, shards(): pl.pallas_call(functools.partial(attend_kernel, heads), out_shape=(jax.Sh...  17.4 us
    pallas_call x1, Pallas kernels, shards(): pl.pallas_call(functools.partial(finish_kernel, cube), out_shape=jax.Shap...  5.95 us
    unnamed x1, local copies, waits for them, and re-layouts  1.47 us

profile of v8, /device:TPU:8, one launch (start us, length us, event | category | flops | bytes accessed | tf_op | source)
XLA Modules:
  0.0 50.0 jit_solution(14633871092310720706)
XLA Ops:
  0.0 25.2 %exchange.1 = (bf16[2,144,256]{2,1,0:T(8,128)(2,1)}, bf16[4,4,2,144,128]{4,3,2,1,0:T(8,128)(2,1)}, bf16[320,112]{1,0:T(8,128)(2,1)}, bf16[64,256]{1,0:T(8,128)(2,1)}) custom-call(bf16[1,4,128,256]{3,2,1,0:T(8,128)(2,1)} %raw_ref.1, bf16[1,4,4,128]{3,2,1,0:T(4,128)(2,1)} %kin_hbm.1, s32[1,128]{1,0:T(1,128)} %reader_hbm.1, s32[1,128]{1,0:T(1,128)} %event_hbm.1, ...), custom_call_target="tpu_custom_call" | custom-call | tf_op jit(solution)/shard_map/exchange/pallas_call | solution.py:699
  25.2 17.4 %attend.1 = (bf16[2,128,256]{2,1,0:T(8,128)(2,1)}, f32[2,8,128]{2,1,0:T(8,128)}) custom-call(bf16[2,144,256]{2,1,0:T(8,128)(2,1)} %get-tuple-element.11.pair_hbm, bf16[4,4,2,144,128]{4,3,2,1,0:T(8,128)(2,1)} %get-tuple-element.12.keys_hbm, bf16[256,256]{1,0:T(8,128)(2,1)} %wq_hbm.1, bf16[256,256]{1,0:T(8,128)(2,1)} %wk_hbm.1, bf16[256,256]{1,0:T(8,128)(2,1)} %wv_hbm.1, ...), custom_call_target="tpu_custom_call" | custom-call | tf_op jit(solution)/shard_map/attend/pallas_call | solution.py:752
  42.6 5.9 %finish.1 = bf16[128,256]{1,0:T(8,128)(2,1)} custom-call(bf16[2,128,256]{2,1,0:T(8,128)(2,1)} %get-tuple-element.15.part_ref, f32[2,8,128]{2,1,0:T(8,128)} %get-tuple-element.16.level_ref, bf16[256,256]{1,0:T(8,128)(2,1)} %wo_ref.1, f32[1,256]{1,0:T(1,128)} %bitcast.8), custom_call_target="tpu_custom_call" | custom-call | tf_op jit(solution)/shard_map/finish/pallas_call | solution.py:791
  48.5 1.5 %copy.15 = bf16[1,128,256]{2,1,0:T(8,128)(2,1)} copy(bf16[1,128,256]{2,1,0:T(8,128)(2,1)} %bitcast.5) | data formatting | bytes 131072

commit v9 on v8

--- a/solution.py
+++ b/solution.py
@@ -158,7 +158,7 @@
         for h in range(0, width, slots)
     ]
     for copy in copies:
-        copy.wait()
+        copy.wait_recv()
     for k in range(1, n_grp):
         kin = kin + jnp.where(wanted == k, kin_in[k, 0:4, :], 0.0)
         sides = [
@@ -228,7 +228,7 @@
             slot += 1
     for copy in here + stores:
         copy.wait()
-    for copy in [swap] + own_x + other_y:
+    for copy in copies + [swap] + own_x + other_y:
         copy.wait_send()
     for copy in moves:
         copy.wait()
@@ -346,7 +346,7 @@
     per_step = TILE // LANES
     z = lax.axis_index("blk") // (ny * nx)
 
-    for load in loads:
+    for load in loads[0:2]:
         load.wait()
 
     def terms_of(mom, rap, azi, mass, ids):
@@ -418,6 +418,8 @@
     to_scalars = pltpu.make_async_copy(ranges, limits, load_sem.at[7])
     to_scalars.start()
 
+    for load in loads[2:]:
+        load.wait()
     wkt = wk_ref[...].astype(F32).T.astype(BF16)
     for yy in range(ny):
         for zz in range(nz):

time: 50.9 us -> 49.8 us (0.978)
  Pallas kernels: 48.5 us -> 47.6 us
    pallas_call x1, Pallas kernels: 17.4 us -> 15.7 us  [shards(): pl.pallas_call(functools.partial(attend_kernel, heads), out_shape=(jax.Sh...]
    pallas_call x1, Pallas kernels: 5.95 us -> 6.77 us  [shards(): pl.pallas_call(functools.partial(finish_kernel, cube), out_shape=jax.Shap...]
where the time goes in v9:
time: 49.8 us; the launch traced here: 49.1 us
  Pallas kernels  47.6 us (96%)
  local copies, waits for them, and re-layouts  1.47 us (3%)
    pallas_call x1, Pallas kernels, shards(): pl.pallas_call(functools.partial(exchange_kernel, n_grp, cube), out_shape...  25.2 us
    pallas_call x1, Pallas kernels, shards(): pl.pallas_call(functools.partial(attend_kernel, heads), out_shape=(jax.Sh...  15.7 us
    pallas_call x1, Pallas kernels, shards(): pl.pallas_call(functools.partial(finish_kernel, cube), out_shape=jax.Shap...  6.77 us
    unnamed x1, local copies, waits for them, and re-layouts  1.47 us

profile of v9, /device:TPU:8, one launch (start us, length us, event | category | flops | bytes accessed | tf_op | source)
XLA Modules:
  0.0 49.1 jit_solution(7190737846014121586)
XLA Ops:
  0.0 25.2 %exchange.1 = (bf16[2,144,256]{2,1,0:T(8,128)(2,1)}, bf16[4,4,2,144,128]{4,3,2,1,0:T(8,128)(2,1)}, bf16[320,112]{1,0:T(8,128)(2,1)}, bf16[64,256]{1,0:T(8,128)(2,1)}) custom-call(bf16[1,4,128,256]{3,2,1,0:T(8,128)(2,1)} %raw_ref.1, bf16[1,4,4,128]{3,2,1,0:T(4,128)(2,1)} %kin_hbm.1, s32[1,128]{1,0:T(1,128)} %reader_hbm.1, s32[1,128]{1,0:T(1,128)} %event_hbm.1, ...), custom_call_target="tpu_custom_call" | custom-call | tf_op jit(solution)/shard_map/exchange/pallas_call | solution.py:701
  25.2 15.7 %attend.1 = (bf16[2,128,256]{2,1,0:T(8,128)(2,1)}, f32[2,8,128]{2,1,0:T(8,128)}) custom-call(bf16[2,144,256]{2,1,0:T(8,128)(2,1)} %get-tuple-element.11.pair_hbm, bf16[4,4,2,144,128]{4,3,2,1,0:T(8,128)(2,1)} %get-tuple-element.12.keys_hbm, bf16[256,256]{1,0:T(8,128)(2,1)} %wq_hbm.1, bf16[256,256]{1,0:T(8,128)(2,1)} %wk_hbm.1, bf16[256,256]{1,0:T(8,128)(2,1)} %wv_hbm.1, ...), custom_call_target="tpu_custom_call" | custom-call | tf_op jit(solution)/shard_map/attend/pallas_call | solution.py:754
  40.9 6.8 %finish.1 = bf16[128,256]{1,0:T(8,128)(2,1)} custom-call(bf16[2,128,256]{2,1,0:T(8,128)(2,1)} %get-tuple-element.15.part_ref, f32[2,8,128]{2,1,0:T(8,128)} %get-tuple-element.16.level_ref, bf16[256,256]{1,0:T(8,128)(2,1)} %wo_ref.1, f32[1,256]{1,0:T(1,128)} %bitcast.8), custom_call_target="tpu_custom_call" | custom-call | tf_op jit(solution)/shard_map/finish/pallas_call | solution.py:793
  47.7 1.5 %copy.15 = bf16[1,128,256]{2,1,0:T(8,128)(2,1)} copy(bf16[1,128,256]{2,1,0:T(8,128)(2,1)} %bitcast.5) | data formatting | bytes 131072

commit v10 on v9

--- a/solution.py
+++ b/solution.py
@@ -287,8 +287,8 @@
     wv_hbm,
     first_hbm,
     second_hbm,
-    out_ref,
-    level_ref,
+    keep_hbm,
+    send_hbm,
     pair_ref,
     keys_ref,
     wq_ref,
@@ -331,7 +331,7 @@
     ]
     for load in loads:
         load.start()
-    nz, slots, width = out_ref.shape
+    nz, slots, width = held_ref.shape[0], held_ref.shape[1] - 2 * heads, held_ref.shape[2]
     ny, nx = keys_ref.shape[0:2]
     half = slots // nz
     own_rows = nz * slots
@@ -604,71 +604,52 @@
                 rows = slice(at + h * GROUP, at + (h + 1) * GROUP)
                 scaled = acc_ref[rows, :] * total[h * GROUP : (h + 1) * GROUP]
                 out = jnp.where(lane_head == h, scaled, out)
-            held_ref[base : base + GROUP, :] = out
-        out_ref[zz] = held_ref[...].astype(BF16)
-        level_ref[zz] = jnp.sum(level.reshape(heads, GROUP, slots), axis=1)
+            acc_ref[base : base + GROUP, :] = out
+        held_ref[zz, 0:slots, :] = acc_ref[0:slots, :].astype(BF16)
+        level = jnp.sum(level.reshape(heads, GROUP, slots), axis=1)
+        high, middle = split_two(level)
+        low = (level - high.astype(F32) - middle.astype(F32)).astype(BF16)
+        held_ref[zz, slots : slots + 2 * heads, :] = jnp.concatenate(
+            [
+                jnp.concatenate([high, middle], axis=1),
+                jnp.concatenate([low, jnp.zeros_like(low)], axis=1),
+            ],
+            axis=0,
+        )
+    stores = [
+        pltpu.make_async_copy(held_ref.at[z], keep_hbm, load_sem.at[0]),
+        pltpu.make_async_copy(held_ref.at[1 - z], send_hbm, load_sem.at[1]),
+    ]
+    for store in stores:
+        store.start()
+    for store in stores:
+        store.wait()
 
 
 def finish_kernel(
-    cube,
-    part_ref,
-    level_ref,
+    heads,
+    keep_ref,
+    came_ref,
     wo_ref,
     gain_ref,
     out_ref,
-    part_in,
-    level_in,
-    part_own,
-    level_own,
-    wo_own,
-    gain_own,
-    send_sem,
-    recv_sem,
-    load_sem,
 ):
-    _, ny, nx = cube
-    z, y, x = mesh_place(cube)
-    near = {"blk": ((1 - z) * ny + y) * nx + x}
-    heads = level_ref.shape[1]
-    width = part_ref.shape[2]
-    barrier = pltpu.get_barrier_semaphore()
-    pl.semaphore_signal(barrier, inc=1, device_id=near, device_id_type=MESH)
-    loads = [
-        pltpu.make_async_copy(part_ref.at[z], part_own, load_sem.at[0]),
-        pltpu.make_async_copy(level_ref.at[z], level_own, load_sem.at[1]),
-        pltpu.make_async_copy(wo_ref, wo_own, load_sem.at[2]),
-        pltpu.make_async_copy(gain_ref, gain_own, load_sem.at[3]),
-    ]
-    for load in loads:
-        load.start()
-    pl.semaphore_wait(barrier, 1)
-    copies = [
-        pltpu.make_async_remote_copy(
-            src_ref=src,
-            dst_ref=dst,
-            send_sem=send_sem.at[i],
-            recv_sem=recv_sem.at[i],
-            device_id=near,
-            device_id_type=MESH,
-        )
-        for i, (src, dst) in enumerate(
-            [(part_ref.at[1 - z], part_in), (level_ref.at[1 - z], level_in)]
-        )
-    ]
-    for copy in copies:
-        copy.start()
+    slots, width = out_ref.shape
     spread = (
         lax.broadcasted_iota(jnp.int32, (heads, width), 1) // (width // heads)
         == lax.broadcasted_iota(jnp.int32, (heads, width), 0)
     ).astype(F32)
-    for copy in loads + copies:
-        copy.wait()
-    share = 1.0 / (1.0 + jnp.exp2(level_in[...] - level_own[...]))
+
+    def level_of(ref):
+        pieces = ref[slots : slots + 2 * heads, :].astype(F32)
+        return pieces[0:heads, 0:slots] + pieces[0:heads, slots:] + pieces[heads:, 0:slots]
+
+    share = 1.0 / (1.0 + jnp.exp2(level_of(came_ref) - level_of(keep_ref)))
     share = jnp.dot(share.T, spread, precision=HIGHEST, preferred_element_type=F32)
-    theirs = part_in[...].astype(F32)
-    attended = theirs + share * (part_own[...].astype(F32) - theirs)
-    mixed = jnp.dot(attended.astype(BF16), wo_own[...], preferred_element_type=F32)
-    out_ref[...] = layer_norm(mixed, gain_own[...]).astype(BF16)
+    theirs = came_ref[0:slots, :].astype(F32)
+    attended = theirs + share * (keep_ref[0:slots, :].astype(F32) - theirs)
+    mixed = jnp.dot(attended.astype(BF16), wo_ref[...], preferred_element_type=F32)
+    out_ref[...] = layer_norm(mixed, gain_ref[...]).astype(BF16)
 
 
 def shards(
@@ -751,14 +732,11 @@
     n_tiles = nz * ny
     groups = UNIT // GROUP
     rows_all = heads * own_rows
-    part, level = pl.pallas_call(
+    keep, send = pl.pallas_call(
         functools.partial(attend_kernel, heads),
-        out_shape=(
-            jax.ShapeDtypeStruct((nz, slots, width), BF16),
-            jax.ShapeDtypeStruct((nz, heads, slots), F32),
-        ),
+        out_shape=(jax.ShapeDtypeStruct((slots + 2 * heads, width), BF16),) * 2,
         in_specs=[free] * 7,
-        out_specs=(vmem, vmem),
+        out_specs=(free, free),
         scratch_shapes=[
             pltpu.VMEM((nz, tall, width), BF16),
             pltpu.VMEM((ny, nx, nz, part_rows, 128), BF16),
@@ -782,7 +760,7 @@
             pltpu.VMEM((2, groups, heads * GROUP, TILE), F32),
             pltpu.VMEM((2, groups, hid * GROUP, TILE), BF16),
             pltpu.VMEM((2, heads * UNIT, TILE), BF16),
-            pltpu.VMEM((slots, width), F32),
+            pltpu.VMEM((nz, slots + 2 * heads, width), BF16),
             pltpu.VMEM((2, own_rows // UNIT, 128), jnp.int32),
             pltpu.SMEM((2, own_rows // UNIT, 128), jnp.int32),
         ],
@@ -790,25 +768,17 @@
         name="attend",
     )(pair, keys, w_query, w_key, w_value, first, second)
 
+    n_blk = nz * ny * nx
+    swap = [(i, (i + ny * nx) % n_blk) for i in range(n_blk)]
+    came = lax.ppermute(send, "blk", swap)
     encoded = pl.pallas_call(
-        functools.partial(finish_kernel, cube),
+        functools.partial(finish_kernel, heads),
         out_shape=jax.ShapeDtypeStruct((slots, width), BF16),
-        in_specs=[free] * 4,
+        in_specs=[vmem] * 4,
         out_specs=vmem,
-        scratch_shapes=[
-            pltpu.VMEM((slots, width), BF16),
-            pltpu.VMEM((heads, slots), F32),
-            pltpu.VMEM((slots, width), BF16),
-            pltpu.VMEM((heads, slots), F32),
-            pltpu.VMEM((width, width), BF16),
-            pltpu.VMEM((1, width), F32),
-            dma((2,)),
-            dma((2,)),
-            dma((4,)),
-        ],
-        compiler_params=pltpu.CompilerParams(collective_id=1, has_side_effects=True),
+        compiler_params=pltpu.CompilerParams(vmem_limit_bytes=8 * 1024 * 1024),
         name="finish",
-    )(part, level, w_out, post_gain[None])
+    )(keep, came, w_out, post_gain[None])
     return encoded[None]
 
 

time: 49.8 us -> 51.6 us (1.036)
  waiting for transfers between devices: 0 us -> 3.55 us
  Pallas kernels: 47.6 us -> 45.2 us
  starting transfers between devices: 0 us -> 1.09 us
  local copies, waits for them, and re-layouts: 1.47 us -> 0.89 us
    pallas_call x1, Pallas kernels: 6.77 us -> 1.28 us  [shards(): pl.pallas_call(functools.partial(finish_kernel, heads), out_shape=jax.Sha...]
    ppermute x0 -> x1, waiting for transfers between devices: none -> 3.55 us  [shards(): came = lax.ppermute(send, 'blk', swap)]
    pallas_call x1, Pallas kernels: 15.7 us -> 18.7 us  [shards(): pl.pallas_call(functools.partial(attend_kernel, heads), out_shape=(jax.Sh...]
    ppermute x0 -> x1, starting transfers between devices: none -> 1.09 us  [shards(): came = lax.ppermute(send, 'blk', swap)]
    unnamed x1 -> x6, local copies, waits for them, and re-layouts: 1.47 us -> 0.89 us
  transfers between devices with their start and end apart: 0 -> 1, of which waited for: 0 -> 1; matrix products, arithmetic and copies ran while one was open for 0% -> 0% of each run, Pallas kernels for 0% -> 0%
where the time goes in v10:
time: 51.6 us; the launch traced here: 50.8 us
  Pallas kernels  45.2 us (88%)
  waiting for transfers between devices  3.55 us (7%)
  starting transfers between devices  1.09 us (2%)
  local copies, waits for them, and re-layouts  0.89 us (2%)
    pallas_call x1, Pallas kernels, shards(): pl.pallas_call(functools.partial(exchange_kernel, n_grp, cube), out_shape...  25.2 us
    pallas_call x1, Pallas kernels, shards(): pl.pallas_call(functools.partial(attend_kernel, heads), out_shape=(jax.Sh...  18.7 us
    ppermute x1, waiting for transfers between devices, shards(): came = lax.ppermute(send, 'blk', swap)  3.55 us
    pallas_call x1, Pallas kernels, shards(): pl.pallas_call(functools.partial(finish_kernel, heads), out_shape=jax.Sha...  1.28 us
    ppermute x1, starting transfers between devices, shards(): came = lax.ppermute(send, 'blk', swap)  1.09 us
  transfers between devices with their start and end apart: 1, of which 1 were waited for; matrix products, arithmetic and copies ran while one was open for 0% of the time, Pallas kernels for 0%

profile of v10, /device:TPU:8, one launch (start us, length us, event | category | flops | bytes accessed | tf_op | source)
XLA Modules:
  0.0 50.8 jit_solution(16318419632324224414)
XLA Ops:
  0.0 0.0 copy-start.2
  0.0 0.0 copy-start
  0.0 25.2 %exchange.1 = (bf16[2,144,256]{2,1,0:T(8,128)(2,1)}, bf16[4,4,2,144,128]{4,3,2,1,0:T(8,128)(2,1)}, bf16[320,112]{1,0:T(8,128)(2,1)}, bf16[64,256]{1,0:T(8,128)(2,1)}) custom-call(bf16[1,4,128,256]{3,2,1,0:T(8,128)(2,1)} %raw_ref.1, bf16[1,4,4,128]{3,2,1,0:T(4,128)(2,1)} %kin_hbm.1, s32[1,128]{1,0:T(1,128)} %reader_hbm.1, s32[1,128]{1,0:T(1,128)} %event_hbm.1, ...), custom_call_target="tpu_custom_call" | custom-call | tf_op jit(solution)/shard_map/exchange/pallas_call | solution.py:682
  25.3 18.7 %attend.1 = (bf16[144,256]{1,0:T(8,128)(2,1)}, bf16[144,256]{1,0:T(8,128)(2,1)}) custom-call(bf16[2,144,256]{2,1,0:T(8,128)(2,1)} %get-tuple-element.11.pair_hbm, bf16[4,4,2,144,128]{4,3,2,1,0:T(8,128)(2,1)} %get-tuple-element.12.keys_hbm, bf16[256,256]{1,0:T(8,128)(2,1)} %wq_hbm.1, bf16[256,256]{1,0:T(8,128)(2,1)} %wk_hbm.1, bf16[256,256]{1,0:T(8,128)(2,1)} %wv_hbm.1, ...), custom_call_target="tpu_custom_call" | custom-call | tf_op jit(solution)/shard_map/attend/pallas_call | solution.py:735
  43.9 1.1 %collective-permute-start = (bf16[144,256]{1,0:T(8,128)(2,1)}, bf16[144,256]{1,0:T(8,128)(2,1)S(1)}, u32[]{:S(2)}, u32[]{:S(2)}) collective-permute-start(bf16[144,256]{1,0:T(8,128)(2,1)} %get-tuple-element.16), channel_id=1, source_target_pairs={{0,16},{1,17},{2,18},{3,19},{4,20},{5,21},{6,22},{7,23},{8,24},{9,... | collective-permute-start | bytes 221192 | tf_op jit(solution)/shard_map/ppermute | solution.py:773
  45.0 3.6 %collective-permute-done.came_ref = bf16[144,256]{1,0:T(8,128)(2,1)S(1)} collective-permute-done((bf16[144,256]{1,0:T(8,128)(2,1)}, bf16[144,256]{1,0:T(8,128)(2,1)S(1)}, u32[]{:S(2)}, u32[]{:S(2)}) %collective-permute-start) | collective-permute-done | bytes 73760 | tf_op jit(solution)/shard_map/ppermute | solution.py:773
  48.6 0.0 copy-done.2
  48.6 0.0 copy-done
  48.6 0.0 copy-start.1
  48.6 0.9 %copy-done.1 = bf16[144,256]{1,0:T(8,128)(2,1)S(1)} copy-done((bf16[144,256]{1,0:T(8,128)(2,1)S(1)}, bf16[144,256]{1,0:T(8,128)(2,1)}, u32[]{:S(2)}) %copy-start.1) | copy-done | bytes 73752
  49.5 1.3 %finish.1 = bf16[128,256]{1,0:T(8,128)(2,1)} custom-call(bf16[144,256]{1,0:T(8,128)(2,1)S(1)} %copy-done.1, bf16[144,256]{1,0:T(8,128)(2,1)S(1)} %collective-permute-done.came_ref, bf16[256,256]{1,0:T(8,128)(2,1)S(1)} %copy-done, f32[1,256]{1,0:T(1,128)S(1)} %bitcast.5), custom_call_target="tpu_custom_call" | custom-call | tf_op jit(solution)/shard_map/finish/pallas_call | solution.py:774
Async XLA Ops:
  0.0 48.6 %copy-start.2 = (f32[256]{0:T(256)S(1)}, f32[256]{0:T(256)}, u32[]{:S(2)}) copy-start(f32[256]{0:T(256)} %param.22) | copy-start | bytes 3076
  0.0 48.6 %copy-start = (bf16[256,256]{1,0:T(8,128)(2,1)S(1)}, bf16[256,256]{1,0:T(8,128)(2,1)}, u32[]{:S(2)}) copy-start(bf16[256,256]{1,0:T(8,128)(2,1)} %wo_ref.1) | copy-start | bytes 393220
  43.9 4.6 %collective-permute-start = (bf16[144,256]{1,0:T(8,128)(2,1)}, bf16[144,256]{1,0:T(8,128)(2,1)S(1)}, u32[]{:S(2)}, u32[]{:S(2)}) collective-permute-start(bf16[144,256]{1,0:T(8,128)(2,1)} %get-tuple-element.16), channel_id=1, source_target_pairs={{0,16},{1,17},{2,18},{3,19},{4,20},{5,21},{6,22},{7,23},{8,24},{9,... | collective-permute-start | bytes 221192 | tf_op jit(solution)/shard_map/ppermute | solution.py:773
  48.6 0.9 %copy-start.1 = (bf16[144,256]{1,0:T(8,128)(2,1)S(1)}, bf16[144,256]{1,0:T(8,128)(2,1)}, u32[]{:S(2)}) copy-start(bf16[144,256]{1,0:T(8,128)(2,1)} %get-tuple-element.15.keep_ref) | copy-start | bytes 221188

commit v11 on v10

--- a/solution.py
+++ b/solution.py
@@ -778,7 +778,7 @@
         out_specs=vmem,
         compiler_params=pltpu.CompilerParams(vmem_limit_bytes=8 * 1024 * 1024),
         name="finish",
-    )(keep, came, w_out, post_gain[None])
+    )(keep.astype(F32), came, w_out, post_gain[None])
     return encoded[None]
 
 

time: 51.6 us -> 49.8 us (0.965)
  the two profiles are of different devices: /device:TPU:8 before, /device:TPU:64 now
where the time goes in v11:
time: 49.8 us; the launch traced here: 48.9 us
  Pallas kernels  44.2 us (89%)
  waiting for transfers between devices  3.54 us (7%)
  other arithmetic  0.89 us (2%)
    pallas_call x1, Pallas kernels, shards(): pl.pallas_call(functools.partial(exchange_kernel, n_grp, cube), out_shape...  25.7 us
    pallas_call x1, Pallas kernels, shards(): pl.pallas_call(functools.partial(attend_kernel, heads), out_shape=(jax.Sh...  17.2 us
    ppermute x1, waiting for transfers between devices, shards(): came = lax.ppermute(send, 'blk', swap)  3.54 us
    pallas_call x1, Pallas kernels, shards(): pl.pallas_call(functools.partial(finish_kernel, heads), out_shape=jax.Sha...  1.28 us
  transfers between devices with their start and end apart: 1, of which 1 were waited for; matrix products, arithmetic and copies ran while one was open for 2% of the time, Pallas kernels for 0%

profile of v11, /device:TPU:64, one launch (start us, length us, event | category | flops | bytes accessed | tf_op | source)
XLA Modules:
  0.0 48.9 jit_solution(3372059146126993875)
XLA Ops:
  0.0 0.0 copy-start.1
  0.0 0.0 copy-start
  0.0 25.7 %exchange.1 = (bf16[2,144,256]{2,1,0:T(8,128)(2,1)}, bf16[4,4,2,144,128]{4,3,2,1,0:T(8,128)(2,1)}, bf16[320,112]{1,0:T(8,128)(2,1)}, bf16[64,256]{1,0:T(8,128)(2,1)}) custom-call(bf16[1,4,128,256]{3,2,1,0:T(8,128)(2,1)} %raw_ref.1, bf16[1,4,4,128]{3,2,1,0:T(4,128)(2,1)} %kin_hbm.1, s32[1,128]{1,0:T(1,128)} %reader_hbm.1, s32[1,128]{1,0:T(1,128)} %event_hbm.1, ...), custom_call_target="tpu_custom_call" | custom-call | tf_op jit(solution)/shard_map/exchange/pallas_call | solution.py:682
  25.7 17.2 %attend.1 = (bf16[144,256]{1,0:T(8,128)(2,1)}, bf16[144,256]{1,0:T(8,128)(2,1)}) custom-call(bf16[2,144,256]{2,1,0:T(8,128)(2,1)} %get-tuple-element.11.pair_hbm, bf16[4,4,2,144,128]{4,3,2,1,0:T(8,128)(2,1)} %get-tuple-element.12.keys_hbm, bf16[256,256]{1,0:T(8,128)(2,1)} %wq_hbm.1, bf16[256,256]{1,0:T(8,128)(2,1)} %wk_hbm.1, bf16[256,256]{1,0:T(8,128)(2,1)} %wv_hbm.1, ...), custom_call_target="tpu_custom_call" | custom-call | tf_op jit(solution)/shard_map/attend/pallas_call | solution.py:735
  42.9 0.2 collective-permute-start
  43.1 0.9 %convert_element_type.3.keep_ref = f32[144,256]{1,0:T(8,128)S(1)} convert(bf16[144,256]{1,0:T(8,128)(2,1)} %get-tuple-element.15) | non-fusion elementwise | flops 36864 | bytes 221184 | tf_op jit(solution)/shard_map/convert_element_type | solution.py:781
  44.0 3.5 %collective-permute-done.came_ref = bf16[144,256]{1,0:T(8,128)(2,1)S(1)} collective-permute-done((bf16[144,256]{1,0:T(8,128)(2,1)}, bf16[144,256]{1,0:T(8,128)(2,1)S(1)}, u32[]{:S(2)}, u32[]{:S(2)}) %collective-permute-start) | collective-permute-done | bytes 73760 | tf_op jit(solution)/shard_map/ppermute | solution.py:773
  47.6 0.0 copy-done.1
  47.6 0.0 copy-done
  47.6 1.3 %finish.1 = bf16[128,256]{1,0:T(8,128)(2,1)} custom-call(f32[144,256]{1,0:T(8,128)S(1)} %convert_element_type.3.keep_ref, bf16[144,256]{1,0:T(8,128)(2,1)S(1)} %collective-permute-done.came_ref, bf16[256,256]{1,0:T(8,128)(2,1)S(1)} %copy-done, f32[1,256]{1,0:T(1,128)S(1)} %bitcast.5), custom_call_target="tpu_custom_call" | custom-call | tf_op jit(solution)/shard_map/finish/pallas_call | solution.py:774
Async XLA Ops:
  0.0 47.6 %copy-start.1 = (f32[256]{0:T(256)S(1)}, f32[256]{0:T(256)}, u32[]{:S(2)}) copy-start(f32[256]{0:T(256)} %param.22) | copy-start | bytes 3076
  0.0 47.6 %copy-start = (bf16[256,256]{1,0:T(8,128)(2,1)S(1)}, bf16[256,256]{1,0:T(8,128)(2,1)}, u32[]{:S(2)}) copy-start(bf16[256,256]{1,0:T(8,128)(2,1)} %wo_ref.1) | copy-start | bytes 393220
  42.9 4.6 %collective-permute-start = (bf16[144,256]{1,0:T(8,128)(2,1)}, bf16[144,256]{1,0:T(8,128)(2,1)S(1)}, u32[]{:S(2)}, u32[]{:S(2)}) collective-permute-start(bf16[144,256]{1,0:T(8,128)(2,1)} %get-tuple-element.16), channel_id=1, source_target_pairs={{0,16},{1,17},{2,18},{3,19},{4,20},{5,21},{6,22},{7,23},{8,24},{9,... | collective-permute-start | bytes 221192 | tf_op jit(solution)/shard_map/ppermute | solution.py:773

commit v12 on v11

--- a/solution.py
+++ b/solution.py
@@ -346,7 +346,7 @@
     per_step = TILE // LANES
     z = lax.axis_index("blk") // (ny * nx)
 
-    for load in loads[0:2]:
+    for load in loads:
         load.wait()
 
     def terms_of(mom, rap, azi, mass, ids):
@@ -418,8 +418,6 @@
     to_scalars = pltpu.make_async_copy(ranges, limits, load_sem.at[7])
     to_scalars.start()
 
-    for load in loads[2:]:
-        load.wait()
     wkt = wk_ref[...].astype(F32).T.astype(BF16)
     for yy in range(ny):
         for zz in range(nz):
@@ -590,22 +588,27 @@
     row = lax.rem(lax.broadcasted_iota(jnp.int32, (rows_g, slots), 0), GROUP)
     for zz in range(nz):
         level = jnp.zeros((rows_g, slots), F32)
+        weight = jnp.ones((rows_g, slots), F32)
         for base in range(0, slots, GROUP):
             at = (zz * slots + base) * heads
             total = jnp.sum(total_ref[at : at + rows_g, :], axis=1, keepdims=True)
-            level = jnp.where(
-                lane == base + row,
-                top_ref[at : at + rows_g, :] * (LOG2E / root) + jnp.log(total) * LOG2E,
-                level,
-            )
+            here = lane == base + row
+            level = jnp.where(here, top_ref[at : at + rows_g, :], level)
+            weight = jnp.where(here, total, weight)
             total = 1.0 / total
-            out = jnp.zeros((GROUP, width), F32)
-            for h in range(heads):
-                rows = slice(at + h * GROUP, at + (h + 1) * GROUP)
-                scaled = acc_ref[rows, :] * total[h * GROUP : (h + 1) * GROUP]
-                out = jnp.where(lane_head == h, scaled, out)
+            sides = []
+            for i in range(0, width, 128):
+                out = jnp.zeros((GROUP, 128), F32)
+                for h in range(i // head_size, (i + 128) // head_size):
+                    rows = slice(at + h * GROUP, at + (h + 1) * GROUP)
+                    scaled = acc_ref[rows, i : i + 128] * total[h * GROUP : (h + 1) * GROUP]
+                    out = jnp.where(lane_head[:, i : i + 128] == h, scaled, out)
+                sides.append(out)
+            out = jnp.concatenate(sides, axis=1)
             acc_ref[base : base + GROUP, :] = out
         held_ref[zz, 0:slots, :] = acc_ref[0:slots, :].astype(BF16)
+        there = lax.rem(lane, GROUP) == row
+        level = jnp.where(there, level * (LOG2E / root) + jnp.log(weight) * LOG2E, 0.0)
         level = jnp.sum(level.reshape(heads, GROUP, slots), axis=1)
         high, middle = split_two(level)
         low = (level - high.astype(F32) - middle.astype(F32)).astype(BF16)

time: 49.8 us -> 49.9 us (level)
  the two profiles are of different devices: /device:TPU:64 before, /device:TPU:8 now
where the time goes in v12:
time: 49.9 us
  Pallas kernels  45.2 us (91%)
  waiting for transfers between devices  2.66 us (5%)
  starting transfers between devices  1.08 us (2%)
  other arithmetic  0.89 us (2%)
    pallas_call x1, Pallas kernels, shards(): pl.pallas_call(functools.partial(exchange_kernel, n_grp, cube), out_shape...  25.2 us
    pallas_call x1, Pallas kernels, shards(): pl.pallas_call(functools.partial(attend_kernel, heads), out_shape=(jax.Sh...  18.7 us
    ppermute x1, waiting for transfers between devices, shards(): came = lax.ppermute(send, 'blk', swap)  2.66 us
    pallas_call x1, Pallas kernels, shards(): pl.pallas_call(functools.partial(finish_kernel, heads), out_shape=jax.Sha...  1.28 us
    ppermute x1, starting transfers between devices, shards(): came = lax.ppermute(send, 'blk', swap)  1.08 us
  transfers between devices with their start and end apart: 1, of which 1 were waited for; matrix products, arithmetic and copies ran while one was open for 2% of the time, Pallas kernels for 0%

profile of v12, /device:TPU:8, one launch (start us, length us, event | category | flops | bytes accessed | tf_op | source)
XLA Modules:
  0.0 49.9 jit_solution(5516460675462260043)
XLA Ops:
  0.0 0.0 copy-start.1
  0.0 0.0 copy-start
  0.0 25.2 %exchange.1 = (bf16[2,144,256]{2,1,0:T(8,128)(2,1)}, bf16[4,4,2,144,128]{4,3,2,1,0:T(8,128)(2,1)}, bf16[320,112]{1,0:T(8,128)(2,1)}, bf16[64,256]{1,0:T(8,128)(2,1)}) custom-call(bf16[1,4,128,256]{3,2,1,0:T(8,128)(2,1)} %raw_ref.1, bf16[1,4,4,128]{3,2,1,0:T(4,128)(2,1)} %kin_hbm.1, s32[1,128]{1,0:T(1,128)} %reader_hbm.1, s32[1,128]{1,0:T(1,128)} %event_hbm.1, ...), custom_call_target="tpu_custom_call" | custom-call | tf_op jit(solution)/shard_map/exchange/pallas_call | solution.py:685
  25.3 18.7 %attend.1 = (bf16[144,256]{1,0:T(8,128)(2,1)}, bf16[144,256]{1,0:T(8,128)(2,1)}) custom-call(bf16[2,144,256]{2,1,0:T(8,128)(2,1)} %get-tuple-element.11.pair_hbm, bf16[4,4,2,144,128]{4,3,2,1,0:T(8,128)(2,1)} %get-tuple-element.12.keys_hbm, bf16[256,256]{1,0:T(8,128)(2,1)} %wq_hbm.1, bf16[256,256]{1,0:T(8,128)(2,1)} %wk_hbm.1, bf16[256,256]{1,0:T(8,128)(2,1)} %wv_hbm.1, ...), custom_call_target="tpu_custom_call" | custom-call | tf_op jit(solution)/shard_map/attend/pallas_call | solution.py:738
  44.0 1.1 %collective-permute-start = (bf16[144,256]{1,0:T(8,128)(2,1)}, bf16[144,256]{1,0:T(8,128)(2,1)S(1)}, u32[]{:S(2)}, u32[]{:S(2)}) collective-permute-start(bf16[144,256]{1,0:T(8,128)(2,1)} %get-tuple-element.16), channel_id=1, source_target_pairs={{0,16},{1,17},{2,18},{3,19},{4,20},{5,21},{6,22},{7,23},{8,24},{9,... | collective-permute-start | bytes 221192 | tf_op jit(solution)/shard_map/ppermute | solution.py:776
  45.1 0.9 %convert_element_type.3.keep_ref = f32[144,256]{1,0:T(8,128)S(1)} convert(bf16[144,256]{1,0:T(8,128)(2,1)} %get-tuple-element.15) | non-fusion elementwise | flops 36864 | bytes 221184 | tf_op jit(solution)/shard_map/convert_element_type | solution.py:784
  46.0 2.7 %collective-permute-done.came_ref = bf16[144,256]{1,0:T(8,128)(2,1)S(1)} collective-permute-done((bf16[144,256]{1,0:T(8,128)(2,1)}, bf16[144,256]{1,0:T(8,128)(2,1)S(1)}, u32[]{:S(2)}, u32[]{:S(2)}) %collective-permute-start) | collective-permute-done | bytes 73760 | tf_op jit(solution)/shard_map/ppermute | solution.py:776
  48.6 0.0 copy-done.1
  48.6 0.0 copy-done
  48.6 1.3 %finish.1 = bf16[128,256]{1,0:T(8,128)(2,1)} custom-call(f32[144,256]{1,0:T(8,128)S(1)} %convert_element_type.3.keep_ref, bf16[144,256]{1,0:T(8,128)(2,1)S(1)} %collective-permute-done.came_ref, bf16[256,256]{1,0:T(8,128)(2,1)S(1)} %copy-done, f32[1,256]{1,0:T(1,128)S(1)} %bitcast.5), custom_call_target="tpu_custom_call" | custom-call | tf_op jit(solution)/shard_map/finish/pallas_call | solution.py:777
Async XLA Ops:
  0.0 48.6 %copy-start.1 = (f32[256]{0:T(256)S(1)}, f32[256]{0:T(256)}, u32[]{:S(2)}) copy-start(f32[256]{0:T(256)} %param.22) | copy-start | bytes 3076
  0.0 48.6 %copy-start = (bf16[256,256]{1,0:T(8,128)(2,1)S(1)}, bf16[256,256]{1,0:T(8,128)(2,1)}, u32[]{:S(2)}) copy-start(bf16[256,256]{1,0:T(8,128)(2,1)} %wo_ref.1) | copy-start | bytes 393220
  44.0 4.6 %collective-permute-start = (bf16[144,256]{1,0:T(8,128)(2,1)}, bf16[144,256]{1,0:T(8,128)(2,1)S(1)}, u32[]{:S(2)}, u32[]{:S(2)}) collective-permute-start(bf16[144,256]{1,0:T(8,128)(2,1)} %get-tuple-element.16), channel_id=1, source_target_pairs={{0,16},{1,17},{2,18},{3,19},{4,20},{5,21},{6,22},{7,23},{8,24},{9,... | collective-permute-start | bytes 221192 | tf_op jit(solution)/shard_map/ppermute | solution.py:776
